TPU v7x, 32 devices: a whole 2x2x4 slice. The times are simulated.
32 devices in a mesh: dp: 4 (over y, x), ctx: 2 (over core), tensor: 4 (over z).
Axes of the slice: x: 2, y: 2, z: 4, core: 2. Of those that a mesh axis runs over, the one named last changes fastest.
Arguments:
- tokens: bfloat16 [2, 4, 1024, 2048], P(None, 'dp', 'ctx'), may hold values from -6 to 6
- out_grad: bfloat16 [2, 4, 1024, 2048], P(None, 'dp', 'ctx'), may hold values from -6 to 6
- norm_gain: float32 [2048], P(('dp', 'ctx')), may hold values from 0.5 to 1.5
- in_weight: float32 [2048, 2, 4096], P(('dp', 'ctx'), None, 'tensor'), may hold values from -0.125 to 0.125
- xproj_weight: float32 [160, 4096], P(('dp', 'ctx'), 'tensor'), may hold values from -0.375 to 0.375
- step_weight: float32 [128, 4096], P(('dp', 'ctx'), 'tensor'), may hold values from -0.5 to 0.5
- outproj_weight: float32 [2048, 4096], P(('dp', 'ctx'), 'tensor'), may hold values from -0.09375 to 0.09375
- channel_table: float32 [23, 4096], P(None, 'tensor'), may hold values from -20 to 3
- gain_second: float32 [2048], P(('dp', 'ctx')), may hold values from 8192 to 67108864
- in_rows: float32 [2048], P(('dp', 'ctx')), may hold values from 8192 to 67108864
- in_cols: float32 [2, 4096], P(None, 'tensor'), may hold values from 8192 to 67108864
- xproj_rows: float32 [160], P(('dp', 'ctx')), may hold values from 8192 to 67108864
- xproj_cols: float32 [4096], P('tensor'), may hold values from 8192 to 67108864
- step_rows: float32 [128], P(('dp', 'ctx')), may hold values from 8192 to 67108864
- step_cols: float32 [4096], P('tensor'), may hold values from 8192 to 67108864
- out_rows: float32 [2048], P(('dp', 'ctx')), may hold values from 8192 to 67108864
- out_cols: float32 [4096], P('tensor'), may hold values from 8192 to 67108864
- table_second: float32 [23, 4096], P(None, 'tensor'), may hold values from 8192 to 67108864
Outputs:
- mixed: bfloat16 [2, 4, 1024, 2048], P(None, 'dp', 'ctx')
- token_grad: bfloat16 [2, 4, 1024, 2048], P(None, 'dp', 'ctx')
- gain_grad: float32 [2048], P(('dp', 'ctx'))
- in_grad: float32 [2048, 2, 4096], P(('dp', 'ctx'), None, 'tensor')
- xproj_grad: float32 [160, 4096], P(('dp', 'ctx'), 'tensor')
- step_grad: float32 [128, 4096], P(('dp', 'ctx'), 'tensor')
- outproj_grad: float32 [2048, 4096], P(('dp', 'ctx'), 'tensor')
- table_grad: float32 [23, 4096], P(None, 'tensor')
- new_gain: float32 [2048], P(('dp', 'ctx'))
- new_in: float32 [2048, 2, 4096], P(('dp', 'ctx'), None, 'tensor')
- new_xproj: float32 [160, 4096], P(('dp', 'ctx'), 'tensor')
- new_step: float32 [128, 4096], P(('dp', 'ctx'), 'tensor')
- new_outproj: float32 [2048, 4096], P(('dp', 'ctx'), 'tensor')
- new_table: float32 [23, 4096], P(None, 'tensor')
- new_gain_second: float32 [2048], P(('dp', 'ctx'))
- new_in_rows: float32 [2048], P(('dp', 'ctx'))
- new_in_cols: float32 [2, 4096], P(None, 'tensor')
- new_xproj_rows: float32 [160], P(('dp', 'ctx'))
- new_xproj_cols: float32 [4096], P('tensor')
- new_step_rows: float32 [128], P(('dp', 'ctx'))
- new_step_cols: float32 [4096], P('tensor')
- new_out_rows: float32 [2048], P(('dp', 'ctx'))
- new_out_cols: float32 [4096], P('tensor')
- new_table_second: float32 [23, 4096], P(None, 'tensor')
- update_rms: float32 [6], replicated
All inputs are finite; a program needn't handle non-finite values.
Results may differ from a plain program's by a relative error of at most 0.018.
The roundings to bfloat16 on the way count: a program that leaves them out, or rounds other values in their place, can miss the bound.
Values may be sent and summed in bfloat16 or wider, within the bound.
No kernel may reach another device: no remote copies, remote signals or barrier semaphores. Data moves between devices by JAX's collectives and lax.ppermute only.
A program may use at most 768 MiB of HBM per device.

v0:
```python
import jax
import jax.numpy as jnp
from jax import lax
from jax.sharding import PartitionSpec as P

D = 2048
E = 4096
N = 16
R = 128
K = 4


norm_epsilon = 1e-05
square_floor = 1e-30
decay_rate = 0.5
clip_limit = 0.5
step_rate = 1.0
precision_highest_mode = lax.Precision.HIGHEST


def shifted(block, axis, distance):
    devices = range(lax.axis_size(axis))
    route = [(i - distance, i) for i in devices if i - distance in devices]
    return lax.ppermute(block, axis, route)


def prefix(part, axis, combine, identity, reverse):
    count = lax.axis_size(axis)
    place = lax.axis_index(axis)
    ahead = count - 1 - place if reverse else place
    gathered = jax.tree.map(lambda a: lax.all_gather(a, axis), part)
    state = jax.tree.map(lambda a, e: jnp.zeros_like(a) + jnp.asarray(e, a.dtype), part, identity)

    def one(lap, state):
        source = count - 1 - lap if reverse else lap
        return combine(
            state, jax.tree.map(lambda a: lax.dynamic_index_in_dim(a, source, 0, False), gathered)
        )

    return lax.fori_loop(0, ahead, one, state)


def silu_slope(value):
    sigma = jax.nn.sigmoid(value)
    return sigma * (1.0 + value * (1.0 - sigma))


def compose(earlier, later):
    return (later[0] * earlier[0], later[0] * earlier[1] + later[1])


def blocked(value, rows):
    return value.reshape((value.shape[0] // rows, rows) + value.shape[1:])


def unblocked(value):
    return value.reshape((value.shape[0] * value.shape[1],) + value.shape[2:])


def order_tables(rows):
    first = lax.broadcasted_iota(jnp.int32, (rows, rows), 0)
    second = lax.broadcasted_iota(jnp.int32, (rows, rows), 1)
    lower_triangle = (first >= second).astype(jnp.float32)
    strict_upper = (second > first).astype(jnp.float32)
    return (lower_triangle, strict_upper)


def local_forward(step_size, values, b_coef, a_neg, rows):
    lower_triangle, strict_upper = order_tables(rows)
    keep = lower_triangle[:, :, None, None] > 0.5

    def advance(carry, item):
        state, through = carry
        logarithm_decay = item[0][:, None, :] * a_neg[None]
        driving_input = (item[0] * item[1])[:, None, :] * item[2][:, :, None]
        running_total = jnp.einsum(
            "mh,hvp->mvp", lower_triangle, logarithm_decay, precision=precision_highest_mode
        )
        gap = jnp.minimum(running_total[:, None] - running_total[None, :], 0.0)
        weight_matrix = jnp.where(keep, jnp.exp(gap), 0.0)
        entering = jnp.exp(running_total)
        states = (
            jnp.einsum(
                "mrfc,rfc->mfc", weight_matrix, driving_input, precision=precision_highest_mode
            )
            + entering * state[None]
        )
        throughs = entering * through[None]
        return ((states[-1], throughs[-1]), (states, throughs))

    start = (jnp.zeros(a_neg.shape, jnp.float32), jnp.ones(a_neg.shape, jnp.float32))
    carry, outs = lax.scan(
        advance, start, (blocked(step_size, rows), blocked(values, rows), blocked(b_coef, rows))
    )
    return (unblocked(outs[0]), unblocked(outs[1]))


def local_adjoint(step_size, c_coef, scan_grad, a_neg, rows):
    lower_triangle, strict_upper = order_tables(rows)
    keep = jnp.transpose(lower_triangle)[:, :, None, None] > 0.5

    def retreat(carry, item):
        tail, factor = carry
        logarithm_decay = item[0][:, None, :] * a_neg[None]
        source_values = item[1][:, :, None] * item[2][:, None, :]
        running_total = jnp.einsum(
            "tu,une->tne", strict_upper, logarithm_decay, precision=precision_highest_mode
        )
        gap = jnp.minimum(running_total[:, None] - running_total[None, :], 0.0)
        weight_matrix = jnp.where(keep, jnp.exp(gap), 0.0)
        leaving = jnp.exp(running_total)
        adjoint = (
            jnp.einsum(
                "mrfc,rfc->mfc", weight_matrix, source_values, precision=precision_highest_mode
            )
            + leaving * tail[None]
        )
        factors = leaving * factor[None]
        first_decay = jnp.exp(logarithm_decay[0])
        return ((first_decay * adjoint[0], first_decay * factors[0]), (adjoint, factors))

    start = (jnp.zeros(a_neg.shape, jnp.float32), jnp.ones(a_neg.shape, jnp.float32))
    carry, outs = lax.scan(
        retreat,
        start,
        (blocked(step_size, rows), blocked(c_coef, rows), blocked(scan_grad, rows)),
        reverse=True,
    )
    return (unblocked(outs[0]), unblocked(outs[1]), carry[0])


def channel_total(term):
    return lax.psum(term, "tensor")


def feature_total(term):
    return lax.psum(term, "tensor")


def token_formula(grad_normed, input_value, inverse, grad_out_low, gain_value):
    scaled = gain_value * grad_normed
    grad_x = inverse * scaled - input_value * inverse * inverse * inverse * jnp.mean(
        input_value * scaled, axis=1, keepdims=True
    )
    return (grad_out_low.astype(jnp.float32) + grad_x).astype(jnp.bfloat16)


def reduce_grads(gain_part, in_part, xproj_part, step_part, outproj_part):
    return (
        lax.psum_scatter(gain_part, ("dp", "ctx"), scatter_dimension=0, tiled=True),
        lax.psum_scatter(in_part, ("dp", "ctx"), scatter_dimension=0, tiled=True),
        lax.psum_scatter(xproj_part, ("dp", "ctx"), scatter_dimension=0, tiled=True),
        lax.psum_scatter(step_part, ("dp", "ctx"), scatter_dimension=0, tiled=True),
        lax.psum_scatter(outproj_part, ("dp", "ctx"), scatter_dimension=0, tiled=True),
    )


def per_device(
    tokens,
    out_grad,
    norm_gain,
    in_weight,
    xproj_weight,
    step_weight,
    outproj_weight,
    channel_table,
    gain_second,
    in_rows,
    in_cols,
    xproj_rows,
    xproj_cols,
    step_rows,
    step_cols,
    out_rows,
    out_cols,
    table_second,
):
    micro = tokens.shape[0]
    length = tokens.shape[2]
    inner = in_weight.shape[2]
    rows = min(16, length)
    n_tensor = lax.axis_size("tensor")
    tensor_index = lax.axis_index("tensor")
    row_share = length // n_tensor
    row_start = tensor_index * row_share
    gain_low, in_low, xproj_low, step_low, outproj_low = (
        lax.all_gather(norm_gain.astype(jnp.bfloat16), ("dp", "ctx"), axis=0, tiled=True),
        lax.all_gather(in_weight.astype(jnp.bfloat16), ("dp", "ctx"), axis=0, tiled=True),
        lax.all_gather(xproj_weight.astype(jnp.bfloat16), ("dp", "ctx"), axis=0, tiled=True),
        lax.all_gather(step_weight.astype(jnp.bfloat16), ("dp", "ctx"), axis=0, tiled=True),
        lax.all_gather(outproj_weight.astype(jnp.bfloat16), ("dp", "ctx"), axis=0, tiled=True),
    )
    in_matrix = in_low.reshape(D, 2 * inner)
    gain_value = gain_low.astype(jnp.float32)
    taps = channel_table[:K]
    conv_bias = channel_table[K]
    step_bias = channel_table[K + 1]
    skip = channel_table[K + 2]
    a_neg = -jnp.exp(channel_table[K + 3 :])
    ones_state = jnp.ones(a_neg.shape, jnp.float32)
    zero_state = jnp.zeros(a_neg.shape, jnp.float32)
    grad_table = jnp.zeros(channel_table.shape, jnp.float32)
    mixed_list = []
    token_list = []
    micro_grads = []
    for m in range(micro):
        input_value = tokens[m, 0].astype(jnp.float32)
        inverse = lax.rsqrt(
            jnp.mean(input_value * input_value, axis=1, keepdims=True) + norm_epsilon
        )
        x_rows = lax.dynamic_slice_in_dim(input_value, row_start, row_share, 0)
        inverse_rows = lax.dynamic_slice_in_dim(inverse, row_start, row_share, 0)
        normalized_rows = (input_value * inverse * gain_value).astype(jnp.bfloat16)
        mixer_input = jnp.dot(
            normalized_rows, in_matrix, preferred_element_type=jnp.float32
        ).astype(jnp.bfloat16)
        conv_in = mixer_input[:, :inner]
        gate_in = mixer_input[:, inner:].astype(jnp.float32)
        earlier = shifted(conv_in[length - (K - 1) :], "ctx", 1)
        padded = jnp.concatenate([earlier, conv_in], axis=0).astype(jnp.float32)
        conv = conv_bias + taps[0] * padded[0:length]
        for k in range(1, K):
            conv = conv + taps[k] * padded[k : k + length]
        values_low = jax.nn.silu(conv).astype(jnp.bfloat16)
        values = values_low.astype(jnp.float32)
        proj = channel_total(
            jnp.einsum("te,pe->tp", values_low, xproj_low, preferred_element_type=jnp.float32)
        )
        rank_low = proj[:, :R].astype(jnp.bfloat16)
        b_coef = proj[:, R : R + N]
        c_coef = proj[:, R + N :]
        pre = jnp.dot(rank_low, step_low, preferred_element_type=jnp.float32) + step_bias
        step_size = jax.nn.softplus(pre)
        local_states, throughs = local_forward(step_size, values, b_coef, a_neg, rows)
        through_all = throughs[-1]
        carried = prefix(
            (through_all, local_states[-1]), "ctx", compose, (ones_state, zero_state), False
        )
        start = carried[1]
        states = local_states + throughs * start[None]
        scan_out = jnp.einsum("tne,tn->te", states, c_coef) + skip * values
        gate = jax.nn.silu(gate_in)
        gated_output = (scan_out * gate).astype(jnp.bfloat16)
        branch = feature_total(
            jnp.einsum("te,de->td", gated_output, outproj_low, preferred_element_type=jnp.float32)
        )
        mixed_list.append((input_value + branch).astype(jnp.bfloat16))
        grad_out_low = out_grad[m, 0]
        grad_gated = jnp.dot(grad_out_low, outproj_low, preferred_element_type=jnp.float32)
        part_outproj = jnp.einsum(
            "td,te->de", grad_out_low, gated_output, preferred_element_type=jnp.float32
        )
        scan_grad = grad_gated * gate
        gate_grad = grad_gated * scan_out * silu_slope(gate_in)
        adjoint_local, factors, head = local_adjoint(step_size, c_coef, scan_grad, a_neg, rows)
        later = prefix((through_all, head), "ctx", compose, (ones_state, zero_state), True)
        adjoint = adjoint_local + factors * later[1][None]
        before = jnp.concatenate([start[None], states[:-1]], axis=0)
        decay = jnp.exp(step_size[:, None, :] * a_neg[None])
        through = adjoint * before * decay
        along_b = jnp.einsum("tne,tn->te", adjoint, b_coef)
        grad_size = along_b * values + jnp.einsum("tne,ne->te", through, a_neg)
        grad_values = along_b * step_size + skip * scan_grad
        grad_bcoef = jnp.einsum("tne,te->tn", adjoint, step_size * values)
        grad_ccoef = jnp.einsum("tne,te->tn", states, scan_grad)
        grad_rate = jnp.einsum("tne,te->ne", through, step_size)
        grad_skip = jnp.sum(scan_grad * values, axis=0)
        grad_pre = grad_size * jax.nn.sigmoid(pre)
        grad_bias = jnp.sum(grad_pre, axis=0)
        pre_low = grad_pre.astype(jnp.bfloat16)
        part_step = jnp.einsum("tr,te->re", rank_low, pre_low, preferred_element_type=jnp.float32)
        grad_rank = jnp.einsum("te,re->tr", pre_low, step_low, preferred_element_type=jnp.float32)
        proj_grad = channel_total(
            jnp.concatenate([grad_rank, grad_bcoef, grad_ccoef], axis=1)
        ).astype(jnp.bfloat16)
        part_xproj = jnp.einsum(
            "tp,te->pe", proj_grad, values_low, preferred_element_type=jnp.float32
        )
        grad_values = grad_values + jnp.dot(
            proj_grad, xproj_low, preferred_element_type=jnp.float32
        )
        grad_conv = grad_values * silu_slope(conv)
        grad_taps = jnp.stack(
            [jnp.sum(grad_conv * padded[k : k + length], axis=0) for k in range(K)]
        )
        tail_zeros = jnp.zeros((K - 1, inner), jnp.float32)
        extended = jnp.concatenate([grad_conv, tail_zeros], axis=0)
        grad_conv_in = taps[K - 1] * extended[0:length]
        for k in range(K - 1):
            grad_conv_in = grad_conv_in + taps[k] * extended[K - 1 - k : K - 1 - k + length]
        head_rows = []
        for p in range(K - 1):
            total = taps[0] * grad_conv[p]
            for k in range(1, p + 1):
                total = total + taps[k] * grad_conv[p - k]
            head_rows.append(total)
        head_grads = jnp.stack(head_rows)
        returned = shifted(head_grads, "ctx", -1)
        grad_conv_in = jnp.concatenate(
            [grad_conv_in[: length - (K - 1)], grad_conv_in[length - (K - 1) :] + returned], axis=0
        )
        grad_mixed = jnp.concatenate([grad_conv_in, gate_grad], axis=1).astype(jnp.bfloat16)
        part_in = jnp.einsum(
            "td,tk->dk", normalized_rows, grad_mixed, preferred_element_type=jnp.float32
        )
        grad_normed = feature_total(
            jnp.einsum("tk,dk->td", grad_mixed, in_matrix, preferred_element_type=jnp.float32)
        )
        grad_rows = lax.dynamic_slice_in_dim(grad_normed, row_start, row_share, 0)
        token_list.append(
            token_formula(grad_normed, input_value, inverse, grad_out_low, gain_value)
        )
        part_gain = jnp.sum(grad_rows * x_rows * inverse_rows, axis=0)
        channel_rows = jnp.stack([jnp.sum(grad_conv, axis=0), grad_bias, grad_skip])
        grad_table = grad_table + jnp.concatenate(
            [grad_taps, channel_rows, grad_rate * a_neg], axis=0
        )
        micro_grads.append((part_gain, part_in, part_xproj, part_step, part_outproj))
    summed_parts = micro_grads[0]
    for part in micro_grads[1:]:
        summed_parts = tuple((summed_parts[i] + part[i] for i in range(5)))
    shards = reduce_grads(
        summed_parts[0], summed_parts[1], summed_parts[2], summed_parts[3], summed_parts[4]
    )
    gain_partial = shards[0]
    shard_in = shards[1].reshape(in_weight.shape)
    matrices = (shard_in, shards[2], shards[3], shards[4])
    weights = (in_weight, xproj_weight, step_weight, outproj_weight)
    old_rows = (in_rows, xproj_rows, step_rows, out_rows)
    old_cols = (in_cols, xproj_cols, step_cols, out_cols)
    width_cols = (2 * E, E, E, E)
    width_rows = (D, R + 2 * N, R, D)
    squares = [matrix * matrix + square_floor for matrix in matrices]
    row_parts = [jnp.sum(square.reshape(square.shape[0], -1), axis=1) for square in squares]
    col_parts = [jnp.sum(square, axis=0) for square in squares]
    row_sums = lax.psum(
        (row_parts[0], row_parts[1], row_parts[2], row_parts[3], gain_partial), "tensor"
    )
    row_news = [
        decay_rate * old_rows[i] + (1.0 - decay_rate) * row_sums[i] / width_cols[i]
        for i in range(4)
    ]
    shard_gain = row_sums[4]
    totals_local = jnp.stack([jnp.sum(row_new) for row_new in row_news])
    summed = lax.psum(
        (col_parts[0], col_parts[1], col_parts[2], col_parts[3], totals_local, grad_table),
        ("dp", "ctx"),
    )
    col_sums = summed[:4]
    row_totals = summed[4]
    table_grad = summed[5]
    col_news = [
        decay_rate * old_cols[i] + (1.0 - decay_rate) * col_sums[i] / width_rows[i]
        for i in range(4)
    ]
    updates = []
    for i in range(4):
        row_mean = row_totals[i] / width_rows[i]
        shape = (-1,) + (1,) * (matrices[i].ndim - 1)
        second = row_news[i].reshape(shape) * col_news[i][None] / row_mean
        updates.append(matrices[i] * lax.rsqrt(second))
    new_gain_second = decay_rate * gain_second + (1.0 - decay_rate) * (
        shard_gain * shard_gain + square_floor
    )
    gain_update = shard_gain * lax.rsqrt(new_gain_second)
    new_table_second = decay_rate * table_second + (1.0 - decay_rate) * (
        table_grad * table_grad + square_floor
    )
    table_update = table_grad * lax.rsqrt(new_table_second)
    n_owner = lax.axis_size("dp") * lax.axis_size("ctx")
    all_updates = [gain_update] + updates + [table_update]
    all_weights = [norm_gain] + list(weights) + [channel_table]
    shares = [1.0 / n_tensor, 1.0, 1.0, 1.0, 1.0, 1.0 / n_owner]
    update_sq = jnp.stack([jnp.sum(all_updates[i] * all_updates[i]) * shares[i] for i in range(6)])
    weight_sq = jnp.stack([jnp.sum(all_weights[i] * all_weights[i]) * shares[i] for i in range(6)])
    total_update, total_weight = lax.psum((update_sq, weight_sq), ("dp", "ctx", "tensor"))
    counts = jnp.array([D, 2 * D * E, (R + 2 * N) * E, R * E, D * E, (K + 3 + N) * E], jnp.float32)
    update_rms = jnp.sqrt(total_update / counts)
    factor = jnp.maximum(1.0, update_rms / clip_limit)
    scale = jnp.sqrt(total_weight / counts)
    stride = step_rate * scale / factor
    new_weights = [all_weights[i] - stride[i] * all_updates[i] for i in range(6)]
    mixed = jnp.stack(mixed_list)[:, None]
    token_grad = jnp.stack(token_list)[:, None]
    return (
        mixed,
        token_grad,
        shard_gain,
        shard_in,
        shards[2],
        shards[3],
        shards[4],
        table_grad,
        new_weights[0],
        new_weights[1],
        new_weights[2],
        new_weights[3],
        new_weights[4],
        new_weights[5],
        new_gain_second,
        row_news[0],
        col_news[0],
        row_news[1],
        col_news[1],
        row_news[2],
        col_news[2],
        row_news[3],
        col_news[3],
        new_table_second,
        update_rms,
    )


def solution(mesh):
    return jax.shard_map(
        per_device,
        mesh=mesh,
        in_specs=(
            P(None, "dp", "ctx", None),
            P(None, "dp", "ctx", None),
            P(("dp", "ctx")),
            P(("dp", "ctx"), None, "tensor"),
            P(("dp", "ctx"), "tensor"),
            P(("dp", "ctx"), "tensor"),
            P(("dp", "ctx"), "tensor"),
            P(None, "tensor"),
            P(("dp", "ctx")),
            P(("dp", "ctx")),
            P(None, "tensor"),
            P(("dp", "ctx")),
            P("tensor"),
            P(("dp", "ctx")),
            P("tensor"),
            P(("dp", "ctx")),
            P("tensor"),
            P(None, "tensor"),
        ),
        out_specs=(
            P(None, "dp", "ctx", None),
            P(None, "dp", "ctx", None),
            P(("dp", "ctx")),
            P(("dp", "ctx"), None, "tensor"),
            P(("dp", "ctx"), "tensor"),
            P(("dp", "ctx"), "tensor"),
            P(("dp", "ctx"), "tensor"),
            P(None, "tensor"),
            P(("dp", "ctx")),
            P(("dp", "ctx"), None, "tensor"),
            P(("dp", "ctx"), "tensor"),
            P(("dp", "ctx"), "tensor"),
            P(("dp", "ctx"), "tensor"),
            P(None, "tensor"),
            P(("dp", "ctx")),
            P(("dp", "ctx")),
            P(None, "tensor"),
            P(("dp", "ctx")),
            P("tensor"),
            P(("dp", "ctx")),
            P("tensor"),
            P(("dp", "ctx")),
            P("tensor"),
            P(None, "tensor"),
            P(),
        ),
        check_vma=False,
    )
```

profile of v0, /device:TPU:0, one launch (start us, length us, event | category | flops | bytes accessed | tf_op | source)
XLA Modules:
  0.0 3243.6 jit_solution(7707444605105938425)
XLA Ops:
  56.6 50.4 %all-gather.7.cloned.1.call-done = bf16[2048,2,1024]{2,1,0:T(2,128)(2,1)} async-done(((bf16[256,2,1024]{2,1,0:T(2,128)(2,1)}), bf16[2048,2,1024]{2,1,0:T(2,128)(2,1)}) %all-gather.7.cloned.1.call-update) | async-done | bytes 8388624 | tf_op jit(solution)/shard_map/all_gather | solution.py:188
  125.8 13.8 collective-permute-start.1
  178.7 27.9 all-reduce.20.cloned.1.call-done
  249.5 382.5 %while.134 = (s32[]{:T(128)}, f32[16,1024]{1,0:T(8,128)S(1)}, f32[16,1024]{1,0:T(8,128)S(1)}, f32[32,16,16,1024]{3,2,1,0:T(8,128)}, f32[32,16,16,1024]{3,2,1,0:T...) while((s32[]{:T(128)}, f32[16,1024]{1,0:T(8,128)S(1)}, ...), condition=%wide.region_15.16_spmd.clone, body=%wide.region_14.15_spmd.clone.sunk | while | flops 72647936 | bytes 18091656 | solution.py:123
  656.7 357.3 %while.132 = (s32[]{:T(128)}, f32[16,1024]{1,0:T(8,128)S(1)}, f32[16,1024]{1,0:T(8,128)S(1)}, f32[32,16,16,1024]{3,2,1,0:T(8,128)}, f32[32,16,16,1024]{3,2,1,0:T...) while((s32[]{:T(128)}, f32[16,1024]{1,0:T(8,128)S(1)}, ...), condition=%wide.region_3.4_spmd.clone, body=%wide.region_2.3_spmd.clone.sunk | while | flops 72369408 | bytes 16911996 | solution.py:92
  1022.0 33.8 %multiply_add_fusion.1 = f32[512,16,1024]{2,1,0:T(8,128)} fusion(f32[16,1024]{1,0:T(8,128)S(1)} %get-tuple-element.837, f32[32,16,16,1024]{3,2,1,0:T(8,128)} %get-tuple-element.836, f32[32,16,16,1024]{3,2,1,0:T(8,128)} %get-tuple-element.835), kind=kLoop, calls=%fused_computation.115 | loop fusion | flops 16777216 | bytes 100728832 | tf_op jit(solution)/shard_map/add | solution.py:240
  1055.8 22.8 slice.415
  1114.4 379.5 %while.133 = (s32[]{:T(128)}, f32[16,1024]{1,0:T(8,128)S(1)}, f32[16,1024]{1,0:T(8,128)S(1)}, f32[32,16,16,1024]{3,2,1,0:T(8,128)}, f32[32,16,16,1024]{3,2,1,0:T...) while((s32[]{:T(128)}, f32[16,1024]{1,0:T(8,128)S(1)}, ...), condition=%wide.region_10.11_spmd.clone, body=%wide.region_9.10_spmd.clone.sunk | while | flops 72369408 | bytes 16911996 | solution.py:92
  1499.6 33.8 %multiply_add_fusion = f32[512,16,1024]{2,1,0:T(8,128)} fusion(f32[16,1024]{1,0:T(8,128)S(1)} %get-tuple-element.840, f32[32,16,16,1024]{3,2,1,0:T(8,128)} %get-tuple-element.839, f32[32,16,16,1024]{3,2,1,0:T(8,128)} %get-tuple-element.838), kind=kLoop, calls=%fused_computation.114 | loop fusion | flops 16777216 | bytes 100728832 | tf_op jit(solution)/shard_map/add | solution.py:240
  1533.4 22.8 slice.421
  1591.9 382.6 %while.135 = (s32[]{:T(128)}, f32[16,1024]{1,0:T(8,128)S(1)}, f32[16,1024]{1,0:T(8,128)S(1)}, f32[32,16,16,1024]{3,2,1,0:T(8,128)}, f32[32,16,16,1024]{3,2,1,0:T...) while((s32[]{:T(128)}, f32[16,1024]{1,0:T(8,128)S(1)}, ...), condition=%wide.region_22.23_spmd.clone, body=%wide.region_21.22_spmd.clone.sunk | while | flops 72647936 | bytes 18091656 | solution.py:123
  1976.7 87.8 %multiply_reduce_fusion.4 = (f32[1024,16]{0,1:T(8,128)S(1)}, f32[1024,16]{0,1:T(8,128)S(1)}, f32[512,16,1024]{2,1,0:T(8,128)}, f32[512,16,1024]{2,1,0:T(8,128)}) fusion(f32[1024,512]{0,1:T(8,128)S(1)} %bitcast.588, f32[16,1024]{1,0:T(8,128)S(1)} %get-tuple-element.2096, f32[512,1024]{1,0:T(8,128)S(1)} %bitcast.587, f32[511,16,1024]{2,1,0:T(8,128)} %slice.421, ...), kind=kLoop, calls=%fused_computation.110 | loop fusion | flops 134184960 | bytes 277151744 | tf_op jit(solution)/shard_map/tne,te->ne/dot_general | solution.py:266
  2078.3 46.2 %multiply_reduce_fusion.7 = (f32[1024,512]{0,1:T(8,128)}, f32[1024,512]{0,1:T(8,128)}) fusion(f32[1024,16]{0,1:T(8,128)S(1)} %get-tuple-element.1372, f32[16,1024]{1,0:T(8,128)S(1)} %get-tuple-element.2096, f32[512,1024]{1,0:T(8,128)} %bitcast.594, f32[512,16,1024]{2,1,0:T(8,128)} %get-tuple-element.1286, f32[511,16,1024]{2,1,0:T(8,128)} %slice.415, ...), kind=kLoop, calls=%fused_computation.113 | loop fusion | flops 99614720 | bytes 142737408 | tf_op jit(solution)/shard_map/tne,ne->te/dot_general | solution.py:262
  2152.8 14.1 fusion.109
  2167.0 14.2 fusion.105
  2181.3 14.4 fusion.107
  2196.8 14.3 fusion.111
  2214.0 31.5 all-reduce.21
  2352.8 18.6 fusion.16
  2378.5 44.5 %reduce-scatter.10.cloned.1.call-done = f32[256,1024]{0,1:T(8,128)} async-done(((f32[2048,1024]{0,1:T(8,128)}), f32[256,1024]{0,1:T(8,128)}) %reduce-scatter.10.cloned.1.call-update) | async-done | bytes 1048592 | tf_op jit(solution)/shard_map/reduce_scatter | solution.py:154
  2425.9 566.2 %all-reduce.18.cloned.1.call-done = (f32[512,2048]{1,0:T(8,128)}, f32[512,2048]{1,0:T(8,128)}, f32[512,2048]{1,0:T(8,128)}, f32[512,2048]{1,0:T(8,128)}) async-done(((f32[512,2048]{1,0:T(8,128)}, f32[512,2048]{1,0:T(8,128)}, f32[512,2048]{1,0:T(8,128)}, f32[512,2048]{1,0:T(8,128)}), (f32[512,2048]{1,0:T(8,128)}, f32[512,2048]{1,0:T(8,128)}, f32[512,2048]{1,0:T(8,128)}, ...) | async-done | bytes 16777232 | tf_op jit(solution)/shard_map/psum | solution.py:137
  3018.2 92.7 %reduce-scatter.6.cloned.1.call-done = f32[256,2048]{1,0:T(8,128)} async-done(((f32[2048,2048]{1,0:T(8,128)}), f32[256,2048]{1,0:T(8,128)}) %reduce-scatter.6.cloned.1.call-update) | async-done | bytes 2097168 | tf_op jit(solution)/shard_map/reduce_scatter | solution.py:151
  3129.3 22.4 all-reduce.6
  3175.9 39.8 %all-reduce.5 = (f32[6]{0:T(128)S(1)}, f32[6]{0:T(128)S(1)}) all-reduce(f32[6]{0:T(128)S(1)} %stack.157, f32[6]{0:T(128)S(1)} %stack.169), channel_id=1, replica_groups=mesh['dp'=4,'ctx'=2,'tensor'=4] {'dp','ctx','tensor'}, use_global_device_ids=true, to_apply=%region_57.58 | all-reduce | flops 12 | bytes 96 | tf_op jit(solution)/shard_map/psum | solution.py:376
  (2115 shorter events, 2002.4 us)
Async XLA Ops:
  7.2 42.9 %all-gather.9.cloned.1.call-start = ((), (), s32[]{:S(2)}) async-start(), calls=%async_computation.4 | async-start | bytes 4718592 | tf_op jit(solution)/shard_map/all_gather | solution.py:191
  10.6 96.4 %all-gather.7.cloned.1.call-start = ((), (), s32[]{:S(2)}) async-start(), calls=%async_computation.3 | async-start | bytes 9437184 | tf_op jit(solution)/shard_map/all_gather | solution.py:188
  14.3 192.2 %all-reduce.20.cloned.1.call-start = ((), (), s32[]{:S(2)}) async-start(), calls=%async_computation.10 | async-start | bytes 1310720 | tf_op jit(solution)/shard_map/psum | solution.py:133
  25.3 114.3 %copy-start.69 = (f32[8,1,256]{2,1,0:T(1,128)}, f32[8,1,256]{2,1,0:T(1,128)S(1)}, u32[]{:S(2)}) copy-start(f32[8,1,256]{2,1,0:T(1,128)S(1)} %convert_element_type.197) | copy-start | bytes 24580
  35.6 128.7 %copy-start.38 = (bf16[160,1024]{1,0:T(8,128)(2,1)}, bf16[160,1024]{1,0:T(8,128)(2,1)S(1)}, u32[]{:S(2)}) copy-start(bf16[160,1024]{1,0:T(8,128)(2,1)S(1)} %reshape.354) | copy-start | bytes 983044
  125.8 21.4 collective-permute-start.1
  145.9 2.1 collective-permute-start
  165.6 2208.6 %all-reduce.16.cloned.1.call-start = ((), (), s32[]{:S(2)}) async-start(), calls=%async_computation.8 | async-start | bytes 196608 | tf_op jit(solution)/shard_map/psum | solution.py:345
  1591.9 384.8 %copy-start.30 = (f32[16,1024]{1,0:T(8,128)S(1)}, f32[16,1024]{1,0:T(8,128)}, u32[]{:S(2)}) copy-start(f32[16,1024]{1,0:T(8,128)} %copy-done.29) | copy-start | bytes 196612
  2259.5 118.0 %reduce-scatter.8.cloned.1.call-start = ((), (), s32[]{:S(2)}) async-start(), calls=%async_computation.6 | async-start | bytes 589824 | tf_op jit(solution)/shard_map/reduce_scatter | solution.py:153
  2268.2 154.9 %reduce-scatter.10.cloned.1.call-start = ((), (), s32[]{:S(2)}) async-start(), calls=%async_computation.7 | async-start | bytes 9437184 | tf_op jit(solution)/shard_map/reduce_scatter | solution.py:154
  2278.0 714.1 %all-reduce.18.cloned.1.call-start = ((), (), s32[]{:S(2)}) async-start(), calls=%async_computation.9 | async-start | bytes 33554432 | tf_op jit(solution)/shard_map/psum | solution.py:137
  2279.7 15.7 collective-permute-start.3
  2293.5 3.5 collective-permute-start.2
  2309.7 801.2 %reduce-scatter.6.cloned.1.call-start = ((), (), s32[]{:S(2)}) async-start(), calls=%async_computation.5 | async-start | bytes 18874368 | tf_op jit(solution)/shard_map/reduce_scatter | solution.py:151
  2371.4 5.7 collective-permute-start.4
  2372.7 4.4 collective-permute-start.5
  2377.5 845.2 %copy-start.59 = (f32[20,1024]{1,0:T(8,128)}, f32[20,1024]{1,0:T(8,128)S(1)}, u32[]{:S(2)}) copy-start(f32[20,1024]{1,0:T(8,128)S(1)} %get-tuple-element.2052) | copy-start | bytes 245764
  3018.1 142.0 %copy-start.113 = (f32[256]{0:T(256)S(1)}, f32[256]{0:T(256)}, u32[]{:S(2)}) copy-start(f32[256]{0:T(256)} %param.43) | copy-start | bytes 3076
  3018.1 145.2 %copy-start.96 = (f32[2,1024]{1,0:T(2,128)S(1)}, f32[2,1024]{1,0:T(2,128)}, u32[]{:S(2)}) copy-start(f32[2,1024]{1,0:T(2,128)} %param.45) | copy-start | bytes 24580
  3018.1 146.5 %copy-start.102 = (f32[1024]{0:T(1024)S(1)}, f32[1024]{0:T(1024)}, u32[]{:S(2)}) copy-start(f32[1024]{0:T(1024)} %param.47) | copy-start | bytes 12292
  3018.1 146.5 %copy-start.103 = (f32[1024]{0:T(1024)S(1)}, f32[1024]{0:T(1024)}, u32[]{:S(2)}) copy-start(f32[1024]{0:T(1024)} %param.49) | copy-start | bytes 12292
  3018.1 146.5 %copy-start.104 = (f32[1024]{0:T(1024)S(1)}, f32[1024]{0:T(1024)}, u32[]{:S(2)}) copy-start(f32[1024]{0:T(1024)} %param.51) | copy-start | bytes 12292
  3018.1 147.3 %copy-start.61 = (f32[16,1024]{1,0:T(8,128)S(1)}, f32[16,1024]{1,0:T(8,128)}, u32[]{:S(2)}) copy-start(f32[16,1024]{1,0:T(8,128)} %reduce-scatter.8.cloned.1.call-done) | copy-start | bytes 196612
  (113 other events, 2942.3 us)
Sparse Core Ops, SparseCore 0:
  10.7 39.4 all-gather.8
  52.6 54.3 all-gather.6
  165.7 40.7 all-reduce.19
  2259.6 49.9 all-reduce.15
  2313.5 34.9 reduce-scatter.7
  2351.7 71.2 reduce-scatter.9
  2426.8 565.2 all-reduce.17
  2996.1 114.7 reduce-scatter.5
where the time goes:
time: 3260 us; the launch traced here: 3240 us
  other arithmetic  1120 us (34%)
  waiting for transfers between devices  793 us (24%)
  local copies, waits for them, and re-layouts  736 us (23%)
  matrix products  363 us (11%)
  blocking collectives  173 us (5%)
    while x256, other arithmetic  643 us
    psum x1, waiting for transfers between devices, feature_total(): return lax.psum(term, 'tensor')  566 us
    dynamic_update_slice x128, local copies, waits for them, and re-layouts, local_forward(): lax.scan(advance, start, (blocked(step_size, rows), blocked(values, rows)...  328 us
    mul x128, local copies, waits for them, and re-layouts, retreat(): source_values = item[1][:, :, None] * item[2][:, None, :]  98.7 us
    reduce_scatter x1, waiting for transfers between devices, reduce_grads(): lax.psum_scatter(in_part, ('dp', 'ctx'), scatter_dimension=0, tiled=True)  92.7 us
    another operation x22, local copies, waits for them, and re-layouts  91.2 us
    dot_general x1, other arithmetic, per_device(): grad_rate = jnp.einsum('tne,te->ne', through, step_size)  87.8 us
    dot_general x64, matrix products, retreat(): jnp.einsum('tu,une->tne', strict_upper, logarithm_decay, precision=precis...  69 us
  transfers between devices with their start and end apart: 14, of which 8 were waited for; matrix products, arithmetic and copies ran while one was open for 5% of the time, Pallas kernels for 0%

commit v1 on v0

v1 whole, which is shorter than its diff:
```python
import functools
import math

import jax
import jax.numpy as jnp
from jax import lax
from jax.experimental import pallas as pl
from jax.experimental.pallas import tpu as pltpu
from jax.sharding import PartitionSpec as P

D = 2048
E = 4096
N = 16
R = 128
K = 4
LANES = 128
LOG_2 = math.log(2.0)
LOW = jnp.bfloat16
FULL = jnp.float32

norm_epsilon = 1e-05
square_floor = 1e-30
decay_rate = 0.5
clip_limit = 0.5
step_rate = 1.0


def bits(axis):
    size = lax.axis_size(axis)
    return [1 << b for b in range(size.bit_length() - 1)]


def swap(block, axis, bit):
    return lax.ppermute(block, axis, [(i, i ^ bit) for i in range(lax.axis_size(axis))])


def shifted(block, axis, distance):
    devices = range(lax.axis_size(axis))
    route = [(i - distance, i) for i in devices if i - distance in devices]
    return lax.ppermute(block, axis, route)


def butterfly(value, axes):
    for axis in axes:
        for bit in bits(axis):
            value = value + swap(value, axis, bit)
    return value


def relative_blocks():
    n_dp, n_ctx = lax.axis_size("dp"), lax.axis_size("ctx")
    dp, ctx = lax.axis_index("dp"), lax.axis_index("ctx")
    return [
        (dp ^ (q % n_dp)) * n_ctx + (ctx ^ (q // n_dp)) for q in range(n_dp * n_ctx)
    ], [
        (ctx ^ (j % n_ctx)) * n_dp + (dp ^ (j // n_ctx)) for j in range(n_dp * n_ctx)
    ]


def pick(blocks, order):
    return jnp.stack([lax.dynamic_index_in_dim(blocks, q, 0, False) for q in order])


def pick_columns(rows, order):
    width = rows.shape[1] // len(order)
    return jnp.concatenate(
        [lax.dynamic_slice_in_dim(rows, q * width, width, 1) for q in order], axis=1
    )


def gather(own):
    if lax.axis_size("dp") == 4:
        half = own.shape[0] // 2
        one = swap(own, "dp", 1)
        two = swap(own, "dp", 2)
        three = [swap(two[:half], "dp", 1), swap(one[half:], "dp", 2)]
        whole = jnp.concatenate([own, one, two] + three, axis=0)
    else:
        whole = own
        for bit in bits("dp"):
            whole = jnp.concatenate([whole, swap(whole, "dp", bit)], axis=0)
    for bit in bits("ctx"):
        whole = jnp.concatenate([whole, swap(whole, "ctx", bit)], axis=0)
    return whole


def scatter(parts):
    for bit in reversed(bits("ctx")):
        half = parts.shape[0] // 2
        parts = (
            parts[:half].astype(FULL) + swap(parts[half:], "ctx", bit).astype(FULL)
        ).astype(LOW)
    if lax.axis_size("dp") == 4:
        half = parts.shape[2] // 2
        left, right = parts[:, :, :half], parts[:, :, half:]
        got_left = swap(jnp.stack([left[1], left[3]]), "dp", 1).astype(FULL)
        got_right = swap(right[2:], "dp", 2).astype(FULL)
        far_left = (left[2].astype(FULL) + got_left[1]).astype(LOW)
        far_right = (right[1].astype(FULL) + got_right[1]).astype(LOW)
        end_left = swap(far_left, "dp", 2).astype(FULL)
        end_right = swap(far_right, "dp", 1).astype(FULL)
        return jnp.concatenate(
            [
                left[0].astype(FULL) + got_left[0] + end_left,
                right[0].astype(FULL) + got_right[0] + end_right,
            ],
            axis=1,
        )
    for bit in reversed(bits("dp")):
        half = parts.shape[0] // 2
        parts = parts[:half].astype(FULL) + swap(parts[half:].astype(LOW), "dp", bit).astype(FULL)
    return parts[0].astype(FULL)


def line_scatter(parts):
    n = lax.axis_size("tensor")
    me = lax.axis_index("tensor")

    def part(index):
        return lax.dynamic_index_in_dim(parts, jnp.clip(index, 0, n - 1), 0, False)

    total = part(me).astype(FULL)
    up = down = None
    for s in range(1, n):
        send_up, send_down = part(n - s + me), part(s - n + me)
        if up is not None:
            send_up = (send_up.astype(FULL) + up.astype(FULL)).astype(LOW)
            send_down = (send_down.astype(FULL) + down.astype(FULL)).astype(LOW)
        up = lax.ppermute(send_up, "tensor", [(i, i + 1) for i in range(s)])
        down = lax.ppermute(send_down, "tensor", [(i, i - 1) for i in range(n - s, n)])
    if up is not None:
        total = total + up.astype(FULL) + down.astype(FULL)
    return total


def line_gather(own):
    n = lax.axis_size("tensor")
    me = lax.axis_index("tensor")
    ups, downs = [own], [own]
    for s in range(1, n):
        ups.append(lax.ppermute(ups[-1], "tensor", [(i, i + 1) for i in range(s - 1, n - 1)]))
        downs.append(lax.ppermute(downs[-1], "tensor", [(i, i - 1) for i in range(1, n - s + 1)]))
    whole = jnp.zeros((n,) + own.shape, own.dtype)
    whole = lax.dynamic_update_index_in_dim(whole, own, me, 0)
    for s in range(1, n):
        value = jnp.where(me >= s, ups[s], downs[n - s])
        whole = lax.dynamic_update_index_in_dim(whole, value, lax.rem(me - s + n, n), 0)
    return whole


def tensor_total(term):
    for bit in bits("tensor"):
        low = term.astype(LOW)
        term = low.astype(FULL) + swap(low, "tensor", bit).astype(FULL)
    return term


def spread(target, columns, place, rows, tile):
    target[pl.ds(place, rows, stride=tile), :] = columns


def splat(target, table, first, rows):
    for n in range(N):
        target[pl.ds(n, rows, stride=N), :] = jnp.broadcast_to(
            table[:, first + n : first + n + 1], (rows, LANES)
        )


def columns_of(j):
    return slice(j * LANES, (j + 1) * LANES)


def edge_kernel(
    rows, groups, tile, unroll, flag, size_ref, value_ref, grad_ref, gate_ref, coef_ref, rate_ref,
    edge_ref, size_s, term_s, coef_s,
):
    backward = flag[0] == 1

    @pl.when(pl.program_id(1) == 0)
    def _():
        edge_ref[...] = jnp.zeros_like(edge_ref)

    for j in range(tile):
        if j < groups:
            spread(size_s, size_ref[:, columns_of(j)], j, rows, tile)
        else:
            spread(size_s, jnp.zeros((rows, LANES), FULL), j, rows, tile)
            spread(term_s, jnp.zeros((rows, LANES), FULL), j, rows, tile)

    def loop(body):
        first = tuple(edge_ref[n] for n in range(N))
        last = lax.fori_loop(0, rows, body, first, unroll=unroll)
        for n in range(N):
            edge_ref[n] = last[n]

    @pl.when(jnp.logical_not(backward))
    def _():
        for j in range(groups):
            cut = columns_of(j)
            spread(term_s, size_ref[:, cut] * value_ref[:, cut].astype(FULL), j, rows, tile)
        splat(coef_s, coef_ref, 0, rows)

        def body(t, state):
            place = pl.ds(pl.multiple_of(t * tile, tile), tile)
            size, term = size_s[place, :], term_s[place, :]
            return tuple(
                jnp.exp2(size * rate_ref[n]) * state[n] + term * coef_s[pl.ds(t * N + n, 1), :]
                for n in range(N)
            )

        loop(body)

    @pl.when(backward)
    def _():
        for j in range(groups):
            cut = columns_of(j)
            gate = gate_ref[:, cut].astype(FULL)
            spread(term_s, grad_ref[:, cut] * gate * jax.nn.sigmoid(gate), j, rows, tile)
        splat(coef_s, coef_ref, N, rows)

        def body(step, state):
            t = rows - 1 - step
            place = pl.ds(pl.multiple_of(t * tile, tile), tile)
            size, term = size_s[place, :], term_s[place, :]
            return tuple(
                jnp.exp2(size * rate_ref[n])
                * (state[n] + term * coef_s[pl.ds(t * N + n, 1), :])
                for n in range(N)
            )

        loop(body)


def forward_kernel(
    rows, groups, tile, part, unroll,
    size_ref, value_ref, grad_ref, gate_ref, coef_ref, rate_ref, start_ref, skip_ref, pick_ref,
    gated_ref, gate_grad_ref, before_ref, grad_c_ref, grad_skip_ref,
    size_s, input_s, grad_s, out_s, b_s, c_s, product_s, state_s,
):
    @pl.when(pl.program_id(1) == 0)
    def _():
        state_s[...] = start_ref[...]
        grad_skip_ref[...] = jnp.zeros_like(grad_skip_ref)

    blank = jnp.zeros((rows, LANES), FULL)
    for j in range(tile):
        if j < groups:
            cut = columns_of(j)
            size = size_ref[:, cut]
            value = value_ref[:, cut].astype(FULL)
            gate = gate_ref[:, cut].astype(FULL)
            scan_grad = grad_ref[:, cut] * gate * jax.nn.sigmoid(gate)
            spread(size_s, size, j, rows, tile)
            spread(input_s, size * value, j, rows, tile)
            spread(grad_s, scan_grad, j, rows, tile)
            grad_skip_ref[:, cut] += jnp.sum(scan_grad * value, axis=0, keepdims=True)
        else:
            for target in (size_s, input_s, grad_s):
                spread(target, blank, j, rows, tile)
    splat(b_s, coef_ref, 0, rows)
    splat(c_s, coef_ref, N, rows)
    for low in range(0, N, part):
        rate = [rate_ref[n] for n in range(low, low + part)]

        def body(t, state):
            state = list(state)
            place = pl.ds(pl.multiple_of(t * tile, tile), tile)
            size, term, grad = size_s[place, :], input_s[place, :], grad_s[place, :]
            out = None
            for k in range(part):
                n = low + k
                before_ref[t, n] = state[k]
                state[k] = (
                    jnp.exp2(size * rate[k]) * state[k] + term * b_s[pl.ds(t * N + n, 1), :]
                )
                read = c_s[pl.ds(t * N + n, 1), :] * state[k]
                out = read if out is None else out + read
                product_s[place, columns_of(n)] = state[k] * grad
            if low == 0:
                out_s[place, :] = out
            else:
                out_s[place, :] = out_s[place, :] + out
            return tuple(state)

        first = tuple(state_s[n] for n in range(low, low + part))
        last = lax.fori_loop(0, rows, body, first, unroll=unroll)
        for k in range(part):
            state_s[low + k] = last[k]
    for j in range(groups):
        cut = columns_of(j)
        scan_out = out_s[pl.ds(j, rows, stride=tile), :] + skip_ref[:, cut] * value_ref[
            :, cut
        ].astype(FULL)
        gate = gate_ref[:, cut].astype(FULL)
        sigma = jax.nn.sigmoid(gate)
        gated_ref[:, cut] = (scan_out * (gate * sigma)).astype(LOW)
        slope = sigma * (1.0 + gate * (1.0 - sigma))
        gate_grad_ref[:, cut] = (grad_ref[:, cut] * scan_out * slope).astype(LOW)
    sums = jnp.dot(product_s[...].astype(LOW), pick_ref[...], preferred_element_type=FULL)
    grad_c_ref[...] = jnp.sum(sums.reshape(rows, tile, LANES), axis=1)


def backward_kernel(
    rows, groups, tile, part, unroll,
    size_ref, value_ref, grad_ref, gate_ref, coef_ref, rate_ref, tail_ref, skip_ref, pick_ref,
    before_ref,
    pre_low_ref, grad_value_ref, grad_b_ref, grad_rate_ref, grad_bias_ref,
    size_s, input_s, grad_s, along_s, rated_s, b_s, c_s, product_s, state_s,
):
    @pl.when(pl.program_id(1) == 0)
    def _():
        state_s[...] = tail_ref[...]
        grad_rate_ref[...] = jnp.zeros_like(grad_rate_ref)
        grad_bias_ref[...] = jnp.zeros_like(grad_bias_ref)

    blank = jnp.zeros((rows, LANES), FULL)
    for j in range(tile):
        if j < groups:
            cut = columns_of(j)
            size = size_ref[:, cut]
            gate = gate_ref[:, cut].astype(FULL)
            spread(size_s, size, j, rows, tile)
            spread(input_s, size * value_ref[:, cut].astype(FULL), j, rows, tile)
            spread(grad_s, grad_ref[:, cut] * gate * jax.nn.sigmoid(gate), j, rows, tile)
        else:
            for target in (size_s, input_s, grad_s):
                spread(target, blank, j, rows, tile)
    splat(b_s, coef_ref, 0, rows)
    splat(c_s, coef_ref, N, rows)
    for low in range(0, N, part):
        rate = [rate_ref[n] for n in range(low, low + part)]

        def body(step, carry):
            state, total = list(carry[0]), list(carry[1])
            t = rows - 1 - step
            place = pl.ds(pl.multiple_of(t * tile, tile), tile)
            size, term, grad = size_s[place, :], input_s[place, :], grad_s[place, :]
            along = rated = None
            for k in range(part):
                n = low + k
                adjoint = c_s[pl.ds(t * N + n, 1), :] * grad + state[k]
                state[k] = jnp.exp2(size * rate[k]) * adjoint
                through = state[k] * before_ref[t, n]
                first = adjoint * b_s[pl.ds(t * N + n, 1), :]
                second = through * rate[k]
                along = first if along is None else along + first
                rated = second if rated is None else rated + second
                total[k] = total[k] + through * size
                product_s[place, columns_of(n)] = adjoint * term
            if low == 0:
                along_s[place, :] = along
                rated_s[place, :] = rated
            else:
                along_s[place, :] = along_s[place, :] + along
                rated_s[place, :] = rated_s[place, :] + rated
            return tuple(state), tuple(total)

        place = range(low, low + part)
        first = (tuple(state_s[n] for n in place), tuple(grad_rate_ref[n] for n in place))
        state, total = lax.fori_loop(0, rows, body, first, unroll=unroll)
        for k in range(part):
            state_s[low + k] = state[k]
            grad_rate_ref[low + k] = total[k]
    for j in range(groups):
        cut = columns_of(j)
        size = size_ref[:, cut]
        along = along_s[pl.ds(j, rows, stride=tile), :]
        rated = rated_s[pl.ds(j, rows, stride=tile), :]
        grad_size = along * value_ref[:, cut].astype(FULL) + LOG_2 * rated
        grad_pre = grad_size * (jnp.tanh(0.5 * size) * (1.0 + jnp.exp(-size)))
        pre_low_ref[:, cut] = grad_pre.astype(LOW)
        grad_bias_ref[:, cut] += jnp.sum(grad_pre, axis=0, keepdims=True)
        scan_grad = grad_s[pl.ds(j, rows, stride=tile), :]
        grad_value_ref[:, cut] = along * size + skip_ref[:, cut] * scan_grad
    sums = jnp.dot(product_s[...].astype(LOW), pick_ref[...], preferred_element_type=FULL)
    grad_b_ref[...] = jnp.sum(sums.reshape(rows, tile, LANES), axis=1)


def picker():
    shape = (N * LANES, LANES)
    state = lax.broadcasted_iota(jnp.int32, shape, 0) // LANES
    return (state == lax.broadcasted_iota(jnp.int32, shape, 1)).astype(LOW)


def tiles(channels):
    groups = channels // LANES
    return groups, 8 * pl.cdiv(groups, 8)


def tiled(table):
    groups, tile = tiles(table.shape[-1])
    table = table.reshape(table.shape[:-1] + (groups, LANES))
    pads = [(0, 0)] * (table.ndim - 2) + [(0, tile - groups), (0, 0)]
    return jnp.pad(table, pads)


def flat(table, channels):
    groups, _ = tiles(channels)
    return table[..., :groups, :].reshape(table.shape[:-2] + (channels,))


def cost(micro, length, ops, size):
    work = micro * length * N * 1024 * ops * 100
    return pl.CostEstimate(flops=work, bytes_accessed=size, transcendentals=0)


def limits():
    return pltpu.CompilerParams(vmem_limit_bytes=56 * 1024 * 1024)


def scan_edge(flag, size, value, grad, gate, coef, rate):
    micro, length, channels = size.shape
    groups, tile = tiles(channels)
    rows = min(64, length)
    count = length // rows

    def place(m, i, f):
        return (m, jnp.where(f[0] == 0, i, count - 1 - i), 0)

    wide = pl.BlockSpec((None, rows, channels), place)
    return pl.pallas_call(
        functools.partial(edge_kernel, rows, groups, tile, 4),
        grid_spec=pltpu.PrefetchScalarGridSpec(
            num_scalar_prefetch=1,
            grid=(micro, count),
            in_specs=[wide] * 4
            + [
                pl.BlockSpec((None, rows, 2 * N), place),
                pl.BlockSpec((N, tile, LANES), lambda m, i, f: (0, 0, 0)),
            ],
            out_specs=pl.BlockSpec((None, N, tile, LANES), lambda m, i, f: (m, 0, 0, 0)),
            scratch_shapes=[pltpu.VMEM((rows * tile, LANES), FULL)] * 2
            + [pltpu.VMEM((rows * N, LANES), FULL)],
        ),
        out_shape=jax.ShapeDtypeStruct((micro, N, tile, LANES), FULL),
        compiler_params=limits(),
        cost_estimate=cost(micro, length, 8, size.size * 12),
        name="scan_edge",
    )(flag, size, value, grad, gate, coef, rate)


def scan_forward(size, value, grad, gate, coef, rate, start, skip):
    micro, length, channels = size.shape
    groups, tile = tiles(channels)
    rows = min(64, length)
    wide = pl.BlockSpec((None, rows, channels), lambda m, i: (m, i, 0))
    row = pl.BlockSpec((1, channels), lambda m, i: (0, 0))
    return pl.pallas_call(
        functools.partial(forward_kernel, rows, groups, tile, 8, 4),
        grid=(micro, length // rows),
        in_specs=[wide] * 4
        + [
            pl.BlockSpec((None, rows, 2 * N), lambda m, i: (m, i, 0)),
            pl.BlockSpec((N, tile, LANES), lambda m, i: (0, 0, 0)),
            pl.BlockSpec((None, N, tile, LANES), lambda m, i: (m, 0, 0, 0)),
            row,
            pl.BlockSpec((N * LANES, LANES), lambda m, i: (0, 0)),
        ],
        out_specs=[
            wide,
            wide,
            pl.BlockSpec((None, rows, N, tile, LANES), lambda m, i: (m, i, 0, 0, 0)),
            pl.BlockSpec((None, rows, LANES), lambda m, i: (m, i, 0)),
            pl.BlockSpec((None, 1, channels), lambda m, i: (m, 0, 0)),
        ],
        out_shape=[
            jax.ShapeDtypeStruct(size.shape, LOW),
            jax.ShapeDtypeStruct(size.shape, LOW),
            jax.ShapeDtypeStruct((micro, length, N, tile, LANES), FULL),
            jax.ShapeDtypeStruct((micro, length, LANES), FULL),
            jax.ShapeDtypeStruct((micro, 1, channels), FULL),
        ],
        scratch_shapes=[pltpu.VMEM((rows * tile, LANES), FULL)] * 4
        + [pltpu.VMEM((rows * N, LANES), FULL)] * 2
        + [pltpu.VMEM((rows * tile, N * LANES), FULL), pltpu.VMEM((N, tile, LANES), FULL)],
        compiler_params=limits(),
        cost_estimate=cost(micro, length, 15, size.size * 80),
        name="scan_forward",
    )(size, value, grad, gate, coef, rate, start, skip, picker())


def scan_backward(size, value, grad, gate, coef, rate, tail, skip, before):
    micro, length, channels = size.shape
    groups, tile = tiles(channels)
    rows = min(64, length)
    last = length // rows - 1
    wide = pl.BlockSpec((None, rows, channels), lambda m, i: (m, last - i, 0))
    row = pl.BlockSpec((1, channels), lambda m, i: (0, 0))
    return pl.pallas_call(
        functools.partial(backward_kernel, rows, groups, tile, 8, 4),
        grid=(micro, length // rows),
        in_specs=[wide] * 4
        + [
            pl.BlockSpec((None, rows, 2 * N), lambda m, i: (m, last - i, 0)),
            pl.BlockSpec((N, tile, LANES), lambda m, i: (0, 0, 0)),
            pl.BlockSpec((None, N, tile, LANES), lambda m, i: (m, 0, 0, 0)),
            row,
            pl.BlockSpec((N * LANES, LANES), lambda m, i: (0, 0)),
            pl.BlockSpec((None, rows, N, tile, LANES), lambda m, i: (m, last - i, 0, 0, 0)),
        ],
        out_specs=[
            wide,
            wide,
            pl.BlockSpec((None, rows, LANES), lambda m, i: (m, last - i, 0)),
            pl.BlockSpec((None, N, tile, LANES), lambda m, i: (m, 0, 0, 0)),
            pl.BlockSpec((None, 1, channels), lambda m, i: (m, 0, 0)),
        ],
        out_shape=[
            jax.ShapeDtypeStruct(size.shape, LOW),
            jax.ShapeDtypeStruct(size.shape, FULL),
            jax.ShapeDtypeStruct((micro, length, LANES), FULL),
            jax.ShapeDtypeStruct((micro, N, tile, LANES), FULL),
            jax.ShapeDtypeStruct((micro, 1, channels), FULL),
        ],
        scratch_shapes=[pltpu.VMEM((rows * tile, LANES), FULL)] * 5
        + [pltpu.VMEM((rows * N, LANES), FULL)] * 2
        + [pltpu.VMEM((rows * tile, N * LANES), FULL), pltpu.VMEM((N, tile, LANES), FULL)],
        compiler_params=limits(),
        cost_estimate=cost(micro, length, 20, size.size * 80),
        name="scan_backward",
    )(size, value, grad, gate, coef, rate, tail, skip, picker(), before)


def edges(size, value, grad, gate, coef, rate):
    count, place = lax.axis_size("ctx"), lax.axis_index("ctx")
    args = (size, value, grad, gate, coef, rate)
    if count == 2:
        edge = scan_edge(place.astype(jnp.int32)[None], *args)
        other = swap(edge, "ctx", 1)
        return jnp.where(place == 1, other, 0.0), jnp.where(place == 0, other, 0.0)
    last = scan_edge(jnp.zeros((1,), jnp.int32), *args)
    head = scan_edge(jnp.ones((1,), jnp.int32), *args)
    through = jnp.exp2(rate[None] * tiled(jnp.sum(size, axis=1))[:, None])
    lasts, heads, throughs = (lax.all_gather(a, "ctx") for a in (last, head, through))
    start = tail = jnp.zeros(last.shape, FULL)
    for i in range(count):
        start = jnp.where(i < place, throughs[i] * start + lasts[i], start)
        j = count - 1 - i
        tail = jnp.where(j > place, throughs[j] * tail + heads[j], tail)
    return start, tail


def silu_slope(value):
    sigma = jax.nn.sigmoid(value)
    return sigma * (1.0 + value * (1.0 - sigma))


def dot(a, b, dims, kind=FULL):
    return lax.dot_general(a, b, (dims, ((), ())), preferred_element_type=FULL).astype(kind)


def per_device(
    tokens,
    out_grad,
    norm_gain,
    in_weight,
    xproj_weight,
    step_weight,
    outproj_weight,
    channel_table,
    gain_second,
    in_rows,
    in_cols,
    xproj_rows,
    xproj_cols,
    step_rows,
    step_cols,
    out_rows,
    out_cols,
    table_second,
):
    micro = tokens.shape[0]
    length = tokens.shape[2]
    inner = in_weight.shape[2]
    n_tensor = lax.axis_size("tensor")
    n_owner = lax.axis_size("dp") * lax.axis_size("ctx")
    owned = in_weight.shape[0]
    order, inverse_order = relative_blocks()
    share = length // n_tensor
    first_row = lax.axis_index("tensor") * share
    own_axes = ("ctx", "dp")

    pad_gain = jnp.pad(norm_gain.astype(LOW), (0, inner - owned))[None]
    n_x, n_s = xproj_weight.shape[0], step_weight.shape[0]
    small = jnp.concatenate([xproj_weight.astype(LOW), step_weight.astype(LOW), pad_gain], axis=0)
    pad_rows = -small.shape[0] % 32
    small = gather(jnp.pad(small, ((0, pad_rows), (0, 0)))).reshape(n_owner, -1, inner)
    conv_low = gather(in_weight[:, 0].astype(LOW))
    gate_low = gather(in_weight[:, 1].astype(LOW))
    out_low = gather(outproj_weight.astype(LOW))
    gain_low = small[:, n_x + n_s, :owned].reshape(D).astype(FULL)
    small = pick(small, inverse_order)
    xproj_low = small[:, :n_x].reshape(n_owner * n_x, inner)
    step_low = small[:, n_x : n_x + n_s].reshape(n_owner * n_s, inner)
    gain_value = pick(gain_low.reshape(n_owner, owned), inverse_order).reshape(D)

    taps = channel_table[:K]
    conv_bias = channel_table[K]
    step_bias = channel_table[K + 1]
    skip = channel_table[K + 2][None]
    a_neg = -jnp.exp(channel_table[K + 3 :])
    rate = tiled(a_neg / LOG_2)

    x_low = tokens[:, 0]
    x = x_low.astype(FULL)
    inverse = lax.rsqrt(jnp.mean(x * x, axis=2, keepdims=True) + norm_epsilon)
    flat_rows = micro * length
    x_rel = pick_columns(x_low.reshape(flat_rows, D), order).astype(FULL)
    normed = (x_rel * inverse.reshape(flat_rows, 1) * gain_low).astype(LOW)
    out_grad_low = out_grad[:, 0]
    grad_rel = pick_columns(out_grad_low.reshape(flat_rows, D), order)
    shape = (micro, length, inner)
    conv_in = dot(normed, conv_low, ((1,), (0,)), LOW).reshape(shape)
    earlier = shifted(conv_in[:, length - (K - 1) :], "ctx", 1)
    padded = jnp.concatenate([earlier, conv_in], axis=1).astype(FULL)
    conv = conv_bias + taps[0] * padded[:, 0:length]
    for k in range(1, K):
        conv = conv + taps[k] * padded[:, k : k + length]
    values = jax.nn.silu(conv).astype(LOW)
    values_flat = values.reshape(flat_rows, inner)
    proj = tensor_total(dot(values_flat, xproj_low, ((1,), (1,))))
    rank_low = proj[:, :R].astype(LOW)
    coef = proj[:, R:].reshape(micro, length, 2 * N)
    pre = dot(rank_low, step_low, ((1,), (0,))) + step_bias
    size = jax.nn.softplus(pre).reshape(shape)
    gate_in = dot(normed, gate_low, ((1,), (0,)), LOW).reshape(shape)
    grad_gated = dot(grad_rel, out_low, ((1,), (0,))).reshape(shape)
    start, tail = edges(size, values, grad_gated, gate_in, coef, rate)
    gated, gate_grad, before, grad_c, grad_skip = scan_forward(
        size, values, grad_gated, gate_in, coef, rate, start, skip
    )
    gated_flat = gated.reshape(flat_rows, inner)
    gate_grad_flat = gate_grad.reshape(flat_rows, inner)

    part_out = dot(grad_rel, gated_flat, ((0,), (0,)), LOW)
    part_gate = dot(normed, gate_grad_flat, ((0,), (0,)), LOW)
    mixed_list, token_list = [], []
    for m in range(micro):
        branch = dot(gated[m], out_low, ((1,), (1,)), LOW)
        own = line_scatter(branch.reshape(n_tensor, share, D))
        x_rows = lax.dynamic_slice_in_dim(x[m], first_row, share, 0)
        own = (x_rows + pick_columns(own, inverse_order)).astype(LOW)
        mixed_list.append(line_gather(own).reshape(length, D))
    shard_out = scatter(part_out.reshape(n_owner, owned, inner))
    shard_gate = scatter(part_gate.reshape(n_owner, owned, inner))

    conv_grads, rank_rows, proj_grads, gain_parts, tables = [], [], [], [], []
    pre_lows = []
    for m in range(micro):
        one = slice(m, m + 1)
        pre_low, grad_value, grad_b, grad_rate, grad_bias = scan_backward(
            size[one], values[one], grad_gated[one], gate_in[one], coef[one], rate, tail[one],
            skip, before[one],
        )
        pre_lows.append(pre_low[0])
        grad_rank = dot(pre_low[0], step_low, ((1,), (1,)))
        proj_grad = tensor_total(
            jnp.concatenate([grad_rank, grad_b[0, :, :N], grad_c[m, :, :N]], axis=1)
        ).astype(LOW)
        proj_grads.append(proj_grad)
        grad_values = grad_value[0] + dot(proj_grad, xproj_low, ((1,), (0,)))
        grad_conv = grad_values * silu_slope(conv[m])
        grad_taps = [
            jnp.sum(grad_conv * padded[m, k : k + length], axis=0) for k in range(K)
        ]
        head_rows = []
        for p in range(K - 1):
            total = taps[0] * grad_conv[p]
            for k in range(1, p + 1):
                total = total + taps[k] * grad_conv[p - k]
            head_rows.append(total)
        returned = shifted(jnp.stack(head_rows), "ctx", -1)
        extended = jnp.concatenate([grad_conv, jnp.zeros((K - 1, inner), FULL)], axis=0)
        grad_conv_in = taps[K - 1] * extended[0:length]
        for k in range(K - 1):
            grad_conv_in = grad_conv_in + taps[k] * extended[K - 1 - k : K - 1 - k + length]
        grad_conv_in = jnp.concatenate(
            [grad_conv_in[: length - (K - 1)], grad_conv_in[length - (K - 1) :] + returned], axis=0
        ).astype(LOW)
        conv_grads.append(grad_conv_in)
        grad_normed = (
            dot(gate_grad[m], gate_low, ((1,), (1,))) + dot(grad_conv_in, conv_low, ((1,), (1,)))
        ).astype(LOW)
        own = pick_columns(line_scatter(grad_normed.reshape(n_tensor, share, D)), inverse_order)
        x_rows = lax.dynamic_slice_in_dim(x[m], first_row, share, 0)
        inverse_rows = lax.dynamic_slice_in_dim(inverse[m], first_row, share, 0)
        grad_rows = lax.dynamic_slice_in_dim(out_grad_low[m], first_row, share, 0).astype(FULL)
        gain_parts.append(jnp.sum(own * x_rows * inverse_rows, axis=0))
        scaled = gain_value * own
        grad_x = inverse_rows * scaled - x_rows * inverse_rows * inverse_rows * inverse_rows * (
            jnp.mean(x_rows * scaled, axis=1, keepdims=True)
        )
        token_list.append(line_gather((grad_rows + grad_x).astype(LOW)).reshape(length, D))
        tables.append(
            jnp.concatenate(
                [
                    jnp.stack(grad_taps + [jnp.sum(grad_conv, axis=0)]),
                    grad_bias[0],
                    grad_skip[m],
                    flat(grad_rate[0], inner) * a_neg,
                ],
                axis=0,
            )
        )
    part_conv = dot(normed, jnp.concatenate(conv_grads, axis=0), ((0,), (0,)), LOW)
    shard_conv = scatter(part_conv.reshape(n_owner, owned, inner))
    part_step = dot(rank_low, jnp.concatenate(pre_lows, axis=0), ((0,), (0,)))
    part_xproj = dot(jnp.concatenate(proj_grads, axis=0), values_flat, ((0,), (0,)))
    part_gain = sum(gain_parts[1:], gain_parts[0]).reshape(n_owner, 1, owned)
    part_small = jnp.concatenate(
        [
            part_xproj.reshape(n_owner, n_x, inner),
            part_step.reshape(n_owner, n_s, inner),
            jnp.pad(part_gain, ((0, 0), (0, 0), (0, inner - owned))),
            jnp.zeros((n_owner, pad_rows, inner), FULL),
        ],
        axis=1,
    ).astype(LOW)
    shard_small = scatter(pick(part_small, order))
    shard_xproj = shard_small[:n_x]
    shard_step = shard_small[n_x : n_x + n_s]
    gain_partial = shard_small[n_x + n_s, :owned]
    grad_table = sum(tables[1:], tables[0])

    shard_in = jnp.stack([shard_conv, shard_gate], axis=1)
    matrices = (shard_in, shard_xproj, shard_step, shard_out)
    weights = (in_weight, xproj_weight, step_weight, outproj_weight)
    all_weights = [norm_gain] + list(weights) + [channel_table]
    shares = jnp.array([1.0 / n_tensor, 1.0, 1.0, 1.0, 1.0, 1.0 / n_owner], FULL)
    weight_sq = jnp.stack([jnp.sum(w * w) for w in all_weights]) * shares
    old_rows = (in_rows, xproj_rows, step_rows, out_rows)
    old_cols = (in_cols, xproj_cols, step_cols, out_cols)
    width_cols = (2 * E, E, E, E)
    width_rows = (D, R + 2 * N, R, D)
    squares = [matrix * matrix + square_floor for matrix in matrices]
    row_parts = [jnp.sum(square.reshape(square.shape[0], -1), axis=1) for square in squares]
    col_parts = [jnp.sum(square, axis=0).reshape(-1, inner) for square in squares]
    row_sums = butterfly(jnp.concatenate(row_parts + [gain_partial, weight_sq]), ("tensor",))
    ends = [0]
    for part in row_parts + [gain_partial, weight_sq]:
        ends.append(ends[-1] + part.shape[0])
    row_sums = [row_sums[ends[i] : ends[i + 1]] for i in range(6)]
    row_news = [
        decay_rate * old_rows[i] + (1.0 - decay_rate) * row_sums[i] / width_cols[i]
        for i in range(4)
    ]
    shard_gain = row_sums[4]
    totals = jnp.stack([jnp.sum(row_new) for row_new in row_news])
    scalars = butterfly(jnp.concatenate([totals, row_sums[5]]), own_axes)
    row_totals, total_weight = scalars[:4], scalars[4:]
    summed = butterfly(jnp.concatenate(col_parts + [grad_table], axis=0), own_axes)
    col_sums = [summed[0:2], summed[2], summed[3], summed[4]]
    table_grad = summed[5:]
    col_news = [
        decay_rate * old_cols[i] + (1.0 - decay_rate) * col_sums[i] / width_rows[i]
        for i in range(4)
    ]
    updates = []
    for i in range(4):
        row_mean = row_totals[i] / width_rows[i]
        shape = (-1,) + (1,) * (matrices[i].ndim - 1)
        second = row_news[i].reshape(shape) * col_news[i][None] / row_mean
        updates.append(matrices[i] * lax.rsqrt(second))
    new_gain_second = decay_rate * gain_second + (1.0 - decay_rate) * (
        shard_gain * shard_gain + square_floor
    )
    gain_update = shard_gain * lax.rsqrt(new_gain_second)
    new_table_second = decay_rate * table_second + (1.0 - decay_rate) * (
        table_grad * table_grad + square_floor
    )
    table_update = table_grad * lax.rsqrt(new_table_second)
    all_updates = [gain_update] + updates + [table_update]
    update_sq = jnp.stack([jnp.sum(u * u) for u in all_updates]) * shares
    total_update = butterfly(update_sq, own_axes + ("tensor",))
    counts = jnp.array([D, 2 * D * E, (R + 2 * N) * E, R * E, D * E, (K + 3 + N) * E], FULL)
    update_rms = jnp.sqrt(total_update / counts)
    factor = jnp.maximum(1.0, update_rms / clip_limit)
    scale = jnp.sqrt(total_weight / counts)
    stride = step_rate * scale / factor
    new_weights = [all_weights[i] - stride[i] * all_updates[i] for i in range(6)]
    mixed = jnp.stack(mixed_list)[:, None]
    token_grad = jnp.stack(token_list)[:, None]
    return (
        mixed,
        token_grad,
        shard_gain,
        shard_in,
        shard_xproj,
        shard_step,
        shard_out,
        table_grad,
        new_weights[0],
        new_weights[1],
        new_weights[2],
        new_weights[3],
        new_weights[4],
        new_weights[5],
        new_gain_second,
        row_news[0],
        col_news[0],
        row_news[1],
        col_news[1],
        row_news[2],
        col_news[2],
        row_news[3],
        col_news[3],
        new_table_second,
        update_rms,
    )


def solution(mesh):
    rows = P(("dp", "ctx"))
    matrix = P(("dp", "ctx"), "tensor")
    cube = P(("dp", "ctx"), None, "tensor")
    table = P(None, "tensor")
    block = P(None, "dp", "ctx", None)
    cols = P("tensor")
    return jax.shard_map(
        per_device,
        mesh=mesh,
        in_specs=(block, block, rows, cube, matrix, matrix, matrix, table, rows)
        + (rows, table, rows, cols, rows, cols, rows, cols, table),
        out_specs=(block, block, rows, cube, matrix, matrix, matrix, table)
        + (rows, cube, matrix, matrix, matrix, table, rows)
        + (rows, table, rows, cols, rows, cols, rows, cols, table, P()),
        check_vma=False,
    )
```

time: 3260 us -> 1010 us (0.31)
  the two profiles are of different devices: /device:TPU:0 before, /device:TPU:24 now
where the time goes in v1:
time: 1010 us; the launch traced here: 1000 us
  starting transfers between devices  243 us (24%)
  waiting for transfers between devices  227 us (22%)
  local copies, waits for them, and re-layouts  192 us (19%)
  Pallas kernels  139 us (14%)
  other arithmetic  107 us (11%)
  matrix products  85.3 us (8%)
    ppermute x60, waiting for transfers between devices, swap(): lax.ppermute(block, axis, [(i, i ^ bit) for i in range(lax.axis_size(axis...  115 us
    ppermute x12, starting transfers between devices, line_scatter(): lax.ppermute(send_down, 'tensor', [(i, i - 1) for i in range(n - s, n)])  114 us
    dot_general x20, matrix products, dot(): lax.dot_general(a, b, (dims, ((), ())), preferred_element_type=FULL)  85.3 us
    ppermute x12, waiting for transfers between devices, line_gather(): lax.ppermute(ups[-1], 'tensor', [(i, i + 1) for i in range(s - 1, n - 1)])  80.1 us
    unnamed x352, local copies, waits for them, and re-layouts  74.3 us
    pallas_call x2, Pallas kernels, scan_backward(): pl.pallas_call(functools.partial(backward_kernel, rows, groups, tile, 8,...  66.6 us
    ppermute x60, starting transfers between devices, swap(): lax.ppermute(block, axis, [(i, i ^ bit) for i in range(lax.axis_size(axis...  64.3 us
    pallas_call x1, Pallas kernels, scan_forward(): pl.pallas_call(functools.partial(forward_kernel, rows, groups, tile, 8, 4...  51.2 us
  transfers between devices with their start and end apart: 111, of which 42 were waited for; matrix products, arithmetic and copies ran while one was open for 29% of the time, Pallas kernels for 3%

profile of v1, /device:TPU:24, one launch (start us, length us, event | category | flops | bytes accessed | tf_op | source)
XLA Modules:
  0.0 1000.6 jit_solution(3637159594326077218)
XLA Ops:
  172.3 10.1 %collective-permute-done.11 = bf16[1024,160]{1,0:T(8,128)(2,1)S(1)} collective-permute-done((bf16[1024,160]{1,0:T(8,128)(2,1)S(1)}, bf16[1024,160]{1,0:T(8,128)(2,1)S(1)}, u32[]{:S(2)}, u32[]{:S(2)}) %collective-permute-start.11) | collective-permute-done | bytes 327712 | tf_op jit(solution)/shard_map/ppermute | solution.py:34
  186.1 20.9 %collective-permute-done.12 = bf16[1024,160]{1,0:T(8,128)(2,1)S(1)} collective-permute-done((bf16[1024,160]{1,0:T(8,128)(2,1)S(1)}, bf16[1024,160]{1,0:T(8,128)(2,1)S(1)}, u32[]{:S(2)}, u32[]{:S(2)}) %collective-permute-start.12) | collective-permute-done | bytes 327712 | tf_op jit(solution)/shard_map/ppermute | solution.py:34
  213.8 21.5 %scan_edge.1 = f32[2,16,8,128]{3,2,1,0:T(8,128)} custom-call(s32[1]{0:T(128)} %bitcast.20.flag, f32[2,512,1024]{2,1,0:T(8,128)} %bitcast.651, bf16[2,512,1024]{2,1,0:T(8,128)(2,1)} %copy-done.4, f32[2,512,1024]{2,1,0:T(8,128)} %bitcast.649, bf16[2,512,1024]{2,1,0:T(8,128)(2,1)} %bitcast.658, f32[2,512,32]{2,1,0:T(8,128)} %bitcast.672, f32[16,8,128]{2,1,0:T(8,128)} %bitcast.682), custom_call_target="tpu_custom_call" | custom-call | flops 13421772800 | bytes 12582912 | tf_op jit(solution)/shard_map/scan_edge/pallas_call | solution.py:421
  237.8 51.2 %scan_forward.1 = (bf16[2,512,1024]{2,1,0:T(8,128)(2,1)}, bf16[2,512,1024]{2,1,0:T(8,128)(2,1)}, f32[2,512,16,8,128]{4,3,2,1,0:T(8,128)}, f32[2,512,128]{2,1,0:T(8,128)}, f32[2,1,1024]{2,1,0:T(1,128)}) custom-call(f32[2,512,1024]{2,1,0:T(8,128)} %bitcast.652, bf16[2,512,1024]{2,1,0:T(8,128)(2,1)} %copy-done.4, f32[2,512,1024]{2,1,0:T(8,128)} %bitcast.650, ...), custom_call_target="tpu_custom_call" | custom-call | flops 25165824000 | bytes 83886080 | tf_op jit(solution)/shard_map/scan_forward/pallas_call | solution.py:448
  296.5 42.7 %fusion.200 = (f32[1,512,16,8,128]{4,3,2,1,0:T(8,128)}, f32[1,512,16,8,128]{4,3,2,1,0:T(8,128)}) fusion(f32[2,512,16,8,128]{4,3,2,1,0:T(8,128)} %get-tuple-element.42), kind=kLoop, calls=%fused_computation.571 | loop fusion | bytes 134217728 | tf_op jit(solution)/shard_map/slice | solution.py:653
  339.9 33.3 %scan_backward.2 = (bf16[1,512,1024]{2,1,0:T(8,128)(2,1)}, f32[1,512,1024]{2,1,0:T(8,128)}, f32[1,512,128]{2,1,0:T(8,128)}, f32[1,16,8,128]{3,2,1,0:T(8,128)}, f32[1,1,1024]{2,1,0:T(1,128)}) custom-call(f32[1,512,1024]{2,1,0:T(8,128)} %get-tuple-element.148.size_ref, bf16[1,512,1024]{2,1,0:T(8,128)(2,1)} %get-tuple-element.188.value_ref, ...), custom_call_target="tpu_custom_call" | custom-call | flops 16777216000 | bytes 41943040 | tf_op jit(solution)/shard_map/scan_backward/pallas_call | solution.py:489
  382.3 33.3 %scan_backward.3 = (bf16[1,512,1024]{2,1,0:T(8,128)(2,1)}, f32[1,512,1024]{2,1,0:T(8,128)}, f32[1,512,128]{2,1,0:T(8,128)}, f32[1,16,8,128]{3,2,1,0:T(8,128)}, f32[1,1,1024]{2,1,0:T(1,128)}) custom-call(f32[1,512,1024]{2,1,0:T(8,128)} %get-tuple-element.147.size_ref, bf16[1,512,1024]{2,1,0:T(8,128)(2,1)} %get-tuple-element.187.value_ref, ...), custom_call_target="tpu_custom_call" | custom-call | flops 16777216000 | bytes 41943040 | tf_op jit(solution)/shard_map/scan_backward/pallas_call | solution.py:489
  471.7 8.9 fusion.8
  495.2 12.4 %collective-permute-start.39 = (bf16[128,2048]{1,0:T(8,128)(2,1)S(1)}, bf16[128,2048]{1,0:T(8,128)(2,1)S(1)}, u32[]{:S(2)}, u32[]{:S(2)}) collective-permute-start(bf16[128,2048]{1,0:T(8,128)(2,1)S(1)} %copy-done.56), channel_id=1, source_target_pairs={{3,2},{7,6},{11,10},{15,14},{19,18},{23,22},{27,26},{31,30}} | collective-permute-start | bytes 1572872 | tf_op jit(solution)/shard_map/ppermute | solution.py:130
  536.9 22.1 %collective-permute-start.69 = (bf16[128,2048]{1,0:T(8,128)(2,1)S(1)}, bf16[128,2048]{1,0:T(8,128)(2,1)S(1)}, u32[]{:S(2)}, u32[]{:S(2)}) collective-permute-start(bf16[128,2048]{1,0:T(8,128)(2,1)S(1)} %get-tuple-element.184), channel_id=1, source_target_pairs={{3,2},{7,6},{11,10},{15,14},{19,18},{23,22},{27,26},{31,30}} | collective-permute-start | bytes 1572872 | tf_op jit(solution)/shard_map/ppermute | solution.py:130
  560.2 18.5 %collective-permute-start.28 = (bf16[128,2048]{1,0:T(8,128)(2,1)S(1)}, bf16[128,2048]{1,0:T(8,128)(2,1)S(1)}, u32[]{:S(2)}, u32[]{:S(2)}) collective-permute-start(bf16[128,2048]{1,0:T(8,128)(2,1)S(1)} %get-tuple-element.190), channel_id=1, source_target_pairs={{2,1},{3,2},{6,5},{7,6},{10,9},{11,10},{14,13},{15,14},{18,17},{19... | collective-permute-start | bytes 1572872 | tf_op jit(solution)/shard_map/ppermute | solution.py:130
  580.5 10.5 %collective-permute-start.40 = (bf16[128,2048]{1,0:T(8,128)(2,1)S(1)}, bf16[128,2048]{1,0:T(8,128)(2,1)S(1)}, u32[]{:S(2)}, u32[]{:S(2)}) collective-permute-start(bf16[128,2048]{1,0:T(8,128)(2,1)S(1)} %get-tuple-element.194), channel_id=1, source_target_pairs={{2,1},{3,2},{6,5},{7,6},{10,9},{11,10},{14,13},{15,14},{18,17},{19... | collective-permute-start | bytes 1572872 | tf_op jit(solution)/shard_map/ppermute | solution.py:130
  591.4 9.2 collective-permute-start.55
  603.1 8.8 collective-permute-start.70
  614.4 8.8 collective-permute-start.29
  627.0 9.4 collective-permute-done.29
  636.5 9.0 collective-permute-start.41
  882.5 10.2 %collective-permute-start.43 = (bf16[128,2048]{1,0:T(8,128)(2,1)S(1)}, bf16[128,2048]{1,0:T(8,128)(2,1)S(1)}, u32[]{:S(2)}, u32[]{:S(2)}) collective-permute-start(bf16[128,2048]{1,0:T(8,128)(2,1)S(1)} %copy-done.57), channel_id=1, source_target_pairs={{1,0},{2,1},{3,2},{5,4},{6,5},{7,6},{9,8},{10,9},{11,10},{13,12},{... | collective-permute-start | bytes 1572872 | tf_op jit(solution)/shard_map/ppermute | solution.py:142
  902.0 13.7 %collective-permute-done.42 = bf16[128,2048]{1,0:T(8,128)(2,1)S(1)} collective-permute-done((bf16[128,2048]{1,0:T(8,128)(2,1)S(1)}, bf16[128,2048]{1,0:T(8,128)(2,1)S(1)}, u32[]{:S(2)}, u32[]{:S(2)}) %collective-permute-start.42) | collective-permute-done | bytes 524320 | tf_op jit(solution)/shard_map/ppermute | solution.py:141
  916.5 10.5 %collective-permute-done.61 = bf16[128,2048]{1,0:T(8,128)(2,1)S(1)} collective-permute-done((bf16[128,2048]{1,0:T(8,128)(2,1)}, bf16[128,2048]{1,0:T(8,128)(2,1)S(1)}, u32[]{:S(2)}, u32[]{:S(2)}) %collective-permute-start.61) | collective-permute-done | bytes 524320 | tf_op jit(solution)/shard_map/ppermute | solution.py:141
  929.2 9.1 collective-permute-done.76
  940.5 9.0 collective-permute-done.34
  952.1 8.6 collective-permute-done.46
  972.1 11.1 %collective-permute-done.77 = bf16[128,2048]{1,0:T(8,128)(2,1)S(1)} collective-permute-done((bf16[128,2048]{1,0:T(8,128)(2,1)S(1)}, bf16[128,2048]{1,0:T(8,128)(2,1)S(1)}, u32[]{:S(2)}, u32[]{:S(2)}) %collective-permute-start.77) | collective-permute-done | bytes 524320 | tf_op jit(solution)/shard_map/ppermute | solution.py:141
  (812 shorter events, 590.4 us)
Async XLA Ops:
  5.9 70.5 %collective-permute-start = (bf16[64,1024]{1,0:T(8,128)(2,1)S(1)}, bf16[64,1024]{1,0:T(8,128)(2,1)S(1)}, u32[]{:S(2)}, u32[]{:S(2)}) collective-permute-start(bf16[64,1024]{1,0:T(8,128)(2,1)S(1)} %get-tuple-element.269), channel_id=1, source_target_pairs={{0,8},{8,0},{16,24},{24,16},{1,9},{9,1},{17,25},{25,17},{2,10},{10... | collective-permute-start | bytes 393224 | tf_op jit(solution)/shard_map/ppermute | solution.py:34
  7.4 67.5 %collective-permute-start.1 = (bf16[64,1024]{1,0:T(8,128)(2,1)S(1)}, bf16[64,1024]{1,0:T(8,128)(2,1)S(1)}, u32[]{:S(2)}, u32[]{:S(2)}) collective-permute-start(bf16[64,1024]{1,0:T(8,128)(2,1)S(1)} %get-tuple-element.269), channel_id=1, source_target_pairs={{0,16},{8,24},{16,0},{24,8},{1,17},{9,25},{17,1},{25,9},{2,18},{10... | collective-permute-start | bytes 393224 | tf_op jit(solution)/shard_map/ppermute | solution.py:34
  12.1 84.1 %collective-permute-start.18 = (bf16[256,1024]{1,0:T(8,128)(2,1)}, bf16[256,1024]{1,0:T(8,128)(2,1)}, u32[]{:S(2)}, u32[]{:S(2)}) collective-permute-start(bf16[256,1024]{1,0:T(8,128)(2,1)} %get-tuple-element.211), channel_id=1, source_target_pairs={{0,8},{8,0},{16,24},{24,16},{1,9},{9,1},{17,25},{25,17},{2,10},{10... | collective-permute-start | bytes 1572872 | tf_op jit(solution)/shard_map/ppermute | solution.py:34
  12.6 69.5 %collective-permute-start.19 = (bf16[256,1024]{1,0:T(8,128)(2,1)}, bf16[256,1024]{1,0:T(8,128)(2,1)}, u32[]{:S(2)}, u32[]{:S(2)}) collective-permute-start(bf16[256,1024]{1,0:T(8,128)(2,1)} %get-tuple-element.211), channel_id=1, source_target_pairs={{0,16},{8,24},{16,0},{24,8},{1,17},{9,25},{17,1},{25,9},{2,18},{10... | collective-permute-start | bytes 1572872 | tf_op jit(solution)/shard_map/ppermute | solution.py:34
  17.4 81.4 %collective-permute-start.5 = (bf16[256,1024]{1,0:T(8,128)(2,1)}, bf16[256,1024]{1,0:T(8,128)(2,1)}, u32[]{:S(2)}, u32[]{:S(2)}) collective-permute-start(bf16[256,1024]{1,0:T(8,128)(2,1)} %get-tuple-element.212), channel_id=1, source_target_pairs={{0,8},{8,0},{16,24},{24,16},{1,9},{9,1},{17,25},{25,17},{2,10},{10... | collective-permute-start | bytes 1572872 | tf_op jit(solution)/shard_map/ppermute | solution.py:34
  382.3 75.3 %collective-permute-start.48 = (bf16[512,160]{0,1:T(8,128)(2,1)}, bf16[512,160]{0,1:T(8,128)(2,1)}, u32[]{:S(2)}, u32[]{:S(2)}) collective-permute-start(bf16[512,160]{0,1:T(8,128)(2,1)} %pad_maximum_fusion.6), channel_id=1, source_target_pairs={{0,1},{1,0},{2,3},{3,2},{4,5},{5,4},{6,7},{7,6},{8,9},{9,8},{10,11... | collective-permute-start | bytes 491528 | tf_op jit(solution)/shard_map/ppermute | solution.py:34
  436.5 227.9 %collective-permute-start.93 = (bf16[4,256,1024]{2,1,0:T(8,128)(2,1)}, bf16[4,256,1024]{2,1,0:T(8,128)(2,1)}, u32[]{:S(2)}, u32[]{:S(2)}) collective-permute-start(bf16[4,256,1024]{2,1,0:T(8,128)(2,1)} %bitcast.166), channel_id=1, source_target_pairs={{0,4},{4,0},{1,5},{5,1},{2,6},{6,2},{3,7},{7,3},{8,12},{12,8},{9,1... | collective-permute-start | bytes 6291464 | tf_op jit(solution)/shard_map/ppermute | solution.py:34
  437.8 88.3 %collective-permute-start.24 = (bf16[128,2048]{1,0:T(8,128)(2,1)}, bf16[128,2048]{1,0:T(8,128)(2,1)}, u32[]{:S(2)}, u32[]{:S(2)}) collective-permute-start(bf16[128,2048]{1,0:T(8,128)(2,1)} %get-tuple-element.191), channel_id=1, source_target_pairs={{0,1},{4,5},{8,9},{12,13},{16,17},{20,21},{24,25},{28,29}} | collective-permute-start | bytes 1572872 | tf_op jit(solution)/shard_map/ppermute | solution.py:129
  439.2 93.0 %collective-permute-start.27 = (bf16[128,2048]{1,0:T(8,128)(2,1)}, bf16[128,2048]{1,0:T(8,128)(2,1)}, u32[]{:S(2)}, u32[]{:S(2)}) collective-permute-start(bf16[128,2048]{1,0:T(8,128)(2,1)} %get-tuple-element.192), channel_id=1, source_target_pairs={{3,2},{7,6},{11,10},{15,14},{19,18},{23,22},{27,26},{31,30}} | collective-permute-start | bytes 1572872 | tf_op jit(solution)/shard_map/ppermute | solution.py:130
  455.8 72.8 %collective-permute-start.36 = (bf16[128,2048]{1,0:T(8,128)(2,1)}, bf16[128,2048]{1,0:T(8,128)(2,1)}, u32[]{:S(2)}, u32[]{:S(2)}) collective-permute-start(bf16[128,2048]{1,0:T(8,128)(2,1)} %get-tuple-element.195), channel_id=1, source_target_pairs={{0,1},{4,5},{8,9},{12,13},{16,17},{20,21},{24,25},{28,29}} | collective-permute-start | bytes 1572872 | tf_op jit(solution)/shard_map/ppermute | solution.py:129
  495.2 41.7 %collective-permute-start.39 = (bf16[128,2048]{1,0:T(8,128)(2,1)S(1)}, bf16[128,2048]{1,0:T(8,128)(2,1)S(1)}, u32[]{:S(2)}, u32[]{:S(2)}) collective-permute-start(bf16[128,2048]{1,0:T(8,128)(2,1)S(1)} %copy-done.56), channel_id=1, source_target_pairs={{3,2},{7,6},{11,10},{15,14},{19,18},{23,22},{27,26},{31,30}} | collective-permute-start | bytes 1572872 | tf_op jit(solution)/shard_map/ppermute | solution.py:130
  536.9 42.3 %collective-permute-start.69 = (bf16[128,2048]{1,0:T(8,128)(2,1)S(1)}, bf16[128,2048]{1,0:T(8,128)(2,1)S(1)}, u32[]{:S(2)}, u32[]{:S(2)}) collective-permute-start(bf16[128,2048]{1,0:T(8,128)(2,1)S(1)} %get-tuple-element.184), channel_id=1, source_target_pairs={{3,2},{7,6},{11,10},{15,14},{19,18},{23,22},{27,26},{31,30}} | collective-permute-start | bytes 1572872 | tf_op jit(solution)/shard_map/ppermute | solution.py:130
  560.1 112.1 %collective-permute-start.83 = (bf16[4,256,1024]{2,1,0:T(8,128)(2,1)S(1)}, bf16[4,256,1024]{2,1,0:T(8,128)(2,1)S(1)}, u32[]{:S(2)}, u32[]{:S(2)}) collective-permute-start(bf16[4,256,1024]{2,1,0:T(8,128)(2,1)S(1)} %bitcast.660), channel_id=1, source_target_pairs={{0,4},{4,0},{1,5},{5,1},{2,6},{6,2},{3,7},{7,3},{8,12},{12,8},{9,1... | collective-permute-start | bytes 6291464 | tf_op jit(solution)/shard_map/ppermute | solution.py:34
  579.1 46.6 %collective-permute-start.26 = (bf16[128,2048]{1,0:T(8,128)(2,1)S(1)}, bf16[128,2048]{1,0:T(8,128)(2,1)S(1)}, u32[]{:S(2)}, u32[]{:S(2)}) collective-permute-start(bf16[128,2048]{1,0:T(8,128)(2,1)S(1)} %get-tuple-element.189), channel_id=1, source_target_pairs={{0,1},{1,2},{2,3},{4,5},{5,6},{6,7},{8,9},{9,10},{10,11},{12,13},{... | collective-permute-start | bytes 1572872 | tf_op jit(solution)/shard_map/ppermute | solution.py:129
  625.6 89.8 %collective-permute-start.78 = (bf16[4,256,1024]{2,1,0:T(8,128)(2,1)}, bf16[4,256,1024]{2,1,0:T(8,128)(2,1)}, u32[]{:S(2)}, u32[]{:S(2)}) collective-permute-start(bf16[4,256,1024]{2,1,0:T(8,128)(2,1)} %bitcast.143), channel_id=1, source_target_pairs={{0,4},{4,0},{1,5},{5,1},{2,6},{6,2},{3,7},{7,3},{8,12},{12,8},{9,1... | collective-permute-start | bytes 6291464 | tf_op jit(solution)/shard_map/ppermute | solution.py:34
  682.7 42.1 %collective-permute-start.96 = (bf16[2,256,512]{2,1,0:T(8,128)(2,1)}, bf16[2,256,512]{2,1,0:T(8,128)(2,1)}, u32[]{:S(2)}, u32[]{:S(2)}) collective-permute-start(bf16[2,256,512]{2,1,0:T(8,128)(2,1)} %slice.876), channel_id=1, source_target_pairs={{0,16},{8,24},{16,0},{24,8},{1,17},{9,25},{17,1},{25,9},{2,18},{10... | collective-permute-start | bytes 1572872 | tf_op jit(solution)/shard_map/ppermute | solution.py:34
  685.1 42.6 %collective-permute-start.84 = (bf16[2,256,512]{2,1,0:T(8,128)(2,1)}, bf16[2,256,512]{2,1,0:T(8,128)(2,1)}, u32[]{:S(2)}, u32[]{:S(2)}) collective-permute-start(bf16[2,256,512]{2,1,0:T(8,128)(2,1)} %pad_maximum_fusion.3), channel_id=1, source_target_pairs={{0,8},{8,0},{16,24},{24,16},{1,9},{9,1},{17,25},{25,17},{2,10},{10... | collective-permute-start | bytes 1572872 | tf_op jit(solution)/shard_map/ppermute | solution.py:34
  718.1 123.5 %collective-permute-start.58 = (bf16[128,2048]{1,0:T(8,128)(2,1)}, bf16[128,2048]{1,0:T(8,128)(2,1)}, u32[]{:S(2)}, u32[]{:S(2)}) collective-permute-start(bf16[128,2048]{1,0:T(8,128)(2,1)} %get-tuple-element.139), channel_id=1, source_target_pairs={{1,0},{2,1},{3,2},{5,4},{6,5},{7,6},{9,8},{10,9},{11,10},{13,12},{... | collective-permute-start | bytes 1572872 | tf_op jit(solution)/shard_map/ppermute | solution.py:142
  754.9 115.5 %collective-permute-start.57 = (bf16[128,2048]{1,0:T(8,128)(2,1)}, bf16[128,2048]{1,0:T(8,128)(2,1)}, u32[]{:S(2)}, u32[]{:S(2)}) collective-permute-start(bf16[128,2048]{1,0:T(8,128)(2,1)} %get-tuple-element.139), channel_id=1, source_target_pairs={{0,1},{1,2},{2,3},{4,5},{5,6},{6,7},{8,9},{9,10},{10,11},{12,13},{... | collective-permute-start | bytes 1572872 | tf_op jit(solution)/shard_map/ppermute | solution.py:141
  761.8 90.1 %collective-permute-start.73 = (bf16[128,2048]{1,0:T(8,128)(2,1)}, bf16[128,2048]{1,0:T(8,128)(2,1)}, u32[]{:S(2)}, u32[]{:S(2)}) collective-permute-start(bf16[128,2048]{1,0:T(8,128)(2,1)} %get-tuple-element.143), channel_id=1, source_target_pairs={{1,0},{2,1},{3,2},{5,4},{6,5},{7,6},{9,8},{10,9},{11,10},{13,12},{... | collective-permute-start | bytes 1572872 | tf_op jit(solution)/shard_map/ppermute | solution.py:142
  809.4 73.1 %collective-permute-start.72 = (bf16[128,2048]{1,0:T(8,128)(2,1)}, bf16[128,2048]{1,0:T(8,128)(2,1)}, u32[]{:S(2)}, u32[]{:S(2)}) collective-permute-start(bf16[128,2048]{1,0:T(8,128)(2,1)} %get-tuple-element.143), channel_id=1, source_target_pairs={{0,1},{1,2},{2,3},{4,5},{5,6},{6,7},{8,9},{9,10},{10,11},{12,13},{... | collective-permute-start | bytes 1572872 | tf_op jit(solution)/shard_map/ppermute | solution.py:141
  837.1 55.7 %collective-permute-start.31 = (bf16[128,2048]{1,0:T(8,128)(2,1)}, bf16[128,2048]{1,0:T(8,128)(2,1)S(1)}, u32[]{:S(2)}, u32[]{:S(2)}) collective-permute-start(bf16[128,2048]{1,0:T(8,128)(2,1)} %get-tuple-element.140), channel_id=1, source_target_pairs={{1,0},{2,1},{3,2},{5,4},{6,5},{7,6},{9,8},{10,9},{11,10},{13,12},{... | collective-permute-start | bytes 1572872 | tf_op jit(solution)/shard_map/ppermute | solution.py:142
  900.8 48.7 %collective-permute-start.34 = (bf16[128,2048]{1,0:T(8,128)(2,1)S(1)}, bf16[128,2048]{1,0:T(8,128)(2,1)S(1)}, u32[]{:S(2)}, u32[]{:S(2)}) collective-permute-start(bf16[128,2048]{1,0:T(8,128)(2,1)S(1)} %collective-permute-done.30), channel_id=1, source_target_pairs={{1,2},{2,3},{5,6},{6,7},{9,10},{10,11},{13,14},{14,15},{17,18},{18... | collective-permute-start | bytes 1572872 | tf_op jit(solution)/shard_map/ppermute | solution.py:141
  950.8 41.2 %collective-permute-start.35 = (bf16[128,2048]{1,0:T(8,128)(2,1)S(1)}, bf16[128,2048]{1,0:T(8,128)(2,1)S(1)}, u32[]{:S(2)}, u32[]{:S(2)}) collective-permute-start(bf16[128,2048]{1,0:T(8,128)(2,1)S(1)} %collective-permute-done.34), channel_id=1, source_target_pairs={{2,3},{6,7},{10,11},{14,15},{18,19},{22,23},{26,27},{30,31}} | collective-permute-start | bytes 1572872 | tf_op jit(solution)/shard_map/ppermute | solution.py:141
  (215 other events, 3989.5 us)

commit v2 on v1

v2 whole, which is shorter than its diff:
```python
import functools
import math

import jax
import jax.numpy as jnp
from jax import lax
from jax.experimental import pallas as pl
from jax.experimental.pallas import tpu as pltpu
from jax.sharding import PartitionSpec as P

D = 2048
E = 4096
N = 16
R = 128
K = 4
LANES = 128
LOG_2 = math.log(2.0)
LOW = jnp.bfloat16
FULL = jnp.float32

norm_epsilon = 1e-05
square_floor = 1e-30
decay_rate = 0.5
clip_limit = 0.5
step_rate = 1.0


def after(value, *others):
    return lax.optimization_barrier((value,) + others)[0]


def bits(axis):
    size = lax.axis_size(axis)
    return [1 << b for b in range(size.bit_length() - 1)]


def swap(block, axis, bit):
    return lax.ppermute(block, axis, [(i, i ^ bit) for i in range(lax.axis_size(axis))])


def shifted(block, axis, distance):
    devices = range(lax.axis_size(axis))
    route = [(i - distance, i) for i in devices if i - distance in devices]
    return lax.ppermute(block, axis, route)


def butterfly(value, axes):
    for axis in axes:
        for bit in bits(axis):
            value = value + swap(value, axis, bit)
    return value


def relative_blocks():
    n_dp, n_ctx = lax.axis_size("dp"), lax.axis_size("ctx")
    dp, ctx = lax.axis_index("dp"), lax.axis_index("ctx")
    return [
        (dp ^ (q % n_dp)) * n_ctx + (ctx ^ (q // n_dp)) for q in range(n_dp * n_ctx)
    ], [
        (ctx ^ (j % n_ctx)) * n_dp + (dp ^ (j // n_ctx)) for j in range(n_dp * n_ctx)
    ]


def pick(blocks, order):
    return jnp.stack([lax.dynamic_index_in_dim(blocks, q, 0, False) for q in order])


def fetch(own):
    if lax.axis_size("dp") != 4:
        blocks = [own]
        for bit in bits("dp"):
            blocks = blocks + [swap(block, "dp", bit) for block in blocks]
        return blocks, blocks[1:]
    half = own.shape[0] // 2
    one, two = swap(own, "dp", 1), swap(own, "dp", 2)
    three = jnp.concatenate([swap(two[:half], "dp", 1), swap(one[half:], "dp", 2)], axis=0)
    return [own, one, two, three], [one, two]


def fetch_two(left, right, release_far, release_all):
    if lax.axis_size("dp") != 4:
        return fetch(left)[0], fetch(right)[0]
    left_one, left_two = swap(left, "dp", 1), swap(left, "dp", 2)
    right_one, right_two = swap(right, "dp", 1), swap(right, "dp", 2)
    left_far = swap(after(left_two, release_far), "dp", 1)
    right_far = swap(after(right_one, release_far), "dp", 2)
    left_far, right_far = after(left_far, *release_all), after(right_far, *release_all)
    return [left, left_one, left_two, left_far], [right, right_one, right_two, right_far]


def join(blocks):
    chunks = [jnp.concatenate(blocks, axis=0)]
    for bit in bits("ctx"):
        chunks = chunks + [swap(chunk, "ctx", bit) for chunk in chunks]
    return chunks


def scatter(chunks):
    for bit in reversed(bits("ctx")):
        half = len(chunks) // 2
        chunks = [
            (keep.astype(FULL) + swap(send, "ctx", bit).astype(FULL)).astype(LOW)
            for keep, send in zip(chunks[:half], chunks[half:])
        ]
    n_dp = lax.axis_size("dp")
    parts = chunks[0].reshape(n_dp, -1, chunks[0].shape[-1])
    if n_dp == 4:
        half = parts.shape[2] // 2
        left, right = parts[:, :, :half], parts[:, :, half:]
        got_left = swap(jnp.stack([left[1], left[3]]), "dp", 1).astype(FULL)
        got_right = swap(right[2:], "dp", 2).astype(FULL)
        far_left = (left[2].astype(FULL) + got_left[1]).astype(LOW)
        far_right = (right[1].astype(FULL) + got_right[1]).astype(LOW)
        end_left = swap(far_left, "dp", 2).astype(FULL)
        end_right = swap(far_right, "dp", 1).astype(FULL)
        return jnp.concatenate(
            [
                left[0].astype(FULL) + got_left[0] + end_left,
                right[0].astype(FULL) + got_right[0] + end_right,
            ],
            axis=1,
        )
    for bit in reversed(bits("dp")):
        half = parts.shape[0] // 2
        parts = parts[:half].astype(FULL) + swap(parts[half:].astype(LOW), "dp", bit).astype(FULL)
    return parts[0].astype(FULL)


def line_scatter(part):
    return lax.psum_scatter(part, "tensor", scatter_dimension=0, tiled=True)


def line_gather(own):
    return lax.all_gather(own, "tensor", axis=0, tiled=True)


def tensor_total(term):
    for bit in bits("tensor"):
        low = term.astype(LOW)
        term = low.astype(FULL) + swap(low, "tensor", bit).astype(FULL)
    return term


def gather_few(row):
    for axis in ("dp", "ctx"):
        for bit in bits(axis):
            row = jnp.concatenate([row, swap(row, axis, bit)], axis=0)
    return pick(row, relative_blocks()[1])


def in_order(parts):
    total = parts[0]
    for part in parts[1:]:
        total = total + part
    return total


def few_total(value, axes):
    for axis in axes:
        n, me = lax.axis_size(axis), lax.axis_index(axis)
        if n == 2:
            value = value + swap(value, axis, 1)
            continue
        parts = jnp.stack([value] + [
            lax.ppermute(value, axis, [(i, i ^ k) for i in range(n)]) for k in range(1, n)
        ])
        value = in_order([lax.dynamic_index_in_dim(parts, me ^ k, 0, False) for k in range(n)])
    return value


def spread(target, columns, place, rows, tile):
    target[pl.ds(place, rows, stride=tile), :] = columns


def splat(target, table, first, rows):
    for n in range(N):
        target[pl.ds(n, rows, stride=N), :] = jnp.broadcast_to(
            table[:, first + n : first + n + 1], (rows, LANES)
        )


def columns_of(j):
    return slice(j * LANES, (j + 1) * LANES)


def edge_kernel(
    rows, groups, tile, unroll, flag, size_ref, value_ref, grad_ref, gate_ref, coef_ref, rate_ref,
    edge_ref, size_s, term_s, coef_s,
):
    backward = flag[0] == 1

    @pl.when(pl.program_id(0) == 0)
    def _():
        edge_ref[...] = jnp.zeros_like(edge_ref)

    for j in range(tile):
        if j < groups:
            spread(size_s, size_ref[:, columns_of(j)], j, rows, tile)
        else:
            spread(size_s, jnp.zeros((rows, LANES), FULL), j, rows, tile)
            spread(term_s, jnp.zeros((rows, LANES), FULL), j, rows, tile)

    def loop(body):
        first = tuple(edge_ref[n] for n in range(N))
        last = lax.fori_loop(0, rows, body, first, unroll=unroll)
        for n in range(N):
            edge_ref[n] = last[n]

    @pl.when(jnp.logical_not(backward))
    def _():
        for j in range(groups):
            cut = columns_of(j)
            spread(term_s, size_ref[:, cut] * value_ref[:, cut].astype(FULL), j, rows, tile)
        splat(coef_s, coef_ref, 0, rows)

        def body(t, state):
            place = pl.ds(pl.multiple_of(t * tile, tile), tile)
            size, term = size_s[place, :], term_s[place, :]
            return tuple(
                jnp.exp2(size * rate_ref[n]) * state[n] + term * coef_s[pl.ds(t * N + n, 1), :]
                for n in range(N)
            )

        loop(body)

    @pl.when(backward)
    def _():
        for j in range(groups):
            cut = columns_of(j)
            gate = gate_ref[:, cut].astype(FULL)
            spread(term_s, grad_ref[:, cut] * gate * jax.nn.sigmoid(gate), j, rows, tile)
        splat(coef_s, coef_ref, N, rows)

        def body(step, state):
            t = rows - 1 - step
            place = pl.ds(pl.multiple_of(t * tile, tile), tile)
            size, term = size_s[place, :], term_s[place, :]
            return tuple(
                jnp.exp2(size * rate_ref[n])
                * (state[n] + term * coef_s[pl.ds(t * N + n, 1), :])
                for n in range(N)
            )

        loop(body)


def forward_kernel(
    rows, groups, tile, part, unroll,
    size_ref, value_ref, grad_ref, gate_ref, coef_ref, rate_ref, start_ref, skip_ref, pick_ref,
    gated_ref, gate_grad_ref, before_ref, grad_c_ref, grad_skip_ref,
    size_s, input_s, grad_s, out_s, b_s, c_s, product_s, state_s,
):
    @pl.when(pl.program_id(0) == 0)
    def _():
        state_s[...] = start_ref[...]
        grad_skip_ref[...] = jnp.zeros_like(grad_skip_ref)

    blank = jnp.zeros((rows, LANES), FULL)
    for j in range(tile):
        if j < groups:
            cut = columns_of(j)
            size = size_ref[:, cut]
            value = value_ref[:, cut].astype(FULL)
            gate = gate_ref[:, cut].astype(FULL)
            scan_grad = grad_ref[:, cut] * gate * jax.nn.sigmoid(gate)
            spread(size_s, size, j, rows, tile)
            spread(input_s, size * value, j, rows, tile)
            spread(grad_s, scan_grad, j, rows, tile)
            grad_skip_ref[:, cut] += jnp.sum(scan_grad * value, axis=0, keepdims=True)
        else:
            for target in (size_s, input_s, grad_s):
                spread(target, blank, j, rows, tile)
    splat(b_s, coef_ref, 0, rows)
    splat(c_s, coef_ref, N, rows)
    for low in range(0, N, part):
        rate = [rate_ref[n] for n in range(low, low + part)]

        def body(t, state):
            state = list(state)
            place = pl.ds(pl.multiple_of(t * tile, tile), tile)
            size, term, grad = size_s[place, :], input_s[place, :], grad_s[place, :]
            out = None
            for k in range(part):
                n = low + k
                before_ref[t, n] = state[k]
                state[k] = (
                    jnp.exp2(size * rate[k]) * state[k] + term * b_s[pl.ds(t * N + n, 1), :]
                )
                read = c_s[pl.ds(t * N + n, 1), :] * state[k]
                out = read if out is None else out + read
                product_s[place, columns_of(n)] = state[k] * grad
            if low == 0:
                out_s[place, :] = out
            else:
                out_s[place, :] = out_s[place, :] + out
            return tuple(state)

        first = tuple(state_s[n] for n in range(low, low + part))
        last = lax.fori_loop(0, rows, body, first, unroll=unroll)
        for k in range(part):
            state_s[low + k] = last[k]
    for j in range(groups):
        cut = columns_of(j)
        scan_out = out_s[pl.ds(j, rows, stride=tile), :] + skip_ref[:, cut] * value_ref[
            :, cut
        ].astype(FULL)
        gate = gate_ref[:, cut].astype(FULL)
        sigma = jax.nn.sigmoid(gate)
        gated_ref[:, cut] = (scan_out * (gate * sigma)).astype(LOW)
        slope = sigma * (1.0 + gate * (1.0 - sigma))
        gate_grad_ref[:, cut] = (grad_ref[:, cut] * scan_out * slope).astype(LOW)
    sums = jnp.dot(product_s[...].astype(LOW), pick_ref[...], preferred_element_type=FULL)
    grad_c_ref[...] = jnp.sum(sums.reshape(rows, tile, LANES), axis=1)


def backward_kernel(
    rows, groups, tile, part, unroll,
    size_ref, value_ref, grad_ref, gate_ref, coef_ref, rate_ref, tail_ref, skip_ref, pick_ref,
    before_ref,
    pre_low_ref, grad_value_ref, grad_b_ref, grad_rate_ref, grad_bias_ref,
    size_s, input_s, grad_s, along_s, rated_s, b_s, c_s, product_s, state_s,
):
    @pl.when(pl.program_id(0) == 0)
    def _():
        state_s[...] = tail_ref[...]
        grad_rate_ref[...] = jnp.zeros_like(grad_rate_ref)
        grad_bias_ref[...] = jnp.zeros_like(grad_bias_ref)

    blank = jnp.zeros((rows, LANES), FULL)
    for j in range(tile):
        if j < groups:
            cut = columns_of(j)
            size = size_ref[:, cut]
            gate = gate_ref[:, cut].astype(FULL)
            spread(size_s, size, j, rows, tile)
            spread(input_s, size * value_ref[:, cut].astype(FULL), j, rows, tile)
            spread(grad_s, grad_ref[:, cut] * gate * jax.nn.sigmoid(gate), j, rows, tile)
        else:
            for target in (size_s, input_s, grad_s):
                spread(target, blank, j, rows, tile)
    splat(b_s, coef_ref, 0, rows)
    splat(c_s, coef_ref, N, rows)
    for low in range(0, N, part):
        rate = [rate_ref[n] for n in range(low, low + part)]

        def body(step, carry):
            state, total = list(carry[0]), list(carry[1])
            t = rows - 1 - step
            place = pl.ds(pl.multiple_of(t * tile, tile), tile)
            size, term, grad = size_s[place, :], input_s[place, :], grad_s[place, :]
            along = rated = None
            for k in range(part):
                n = low + k
                adjoint = c_s[pl.ds(t * N + n, 1), :] * grad + state[k]
                state[k] = jnp.exp2(size * rate[k]) * adjoint
                through = state[k] * before_ref[t, n]
                first = adjoint * b_s[pl.ds(t * N + n, 1), :]
                second = through * rate[k]
                along = first if along is None else along + first
                rated = second if rated is None else rated + second
                total[k] = total[k] + through * size
                product_s[place, columns_of(n)] = adjoint * term
            if low == 0:
                along_s[place, :] = along
                rated_s[place, :] = rated
            else:
                along_s[place, :] = along_s[place, :] + along
                rated_s[place, :] = rated_s[place, :] + rated
            return tuple(state), tuple(total)

        place = range(low, low + part)
        first = (tuple(state_s[n] for n in place), tuple(grad_rate_ref[n] for n in place))
        state, total = lax.fori_loop(0, rows, body, first, unroll=unroll)
        for k in range(part):
            state_s[low + k] = state[k]
            grad_rate_ref[low + k] = total[k]
    for j in range(groups):
        cut = columns_of(j)
        size = size_ref[:, cut]
        along = along_s[pl.ds(j, rows, stride=tile), :]
        rated = rated_s[pl.ds(j, rows, stride=tile), :]
        grad_size = along * value_ref[:, cut].astype(FULL) + LOG_2 * rated
        grad_pre = grad_size * (jnp.tanh(0.5 * size) * (1.0 + jnp.exp(-size)))
        pre_low_ref[:, cut] = grad_pre.astype(LOW)
        grad_bias_ref[:, cut] += jnp.sum(grad_pre, axis=0, keepdims=True)
        scan_grad = grad_s[pl.ds(j, rows, stride=tile), :]
        grad_value_ref[:, cut] = along * size + skip_ref[:, cut] * scan_grad
    sums = jnp.dot(product_s[...].astype(LOW), pick_ref[...], preferred_element_type=FULL)
    grad_b_ref[...] = jnp.sum(sums.reshape(rows, tile, LANES), axis=1)


def picker():
    shape = (N * LANES, LANES)
    state = lax.broadcasted_iota(jnp.int32, shape, 0) // LANES
    return (state == lax.broadcasted_iota(jnp.int32, shape, 1)).astype(LOW)


def tiles(channels):
    groups = channels // LANES
    return groups, 8 * pl.cdiv(groups, 8)


def tiled(table):
    groups, tile = tiles(table.shape[-1])
    table = table.reshape(table.shape[:-1] + (groups, LANES))
    pads = [(0, 0)] * (table.ndim - 2) + [(0, tile - groups), (0, 0)]
    return jnp.pad(table, pads)


def flat(table, channels):
    groups, _ = tiles(channels)
    return table[..., :groups, :].reshape(table.shape[:-2] + (channels,))


def cost(micro, length, ops, size):
    work = micro * length * N * 1024 * ops * 100
    return pl.CostEstimate(flops=work, bytes_accessed=size, transcendentals=0)


def limits():
    return pltpu.CompilerParams(vmem_limit_bytes=56 * 1024 * 1024)


def scan_edge(flag, size, value, grad, gate, coef, rate):
    length, channels = size.shape
    groups, tile = tiles(channels)
    rows = min(64, length)
    count = length // rows

    def place(i, f):
        return (jnp.where(f[0] == 0, i, count - 1 - i), 0)

    wide = pl.BlockSpec((rows, channels), place)
    cube = pl.BlockSpec((N, tile, LANES), lambda i, f: (0, 0, 0))
    return pl.pallas_call(
        functools.partial(edge_kernel, rows, groups, tile, 4),
        grid_spec=pltpu.PrefetchScalarGridSpec(
            num_scalar_prefetch=1,
            grid=(count,),
            in_specs=[wide] * 4 + [pl.BlockSpec((rows, 2 * N), place), cube],
            out_specs=cube,
            scratch_shapes=[pltpu.VMEM((rows * tile, LANES), FULL)] * 2
            + [pltpu.VMEM((rows * N, LANES), FULL)],
        ),
        out_shape=jax.ShapeDtypeStruct((N, tile, LANES), FULL),
        compiler_params=limits(),
        cost_estimate=cost(1, length, 8, size.size * 12),
        name="scan_edge",
    )(flag, size, value, grad, gate, coef, rate)


def scan_forward(size, value, grad, gate, coef, rate, start, skip):
    length, channels = size.shape
    groups, tile = tiles(channels)
    rows = min(64, length)
    wide = pl.BlockSpec((rows, channels), lambda i: (i, 0))
    row = pl.BlockSpec((1, channels), lambda i: (0, 0))
    cube = pl.BlockSpec((N, tile, LANES), lambda i: (0, 0, 0))
    return pl.pallas_call(
        functools.partial(forward_kernel, rows, groups, tile, 8, 4),
        grid=(length // rows,),
        in_specs=[wide] * 4
        + [
            pl.BlockSpec((rows, 2 * N), lambda i: (i, 0)),
            cube,
            cube,
            row,
            pl.BlockSpec((N * LANES, LANES), lambda i: (0, 0)),
        ],
        out_specs=[
            wide,
            wide,
            pl.BlockSpec((rows, N, tile, LANES), lambda i: (i, 0, 0, 0)),
            pl.BlockSpec((rows, LANES), lambda i: (i, 0)),
            row,
        ],
        out_shape=[
            jax.ShapeDtypeStruct(size.shape, LOW),
            jax.ShapeDtypeStruct(size.shape, LOW),
            jax.ShapeDtypeStruct((length, N, tile, LANES), FULL),
            jax.ShapeDtypeStruct((length, LANES), FULL),
            jax.ShapeDtypeStruct((1, channels), FULL),
        ],
        scratch_shapes=[pltpu.VMEM((rows * tile, LANES), FULL)] * 4
        + [pltpu.VMEM((rows * N, LANES), FULL)] * 2
        + [pltpu.VMEM((rows * tile, N * LANES), FULL), pltpu.VMEM((N, tile, LANES), FULL)],
        compiler_params=limits(),
        cost_estimate=cost(1, length, 15, size.size * 80),
        name="scan_forward",
    )(size, value, grad, gate, coef, rate, start, skip, picker())


def scan_backward(size, value, grad, gate, coef, rate, tail, skip, before):
    length, channels = size.shape
    groups, tile = tiles(channels)
    rows = min(64, length)
    last = length // rows - 1
    wide = pl.BlockSpec((rows, channels), lambda i: (last - i, 0))
    row = pl.BlockSpec((1, channels), lambda i: (0, 0))
    cube = pl.BlockSpec((N, tile, LANES), lambda i: (0, 0, 0))
    return pl.pallas_call(
        functools.partial(backward_kernel, rows, groups, tile, 8, 4),
        grid=(length // rows,),
        in_specs=[wide] * 4
        + [
            pl.BlockSpec((rows, 2 * N), lambda i: (last - i, 0)),
            cube,
            cube,
            row,
            pl.BlockSpec((N * LANES, LANES), lambda i: (0, 0)),
            pl.BlockSpec((rows, N, tile, LANES), lambda i: (last - i, 0, 0, 0)),
        ],
        out_specs=[wide, wide, pl.BlockSpec((rows, LANES), lambda i: (last - i, 0)), cube, row],
        out_shape=[
            jax.ShapeDtypeStruct(size.shape, LOW),
            jax.ShapeDtypeStruct(size.shape, FULL),
            jax.ShapeDtypeStruct((length, LANES), FULL),
            jax.ShapeDtypeStruct((N, tile, LANES), FULL),
            jax.ShapeDtypeStruct((1, channels), FULL),
        ],
        scratch_shapes=[pltpu.VMEM((rows * tile, LANES), FULL)] * 5
        + [pltpu.VMEM((rows * N, LANES), FULL)] * 2
        + [pltpu.VMEM((rows * tile, N * LANES), FULL), pltpu.VMEM((N, tile, LANES), FULL)],
        compiler_params=limits(),
        cost_estimate=cost(1, length, 20, size.size * 80),
        name="scan_backward",
    )(size, value, grad, gate, coef, rate, tail, skip, picker(), before)


def edges(size, value, grad, gate, coef, rate):
    count, place = lax.axis_size("ctx"), lax.axis_index("ctx")
    args = (size, value, grad, gate, coef, rate)
    if count == 2:
        edge = scan_edge(place.astype(jnp.int32)[None], *args)
        other = swap(edge, "ctx", 1)
        return jnp.where(place == 1, other, 0.0), jnp.where(place == 0, other, 0.0)
    last = scan_edge(jnp.zeros((1,), jnp.int32), *args)
    head = scan_edge(jnp.ones((1,), jnp.int32), *args)
    through = jnp.exp2(rate * tiled(jnp.sum(size, axis=0, keepdims=True)))
    lasts, heads, throughs = (lax.all_gather(a, "ctx") for a in (last, head, through))
    start = tail = jnp.zeros(last.shape, FULL)
    for i in range(count):
        start = jnp.where(i < place, throughs[i] * start + lasts[i], start)
        j = count - 1 - i
        tail = jnp.where(j > place, throughs[j] * tail + heads[j], tail)
    return start, tail


def block_of(index, width):
    return pl.ds(pl.multiple_of(index * width, width), width)


def normalize_kernel(width, chunks, order, x_ref, grad_ref, gain_ref, *outs):
    x = x_ref[...].astype(FULL)
    inverse = lax.rsqrt(jnp.mean(x * x, axis=1, keepdims=True) + norm_epsilon)
    columns = D // chunks
    for chunk in range(chunks):
        for low in range(0, columns, width):
            q = (chunk * columns + low) // width
            source = block_of(order[q], width)
            place = slice(low, low + width)
            value = x_ref[:, source].astype(FULL) * inverse * gain_ref[q : q + 1, :]
            outs[chunk][:, place] = value.astype(LOW)
            outs[chunks + chunk][:, place] = grad_ref[:, source]


def normalize(order, m, length, x, grad, gain, n_ctx):
    height, width = length, D // len(order)
    if width % LANES:
        x, grad = x[m * length : (m + 1) * length], grad[m * length : (m + 1) * length]
        full = x.astype(FULL)
        inverse = lax.rsqrt(jnp.mean(full * full, axis=1, keepdims=True) + norm_epsilon)

        def arrange(array):
            blocks = jnp.swapaxes(array.reshape(height, len(order), width), 0, 1)
            blocks = pick(blocks, order).reshape(n_ctx, -1, height, width)
            return list(jnp.swapaxes(blocks, 1, 2).reshape(n_ctx, height, D // n_ctx))

        gain = pick(gain, inverse_of(order))
        return arrange((full * inverse * gain.reshape(1, D)).astype(LOW)), arrange(grad)
    rows = min(128, height)
    wide = pl.BlockSpec((rows, D), lambda i, o: (m * (length // rows) + i, 0))
    out = pl.BlockSpec((rows, D // n_ctx), lambda i, o: (i, 0))
    shape = jax.ShapeDtypeStruct((height, D // n_ctx), LOW)
    outs = pl.pallas_call(
        functools.partial(normalize_kernel, width, n_ctx),
        grid_spec=pltpu.PrefetchScalarGridSpec(
            num_scalar_prefetch=1,
            grid=(height // rows,),
            in_specs=[wide, wide, pl.BlockSpec((len(order), width), lambda i, o: (0, 0))],
            out_specs=[out] * (2 * n_ctx),
        ),
        out_shape=[shape] * (2 * n_ctx),
        compiler_params=limits(),
        name="normalize",
    )(jnp.stack(order).astype(jnp.int32), x, grad, gain)
    return outs[:n_ctx], outs[n_ctx:]


def inverse_of(order):
    return relative_blocks()[1]


def unpermuted(chunks, inverse_order):
    rows, width = jnp.concatenate(chunks, axis=1), D // len(inverse_order)
    return jnp.concatenate(
        [lax.dynamic_slice_in_dim(rows, q * width, width, 1) for q in inverse_order], axis=1
    )


def own_block(block, share):
    return pl.BlockSpec((share, D), lambda i, o: (o[block], 0))


def whole_of(array):
    return pl.BlockSpec(array.shape, lambda i, o: (0,) * array.ndim)


def mix_kernel(width, per_chunk, order, x_ref, branch_ref, out_ref):
    for q in range(D // width):
        place = block_of(order[q], width)
        value = branch_ref[:, q * width : (q + 1) * width].astype(FULL)
        out_ref[:, place] = (x_ref[:, place].astype(FULL) + value).astype(LOW)


def mix(order, block, x, branch):
    width, share = D // len(order), branch.shape[0]
    if width % LANES:
        x = lax.dynamic_slice_in_dim(x, block * share, share, 0)
        return (x.astype(FULL) + unpermuted([branch.astype(FULL)], inverse_of(order))).astype(LOW)
    return pl.pallas_call(
        functools.partial(mix_kernel, width, 0),
        grid_spec=pltpu.PrefetchScalarGridSpec(
            num_scalar_prefetch=1,
            grid=(1,),
            in_specs=[own_block(len(order), share), whole_of(branch)],
            out_specs=whole_of(branch),
        ),
        out_shape=jax.ShapeDtypeStruct((share, D), LOW),
        compiler_params=limits(),
        name="mix",
    )(jnp.stack(order + [block]).astype(jnp.int32), x, branch)


def token_kernel(width, order, x_ref, grad_ref, gain_ref, normed_ref, out_ref, gain_out_ref, scaled_s):
    x = x_ref[...].astype(FULL)
    inverse = lax.rsqrt(jnp.mean(x * x, axis=1, keepdims=True) + norm_epsilon)
    total = jnp.zeros_like(inverse)
    for q in range(D // width):
        place = block_of(order[q], width)
        value = normed_ref[:, q * width : (q + 1) * width].astype(FULL)
        part = x_ref[:, place].astype(FULL)
        gain_out_ref[pl.ds(order[q], 1), :] = jnp.sum(
            value * part * inverse, axis=0, keepdims=True
        )
        scaled = value * gain_ref[q : q + 1, :]
        total = total + jnp.sum(part * scaled, axis=1, keepdims=True)
        scaled_s[:, place] = scaled
    slope = inverse * inverse * inverse * (total / D)
    out_ref[...] = (
        grad_ref[...].astype(FULL) + inverse * scaled_s[...] - x * slope
    ).astype(LOW)


def token_rows(order, block, x, grad, gain, normed):
    width, share = D // len(order), normed.shape[0]
    if width % LANES:
        x = lax.dynamic_slice_in_dim(x, block * share, share, 0).astype(FULL)
        grad = lax.dynamic_slice_in_dim(grad, block * share, share, 0).astype(FULL)
        value = unpermuted([normed.astype(FULL)], inverse_of(order))
        inverse = lax.rsqrt(jnp.mean(x * x, axis=1, keepdims=True) + norm_epsilon)
        part = jnp.sum(value * x * inverse, axis=0).reshape(len(order), width)
        scaled = value * pick(gain, inverse_of(order)).reshape(1, D)
        slope = inverse * inverse * inverse * jnp.mean(x * scaled, axis=1, keepdims=True)
        return (grad + inverse * scaled - x * slope).astype(LOW), part
    wide = own_block(len(order), share)
    return pl.pallas_call(
        functools.partial(token_kernel, width),
        grid_spec=pltpu.PrefetchScalarGridSpec(
            num_scalar_prefetch=1,
            grid=(1,),
            in_specs=[wide, wide, whole_of(gain), whole_of(normed)],
            out_specs=[whole_of(normed), whole_of(gain)],
            scratch_shapes=[pltpu.VMEM((share, D), FULL)],
        ),
        out_shape=[
            jax.ShapeDtypeStruct((share, D), LOW),
            jax.ShapeDtypeStruct((len(order), width), FULL),
        ],
        compiler_params=limits(),
        name="token_rows",
    )(jnp.stack(order + [block]).astype(jnp.int32), x, grad, gain, normed)


def conv_kernel(
    value_grad_ref, proj_ref, xproj_ref, conv_in_ref, earlier_ref, table_ref,
    out_ref, last_ref, head_ref, sums_ref, padded_s, grad_s,
):
    length = conv_in_ref.shape[0]
    taps = [table_ref[k : k + 1, :] for k in range(K)]
    padded_s[pl.ds(0, 8), :] = earlier_ref[...].astype(FULL)
    padded_s[pl.ds(8, length), :] = conv_in_ref[...].astype(FULL)
    conv = table_ref[K : K + 1, :] + taps[0] * padded_s[pl.ds(9 - K, length), :]
    for k in range(1, K):
        conv = conv + taps[k] * padded_s[pl.ds(9 - K + k, length), :]
    sigma = jax.nn.sigmoid(conv)
    slope = sigma * (1.0 + conv * (1.0 - sigma))
    grad_values = value_grad_ref[...] + jnp.dot(
        proj_ref[...], xproj_ref[...], preferred_element_type=FULL
    )
    grad_conv = grad_values * slope
    grad_s[pl.ds(0, length), :] = grad_conv
    grad_s[pl.ds(length, 8), :] = jnp.zeros((8, grad_conv.shape[1]), FULL)
    for k in range(K):
        sums_ref[k : k + 1, :] = jnp.sum(
            grad_conv * padded_s[pl.ds(9 - K + k, length), :], axis=0, keepdims=True
        )
    sums_ref[K : K + 1, :] = jnp.sum(grad_conv, axis=0, keepdims=True)
    sums_ref[K + 1 :, :] = jnp.zeros((7 - K, grad_conv.shape[1]), FULL)
    total = taps[K - 1] * grad_conv
    for k in range(K - 1):
        total = total + taps[k] * grad_s[pl.ds(K - 1 - k, length), :]
    out_ref[...] = total.astype(LOW)
    last_ref[...] = total[length - 8 :]
    head_ref[...] = jnp.zeros_like(head_ref)
    for p in range(K - 1):
        row = taps[0] * grad_s[pl.ds(p, 1), :]
        for k in range(1, p + 1):
            row = row + taps[k] * grad_s[pl.ds(p - k, 1), :]
        head_ref[9 - K + p : 10 - K + p, :] = row


def conv_backward(value_grad, proj_grad, xproj_low, conv_in, earlier, table):
    length, channels = value_grad.shape
    width = min(256, channels)
    tall = pl.BlockSpec((length, width), lambda j: (0, j))
    short = pl.BlockSpec((8, width), lambda j: (0, j))
    few = jax.ShapeDtypeStruct((8, channels), FULL)
    return pl.pallas_call(
        conv_kernel,
        grid=(channels // width,),
        in_specs=[
            tall,
            pl.BlockSpec(proj_grad.shape, lambda j: (0, 0)),
            pl.BlockSpec((proj_grad.shape[1], width), lambda j: (0, j)),
            tall,
            short,
            pl.BlockSpec((8, width), lambda j: (0, j)),
        ],
        out_specs=[tall, short, short, short],
        out_shape=[jax.ShapeDtypeStruct((length, channels), LOW), few, few, few],
        scratch_shapes=[pltpu.VMEM((length + 8, width), FULL)] * 2,
        compiler_params=limits(),
        name="conv_backward",
    )(value_grad, proj_grad, xproj_low, conv_in, earlier, table)


def dot(a, b, dims, kind=FULL):
    return lax.dot_general(a, b, (dims, ((), ())), preferred_element_type=FULL).astype(kind)


def per_device(
    tokens,
    out_grad,
    norm_gain,
    in_weight,
    xproj_weight,
    step_weight,
    outproj_weight,
    channel_table,
    gain_second,
    in_rows,
    in_cols,
    xproj_rows,
    xproj_cols,
    step_rows,
    step_cols,
    out_rows,
    out_cols,
    table_second,
):
    micro = tokens.shape[0]
    length = tokens.shape[2]
    inner = in_weight.shape[2]
    n_tensor = lax.axis_size("tensor")
    n_owner = lax.axis_size("dp") * lax.axis_size("ctx")
    owned = in_weight.shape[0]
    order, inverse_order = relative_blocks()
    n_ctx = lax.axis_size("ctx")
    own_axes = ("ctx", "dp")
    me = lax.axis_index("tensor")

    n_x, n_s = xproj_weight.shape[0], step_weight.shape[0]
    gain_row = jnp.pad(norm_gain.astype(LOW), (0, inner - owned))[None]
    in_own = in_weight.reshape(owned, 2 * inner).astype(LOW)
    first_own = [in_own[:, :inner], xproj_weight.astype(LOW), step_weight.astype(LOW), gain_row]
    pad_rows = -(owned + n_x + n_s + 1) % 64
    if pad_rows:
        first_own.append(jnp.zeros((pad_rows, inner), LOW))
    blocks, arrived = fetch(jnp.concatenate(first_own, axis=0))
    small = jnp.concatenate(join([block[owned:] for block in blocks]), axis=0)
    small = small.reshape(n_owner, -1, inner)
    conv_low = join([block[:owned] for block in blocks])
    gain_low = small[:, n_x + n_s, :owned].astype(FULL)
    small = pick(small, inverse_order)
    xproj_low = small[:, :n_x].reshape(n_owner * n_x, inner)
    step_low = small[:, n_x : n_x + n_s].reshape(n_owner * n_s, inner)
    gate_own = after(in_own[:, inner:], *arrived)
    out_own = after(outproj_weight.astype(LOW), *arrived)

    taps = channel_table[:K]
    conv_bias = channel_table[K]
    step_bias = channel_table[K + 1]
    skip = channel_table[K + 2][None]
    a_neg = -jnp.exp(channel_table[K + 3 :])
    rate = tiled(a_neg / LOG_2)

    def contract(parts, weights):
        total = dot(parts[0], weights[0], ((1,), (0,)))
        for part, weight in zip(parts[1:], weights[1:]):
            total = total + dot(part, weight, ((1,), (0,)))
        return total

    every = range(micro)
    tokens_flat = tokens.reshape(micro * length, D)
    grad_flat = out_grad.reshape(micro * length, D)
    normed, grad_rel = zip(
        *(normalize(order, m, length, tokens_flat, grad_flat, gain_low, n_ctx) for m in every)
    )
    conv_in = [contract(normed[m], conv_low).astype(LOW) for m in every]
    earlier, values, part_proj = [], [], []
    for m in every:
        earlier.append(shifted(conv_in[m][length - 8 :], "ctx", 1))
        padded = jnp.concatenate([earlier[m], conv_in[m]], axis=0).astype(FULL)
        conv = conv_bias + taps[0] * padded[9 - K : 9 - K + length]
        for k in range(1, K):
            conv = conv + taps[k] * padded[9 - K + k : 9 - K + k + length]
        values.append(jax.nn.silu(conv).astype(LOW))
        part_proj.append(dot(values[m], xproj_low, ((1,), (1,))))
    gate_blocks, out_blocks = fetch_two(gate_own, out_own, conv_in[0], part_proj)
    gate_low, out_low = join(gate_blocks), join(out_blocks)
    gate_in = [contract(normed[m], gate_low).astype(LOW) for m in every]
    grad_gated, size, coef, rank_low = [], [], [], []
    for m in every:
        proj = tensor_total(part_proj[m])
        rank_low.append(proj[:, :R].astype(LOW))
        coef.append(proj[:, R:])
        pre = dot(rank_low[m], step_low, ((1,), (0,))) + step_bias
        size.append(jax.nn.softplus(pre))
    gated, gate_grad, before, grad_c, grad_skip, tail, branch = [], [], [], [], [], [], []
    for m in every:
        weights_now = out_low if m == 0 else [after(w, branch[-1]) for w in out_low]
        grad_gated.append(contract(grad_rel[m], weights_now))
        args = (size[m], values[m], grad_gated[m], gate_in[m], coef[m], rate)
        entering, leaving = edges(*args)
        tail.append(leaving)
        outs = scan_forward(*args, entering, skip)
        for held, out in zip((gated, gate_grad, before, grad_c, grad_skip), outs):
            held.append(out)
        branch.append(
            jnp.concatenate([dot(gated[m], w, ((1,), (1,)), LOW) for w in out_low], axis=1)
        )
    own_mixed = [
        mix(order, m * n_tensor + me, tokens_flat, line_scatter(branch[m])) for m in every
    ]

    mixed_list = [line_gather(own) for own in own_mixed]

    def stacked(parts):
        ends = ((0, micro - 1, 0), (0, 0, 0), (0, 0, 0))
        whole = lax.pad(parts[0][None], jnp.zeros((), LOW), ends)
        for m in range(1, micro):
            whole = lax.dynamic_update_slice(whole, parts[m][None], (m, 0, 0))
        return whole

    def over_micros(left, right):
        total = dot(left[0], right[0], ((0,), (0,)))
        for a, b in zip(left[1:], right[1:]):
            total = total + dot(a, b, ((0,), (0,)))
        return total

    def chunks_of(parts):
        return list(zip(*parts))

    conv_grads, proj_grads, gain_parts, tables, partial, pre_lows = [], [], [], [], [], []
    part_out = part_gate = ()
    tokens_out, before_next = [], []
    mixed_ready = [own_mixed[0]]
    for m in every:
        leaving = after(tail[m], branch[-1], *mixed_ready, *before_next)
        pre_low, value_grad, grad_b, grad_rate, grad_bias = scan_backward(
            size[m], values[m], grad_gated[m], gate_in[m], coef[m], rate, leaving, skip, before[m]
        )
        if m > 0:
            pre_low = after(pre_low, mixed_list[-1])
        pre_lows.append(pre_low)
        grad_rank = dot(pre_low, step_low, ((1,), (1,)))
        part = jnp.concatenate([grad_rank, grad_b[:, :N], grad_c[m][:, :N]], axis=1)
        proj_grad = tensor_total(part).astype(LOW)
        proj_grads.append(proj_grad)
        if m == 0:
            gated_then = [after(gated[0], part)] + gated[1:]
            part_out = [over_micros(g, gated_then).astype(LOW) for g in chunks_of(grad_rel)]
            filler = part_out
        else:
            normed_then = [[after(n, part) for n in parts] for parts in normed]
            if m == micro - 1:
                part_gate = [
                    over_micros(g, gate_grad).astype(LOW) for g in chunks_of(normed_then)
                ]
            filler = list(part_gate)
        gate_grad_then = after(gate_grad[m], part)
        gate_part = [dot(gate_grad_then, g, ((1,), (1,))) for g in gate_low]
        conv_grad, last, head, sums = conv_backward(
            after(value_grad, *filler, *gate_part, *tokens_out, mixed_list[0]),
            proj_grad, xproj_low, conv_in[m], earlier[m], channel_table[:8],
        )
        last = last + shifted(head, "ctx", -1)
        conv_grad = lax.dynamic_update_slice(conv_grad, last.astype(LOW), (length - 8, 0))
        conv_grads.append(conv_grad)
        partial.append(
            jnp.concatenate(
                [
                    (g + dot(conv_grad, c, ((1,), (1,)))).astype(LOW)
                    for g, c in zip(gate_part, conv_low)
                ],
                axis=1,
            )
        )
        mixed_ready, before_next = own_mixed, [partial[m]]
        partial[m] = after(partial[m], mixed_list[-1])
        token, gain_part = token_rows(
            order, m * n_tensor + me, tokens_flat, grad_flat, gain_low, line_scatter(partial[m])
        )
        gain_parts.append(gain_part)
        tokens_out.append(token)
        tables.append(
            jnp.concatenate(
                [sums[: K + 1], grad_bias, grad_skip[m], flat(grad_rate, inner) * a_neg], axis=0
            )
        )
    normed_then = [[after(n, partial[-1]) for n in parts] for parts in normed]
    part_conv = [over_micros(g, conv_grads).astype(LOW) for g in chunks_of(normed_then)]
    shard_out = scatter(part_out)
    shard_gate = scatter(part_gate)
    shard_conv = scatter(part_conv)
    token_grad = stacked([line_gather(token) for token in tokens_out])
    token_grad = token_grad.reshape(tokens.shape)
    mixed = stacked(mixed_list).reshape(tokens.shape)
    part_step = over_micros(rank_low, pre_lows)
    part_xproj = over_micros(proj_grads, values)
    part_small = jnp.concatenate(
        [part_xproj.reshape(n_owner, n_x, inner), part_step.reshape(n_owner, n_s, inner)], axis=1
    )
    pad_rows = -(n_x + n_s) % 16
    part_small = jnp.pad(part_small, ((0, 0), (0, pad_rows), (0, 0))).astype(LOW)
    shard_small = scatter(list(pick(part_small, order).reshape(n_ctx, -1, inner)))
    shard_xproj = shard_small[:n_x]
    shard_step = shard_small[n_x : n_x + n_s]
    gain_grad = butterfly(in_order(gain_parts), ("tensor",) + own_axes)
    owner = lax.axis_index("dp") * n_ctx + lax.axis_index("ctx")
    shard_gain = lax.dynamic_index_in_dim(gain_grad, owner, 0, False)
    grad_table = in_order(tables)

    shard_in = jnp.stack([shard_conv, shard_gate], axis=1)
    matrices = (shard_in, shard_xproj, shard_step, shard_out)
    weights = (in_weight, xproj_weight, step_weight, outproj_weight)
    all_weights = [norm_gain] + list(weights) + [channel_table]
    shares = jnp.array([1.0 / n_tensor, 1.0, 1.0, 1.0, 1.0, 1.0 / n_owner], FULL)
    weight_sq = jnp.stack([jnp.sum(jnp.square(after(w, pre_lows[0]))) for w in all_weights]) * shares
    old_rows = (in_rows, xproj_rows, step_rows, out_rows)
    old_cols = (in_cols, xproj_cols, step_cols, out_cols)
    width_cols = (2 * E, E, E, E)
    width_rows = (D, R + 2 * N, R, D)
    squares = [matrix * matrix + square_floor for matrix in matrices]
    row_parts = [jnp.sum(square.reshape(square.shape[0], -1), axis=1) for square in squares]
    col_parts = [jnp.sum(square, axis=0).reshape(-1, inner) for square in squares]
    row_sums = few_total(jnp.concatenate(row_parts + [weight_sq]), ("tensor",))
    ends = [0]
    for part in row_parts + [weight_sq]:
        ends.append(ends[-1] + part.shape[0])
    row_sums = [row_sums[ends[i] : ends[i + 1]] for i in range(5)]
    row_news = [
        decay_rate * old_rows[i] + (1.0 - decay_rate) * row_sums[i] / width_cols[i]
        for i in range(4)
    ]
    totals = jnp.stack([jnp.sum(row_new) for row_new in row_news])
    scalars = few_total(jnp.concatenate([totals, row_sums[4]]), own_axes)
    row_totals, total_weight = scalars[:4], scalars[4:]
    summed = butterfly(jnp.concatenate(col_parts + [grad_table], axis=0), own_axes)
    col_sums = [summed[0:2], summed[2], summed[3], summed[4]]
    table_grad = summed[5:]
    col_news = [
        decay_rate * old_cols[i] + (1.0 - decay_rate) * col_sums[i] / width_rows[i]
        for i in range(4)
    ]
    updates = []
    for i in range(4):
        row_mean = row_totals[i] / width_rows[i]
        shape = (-1,) + (1,) * (matrices[i].ndim - 1)
        second = row_news[i].reshape(shape) * col_news[i][None] / row_mean
        updates.append(matrices[i] * lax.rsqrt(second))
    every_second = decay_rate * gather_few(after(gain_second[None], pre_lows[0])) + (
        1.0 - decay_rate
    ) * (gain_grad * gain_grad + square_floor)
    every_update = gain_grad * lax.rsqrt(every_second)
    new_gain_second = lax.dynamic_index_in_dim(every_second, owner, 0, False)
    gain_update = lax.dynamic_index_in_dim(every_update, owner, 0, False)
    new_table_second = decay_rate * table_second + (1.0 - decay_rate) * (
        table_grad * table_grad + square_floor
    )
    table_update = table_grad * lax.rsqrt(new_table_second)
    all_updates = [gain_update] + updates + [table_update]
    update_sq = jnp.stack([jnp.sum(u * u) for u in all_updates[1:]]) * shares[1:]
    total_update = few_total(update_sq, own_axes + ("tensor",))
    gain_sq = jnp.sum(every_update * every_update)[None]
    total_update = jnp.concatenate([gain_sq, total_update])
    counts = jnp.array([D, 2 * D * E, (R + 2 * N) * E, R * E, D * E, (K + 3 + N) * E], FULL)
    update_rms = jnp.sqrt(total_update / counts)
    factor = jnp.maximum(1.0, update_rms / clip_limit)
    scale = jnp.sqrt(total_weight / counts)
    stride = step_rate * scale / factor
    new_weights = [all_weights[i] - stride[i] * all_updates[i] for i in range(6)]
    return (
        mixed,
        token_grad,
        shard_gain,
        shard_in,
        shard_xproj,
        shard_step,
        shard_out,
        table_grad,
        new_weights[0],
        new_weights[1],
        new_weights[2],
        new_weights[3],
        new_weights[4],
        new_weights[5],
        new_gain_second,
        row_news[0],
        col_news[0],
        row_news[1],
        col_news[1],
        row_news[2],
        col_news[2],
        row_news[3],
        col_news[3],
        new_table_second,
        update_rms,
    )


def solution(mesh):
    rows = P(("dp", "ctx"))
    matrix = P(("dp", "ctx"), "tensor")
    cube = P(("dp", "ctx"), None, "tensor")
    table = P(None, "tensor")
    block = P(None, "dp", "ctx", None)
    cols = P("tensor")
    return jax.shard_map(
        per_device,
        mesh=mesh,
        in_specs=(block, block, rows, cube, matrix, matrix, matrix, table, rows)
        + (rows, table, rows, cols, rows, cols, rows, cols, table),
        out_specs=(block, block, rows, cube, matrix, matrix, matrix, table)
        + (rows, cube, matrix, matrix, matrix, table, rows)
        + (rows, table, rows, cols, rows, cols, rows, cols, table, P()),
        check_vma=False,
    )
```

time: 1010 us -> 690 us (0.68)
  the two profiles are of different devices: /device:TPU:24 before, /device:TPU:0 now
where the time goes in v2:
time: 690 us; the launch traced here: 680 us
  Pallas kernels  183 us (27%)
  waiting for transfers between devices  130 us (19%)
  matrix products  117 us (17%)
  other arithmetic  94.7 us (14%)
  starting transfers between devices  73.1 us (11%)
  local copies, waits for them, and re-layouts  63.4 us (9%)
  between operations  19.1 us (3%)
    ppermute x57, waiting for transfers between devices, swap(): lax.ppermute(block, axis, [(i, i ^ bit) for i in range(lax.axis_size(axis...  122 us
    dot_general x46, matrix products, dot(): lax.dot_general(a, b, (dims, ((), ())), preferred_element_type=FULL)  117 us
    pallas_call x2, Pallas kernels, scan_backward(): pl.pallas_call(functools.partial(backward_kernel, rows, groups, tile, 8,...  67.2 us
    pallas_call x2, Pallas kernels, scan_forward(): pl.pallas_call(functools.partial(forward_kernel, rows, groups, tile, 8, 4...  54 us
    ppermute x57, starting transfers between devices, swap(): lax.ppermute(block, axis, [(i, i ^ bit) for i in range(lax.axis_size(axis...  51.7 us
    unnamed x273, local copies, waits for them, and re-layouts  25.2 us
    pallas_call x2, Pallas kernels, scan_edge(): pl.pallas_call(functools.partial(edge_kernel, rows, groups, tile, 4), gri...  23 us
    ppermute x12, starting transfers between devices, few_total(): lax.ppermute(value, axis, [(i, i ^ k) for i in range(n)])  14.9 us
  transfers between devices with their start and end apart: 81, of which 32 were waited for; matrix products, arithmetic and copies ran while one was open for 35% of the time, Pallas kernels for 21%

profile of v2, /device:TPU:0, one launch (start us, length us, event | category | flops | bytes accessed | tf_op | source)
XLA Modules:
  0.0 679.6 jit_solution(17670469965628953161)
XLA Ops:
  15.6 13.2 %collective-permute-done = bf16[320,1024]{1,0:T(8,128)(2,1)S(1)} collective-permute-done((bf16[320,1024]{1,0:T(8,128)(2,1)S(1)}, bf16[320,1024]{1,0:T(8,128)(2,1)S(1)}, u32[]{:S(2)}, u32[]{:S(2)}) %collective-permute-start) | collective-permute-done | bytes 655392 | tf_op jit(solution)/shard_map/ppermute | solution.py:38
  34.2 5.4 collective-permute-done.2
  60.1 5.7 normalize.3
  65.8 5.7 normalize.2
  95.4 5.5 collective-permute-done.16
  118.0 8.1 %collective-permute-done.19 = bf16[512,160]{1,0:T(8,128)(2,1)S(1)} collective-permute-done((bf16[512,160]{1,0:T(8,128)(2,1)S(1)}, bf16[512,160]{1,0:T(8,128)(2,1)S(1)}, u32[]{:S(2)}, u32[]{:S(2)}) %collective-permute-start.19) | collective-permute-done | bytes 163872 | tf_op jit(solution)/shard_map/ppermute | solution.py:38
  126.3 8.3 %collective-permute-done.8 = bf16[512,160]{1,0:T(8,128)(2,1)S(1)} collective-permute-done((bf16[512,160]{1,0:T(8,128)(2,1)S(1)}, bf16[512,160]{1,0:T(8,128)(2,1)S(1)}, u32[]{:S(2)}, u32[]{:S(2)}) %collective-permute-start.8) | collective-permute-done | bytes 163872 | tf_op jit(solution)/shard_map/ppermute | solution.py:38
  158.4 11.5 %scan_edge.2 = f32[16,8,128]{2,1,0:T(8,128)} custom-call(s32[1]{0:T(128)} %bitcast.21.flag, f32[512,1024]{1,0:T(8,128)} %compare_select_fusion.1.size_ref, bf16[512,1024]{1,0:T(8,128)(2,1)} %copy-done.4, f32[512,1024]{1,0:T(8,128)} %convolution_add_fusion.1.grad_ref, bf16[512,1024]{1,0:T(8,128)(2,1)} %add_convert_fusion.14.gate_ref, ...), custom_call_target="tpu_custom_call" | custom-call | flops 6710886400 | bytes 6291456 | tf_op jit(solution)/shard_map/scan_edge/pallas_call | solution.py:435
  175.1 27.2 %scan_forward.2 = (bf16[512,1024]{1,0:T(8,128)(2,1)}, bf16[512,1024]{1,0:T(8,128)(2,1)}, f32[512,16,8,128]{3,2,1,0:T(8,128)}, f32[512,128]{1,0:T(8,128)}, f32[1,1024]{1,0:T(1,128)}) custom-call(f32[512,1024]{1,0:T(8,128)} %compare_select_fusion.1.size_ref, bf16[512,1024]{1,0:T(8,128)(2,1)} %copy-done.4, f32[512,1024]{1,0:T(8,128)} %convolution_add_fusion.1.grad_ref, ...), custom_call_target="tpu_custom_call" | custom-call | flops 12582912000 | bytes 41943040 | tf_op jit(solution)/shard_map/scan_forward/pallas_call | solution.py:459
  209.1 4.6 add_convert_fusion.13.gate_ref
  218.3 11.4 %scan_edge.3 = f32[16,8,128]{2,1,0:T(8,128)} custom-call(s32[1]{0:T(128)} %bitcast.21.flag, f32[512,1024]{1,0:T(8,128)} %compare_select_fusion.size_ref, bf16[512,1024]{1,0:T(8,128)(2,1)} %copy-done.6, f32[512,1024]{1,0:T(8,128)} %convolution_add_fusion.grad_ref, bf16[512,1024]{1,0:T(8,128)(2,1)} %add_convert_fusion.13.gate_ref, f32[512,32]{1,0:T(8,128)} %slice.540.coef_ref, ...), custom_call_target="tpu_custom_call" | custom-call | flops 6710886400 | bytes 6291456 | tf_op jit(solution)/shard_map/scan_edge/pallas_call | solution.py:435
  232.1 26.8 %scan_forward.3 = (bf16[512,1024]{1,0:T(8,128)(2,1)}, bf16[512,1024]{1,0:T(8,128)(2,1)}, f32[512,16,8,128]{3,2,1,0:T(8,128)}, f32[512,128]{1,0:T(8,128)}, f32[1,1024]{1,0:T(1,128)}) custom-call(f32[512,1024]{1,0:T(8,128)} %compare_select_fusion.size_ref, bf16[512,1024]{1,0:T(8,128)(2,1)} %copy-done.6, f32[512,1024]{1,0:T(8,128)} %convolution_add_fusion.grad_ref, ...), custom_call_target="tpu_custom_call" | custom-call | flops 12582912000 | bytes 41943040 | tf_op jit(solution)/shard_map/scan_forward/pallas_call | solution.py:459
  268.8 33.9 %scan_backward.2 = (bf16[512,1024]{1,0:T(8,128)(2,1)}, f32[512,1024]{1,0:T(8,128)}, f32[512,128]{1,0:T(8,128)}, f32[16,8,128]{2,1,0:T(8,128)}, f32[1,1024]{1,0:T(1,128)}) custom-call(f32[512,1024]{1,0:T(8,128)} %compare_select_fusion.1.size_ref, bf16[512,1024]{1,0:T(8,128)(2,1)} %copy-done.4, f32[512,1024]{1,0:T(8,128)} %convolution_add_fusion.1.grad_ref, ...), custom_call_target="tpu_custom_call" | custom-call | flops 16777216000 | bytes 41943040 | tf_op jit(solution)/shard_map/scan_backward/pallas_call | solution.py:501
  318.7 4.7 fusion.109
  363.3 8.7 %collective-permute-done.23 = bf16[512,160]{1,0:T(8,128)(2,1)} collective-permute-done((bf16[512,160]{1,0:T(8,128)(2,1)}, bf16[512,160]{1,0:T(8,128)(2,1)}, u32[]{:S(2)}, u32[]{:S(2)}) %collective-permute-start.23) | collective-permute-done | bytes 163872 | tf_op jit(solution)/shard_map/ppermute | solution.py:38
  376.5 7.4 %conv_backward.2 = (bf16[512,1024]{1,0:T(8,128)(2,1)}, f32[8,1024]{1,0:T(8,128)}, f32[8,1024]{1,0:T(8,128)}, f32[8,1024]{1,0:T(8,128)}) custom-call(f32[512,1024]{1,0:T(8,128)} %get-tuple-element.125.value_grad_ref, bf16[512,160]{1,0:T(8,128)(2,1)} %add_convert_fusion.19.proj_ref, bf16[160,1024]{1,0:T(8,128)(2,1)} %copy-done.14, ...), custom_call_target="tpu_custom_call" | custom-call | tf_op jit(solution)/shard_map/conv_backward/pallas_call | solution.py:739
  395.5 33.3 %scan_backward.3 = (bf16[512,1024]{1,0:T(8,128)(2,1)}, f32[512,1024]{1,0:T(8,128)}, f32[512,128]{1,0:T(8,128)}, f32[16,8,128]{2,1,0:T(8,128)}, f32[1,1024]{1,0:T(1,128)}) custom-call(f32[512,1024]{1,0:T(8,128)} %compare_select_fusion.size_ref, bf16[512,1024]{1,0:T(8,128)(2,1)} %copy-done.6, f32[512,1024]{1,0:T(8,128)} %convolution_add_fusion.grad_ref, ...), custom_call_target="tpu_custom_call" | custom-call | flops 16777216000 | bytes 41943040 | tf_op jit(solution)/shard_map/scan_backward/pallas_call | solution.py:501
  457.8 27.9 %collective-permute-done.26 = bf16[512,160]{1,0:T(8,128)(2,1)S(1)} collective-permute-done((bf16[512,160]{1,0:T(8,128)(2,1)S(1)}, bf16[512,160]{1,0:T(8,128)(2,1)S(1)}, u32[]{:S(2)}, u32[]{:S(2)}) %collective-permute-start.26) | collective-permute-done | bytes 163872 | tf_op jit(solution)/shard_map/ppermute | solution.py:38
  491.5 4.9 add_convert_fusion.1
  499.8 7.3 %conv_backward.3 = (bf16[512,1024]{1,0:T(8,128)(2,1)}, f32[8,1024]{1,0:T(8,128)}, f32[8,1024]{1,0:T(8,128)}, f32[8,1024]{1,0:T(8,128)}) custom-call(f32[512,1024]{1,0:T(8,128)} %get-tuple-element.144.value_grad_ref, bf16[512,160]{1,0:T(8,128)(2,1)} %copy-done.48, bf16[160,1024]{1,0:T(8,128)(2,1)} %copy-done.14, bf16[512,1024]{1,0:T(8,128)(2,1)} %copy-done.19, ...), custom_call_target="tpu_custom_call" | custom-call | tf_op jit(solution)/shard_map/conv_backward/pallas_call | solution.py:739
  542.7 5.8 collective-permute-done.39
  551.2 8.6 %collective-permute-done.34 = bf16[2,256,512]{2,1,0:T(8,128)(2,1)S(1)} collective-permute-done((bf16[2,256,512]{2,1,0:T(8,128)(2,1)S(1)}, bf16[2,256,512]{2,1,0:T(8,128)(2,1)S(1)}, u32[]{:S(2)}, u32[]{:S(2)}) %collective-permute-start.34) | collective-permute-done | bytes 524320 | tf_op jit(solution)/shard_map/ppermute | solution.py:38
  632.1 4.6 collective-permute-done.29
  667.9 4.6 maximum_bitcast_fusion.1
  (661 shorter events, 375.4 us)
Async XLA Ops:
  7.2 258.8 %reduce-scatter.5.cloned.1.call-start = ((), (), s32[]{:S(2)}) async-start(), calls=%async_computation.4 | async-start | bytes 2621440 | tf_op jit(solution)/shard_map/reduce_scatter | solution.py:130
  32.3 22.9 %collective-permute-start.15 = (bf16[256,1024]{1,0:T(8,128)(2,1)S(1)}, bf16[256,1024]{1,0:T(8,128)(2,1)}, u32[]{:S(2)}, u32[]{:S(2)}) collective-permute-start(bf16[256,1024]{1,0:T(8,128)(2,1)S(1)} %get-tuple-element.107), channel_id=1, source_target_pairs={{0,16},{8,24},{16,0},{24,8},{1,17},{9,25},{17,1},{25,9},{2,18},{10... | collective-permute-start | bytes 1572872 | tf_op jit(solution)/shard_map/ppermute | solution.py:38
  32.9 20.0 %collective-permute-start.14 = (bf16[256,1024]{1,0:T(8,128)(2,1)S(1)}, bf16[256,1024]{1,0:T(8,128)(2,1)}, u32[]{:S(2)}, u32[]{:S(2)}) collective-permute-start(bf16[256,1024]{1,0:T(8,128)(2,1)S(1)} %get-tuple-element.107), channel_id=1, source_target_pairs={{0,8},{8,0},{16,24},{24,16},{1,9},{9,1},{17,25},{25,17},{2,10},{10... | collective-permute-start | bytes 1572872 | tf_op jit(solution)/shard_map/ppermute | solution.py:38
  42.9 29.9 %collective-permute-start.5 = (bf16[1024,1024]{1,0:T(8,128)(2,1)}, bf16[1024,1024]{1,0:T(8,128)(2,1)}, u32[]{:S(2)}, u32[]{:S(2)}) collective-permute-start(bf16[1024,1024]{1,0:T(8,128)(2,1)} %fusion.8), channel_id=1, source_target_pairs={{0,4},{4,0},{1,5},{5,1},{2,6},{6,2},{3,7},{7,3},{8,12},{12,8},{9,1... | collective-permute-start | bytes 6291464 | tf_op jit(solution)/shard_map/ppermute | solution.py:38
  50.5 51.9 %collective-permute-start.9 = (bf16[256,1024]{1,0:T(8,128)(2,1)}, bf16[256,1024]{1,0:T(8,128)(2,1)}, u32[]{:S(2)}, u32[]{:S(2)}) collective-permute-start(bf16[256,1024]{1,0:T(8,128)(2,1)} %convert_element_type.407), channel_id=1, source_target_pairs={{0,8},{8,0},{16,24},{24,16},{1,9},{9,1},{17,25},{25,17},{2,10},{10... | collective-permute-start | bytes 1572872 | tf_op jit(solution)/shard_map/ppermute | solution.py:38
  52.9 56.6 %collective-permute-start.10 = (bf16[256,1024]{1,0:T(8,128)(2,1)}, bf16[256,1024]{1,0:T(8,128)(2,1)}, u32[]{:S(2)}, u32[]{:S(2)}) collective-permute-start(bf16[256,1024]{1,0:T(8,128)(2,1)} %convert_element_type.407), channel_id=1, source_target_pairs={{0,16},{8,24},{16,0},{24,8},{1,17},{9,25},{17,1},{25,9},{2,18},{10... | collective-permute-start | bytes 1572872 | tf_op jit(solution)/shard_map/ppermute | solution.py:38
  101.7 44.4 %collective-permute-start.17 = (bf16[1024,1024]{1,0:T(8,128)(2,1)}, bf16[1024,1024]{1,0:T(8,128)(2,1)}, u32[]{:S(2)}, u32[]{:S(2)}) collective-permute-start(bf16[1024,1024]{1,0:T(8,128)(2,1)} %constant_dynamic-update-slice_fusion.4), channel_id=1, source_target_pairs={{0,4},{4,0},{1,5},{5,1},{2,6},{6,2},{3,7},{7,3},{8,12},{12,8},{9,1... | collective-permute-start | bytes 6291464 | tf_op jit(solution)/shard_map/ppermute | solution.py:38
  114.5 20.0 %collective-permute-start.8 = (bf16[512,160]{1,0:T(8,128)(2,1)S(1)}, bf16[512,160]{1,0:T(8,128)(2,1)S(1)}, u32[]{:S(2)}, u32[]{:S(2)}) collective-permute-start(bf16[512,160]{1,0:T(8,128)(2,1)S(1)} %add_convert_fusion.22), channel_id=1, source_target_pairs={{0,2},{1,3},{2,0},{3,1},{4,6},{5,7},{6,4},{7,5},{8,10},{9,11},{10,... | collective-permute-start | bytes 491528 | tf_op jit(solution)/shard_map/ppermute | solution.py:38
  118.0 35.0 %collective-permute-start.13 = (bf16[1024,1024]{1,0:T(8,128)(2,1)}, bf16[1024,1024]{1,0:T(8,128)(2,1)S(1)}, u32[]{:S(2)}, u32[]{:S(2)}) collective-permute-start(bf16[1024,1024]{1,0:T(8,128)(2,1)} %constant_dynamic-update-slice_fusion), channel_id=1, source_target_pairs={{0,4},{4,0},{1,5},{5,1},{2,6},{6,2},{3,7},{7,3},{8,12},{12,8},{9,1... | collective-permute-start | bytes 6291464 | tf_op jit(solution)/shard_map/ppermute | solution.py:38
  207.9 152.5 %reduce-scatter.7.cloned.1.call-start = ((), (), s32[]{:S(2)}) async-start(), calls=%async_computation.6 | async-start | bytes 2621440 | tf_op jit(solution)/shard_map/reduce_scatter | solution.py:130
  264.3 112.2 %all-gather.5.cloned.1.call-start = ((), (), s32[]{:S(2)}) async-start(), calls=%async_computation.5 | async-start | bytes 2621440 | tf_op jit(solution)/shard_map/all_gather | solution.py:134
  311.2 22.3 %collective-permute-start.48 = (bf16[1024,1024]{1,0:T(8,128)(2,1)}, bf16[1024,1024]{1,0:T(8,128)(2,1)}, u32[]{:S(2)}, u32[]{:S(2)}) collective-permute-start(bf16[1024,1024]{1,0:T(8,128)(2,1)} %add_convert_fusion.7), channel_id=1, source_target_pairs={{0,4},{4,0},{1,5},{5,1},{2,6},{6,2},{3,7},{7,3},{8,12},{12,8},{9,1... | collective-permute-start | bytes 6291464 | tf_op jit(solution)/shard_map/ppermute | solution.py:38
  314.5 32.6 %collective-permute-start.22 = (bf16[512,160]{1,0:T(8,128)(2,1)}, bf16[512,160]{1,0:T(8,128)(2,1)}, u32[]{:S(2)}, u32[]{:S(2)}) collective-permute-start(bf16[512,160]{1,0:T(8,128)(2,1)} %pad_maximum_fusion.7), channel_id=1, source_target_pairs={{0,1},{1,0},{2,3},{3,2},{4,5},{5,4},{6,7},{7,6},{8,9},{9,8},{10,11... | collective-permute-start | bytes 491528 | tf_op jit(solution)/shard_map/ppermute | solution.py:38
  315.5 116.4 %all-gather.7.cloned.1.call-start = ((), (), s32[]{:S(2)}) async-start(), calls=%async_computation.7 | async-start | bytes 2621440 | tf_op jit(solution)/shard_map/all_gather | solution.py:134
  349.1 22.9 %collective-permute-start.23 = (bf16[512,160]{1,0:T(8,128)(2,1)}, bf16[512,160]{1,0:T(8,128)(2,1)}, u32[]{:S(2)}, u32[]{:S(2)}) collective-permute-start(bf16[512,160]{1,0:T(8,128)(2,1)} %add_convert_fusion.20), channel_id=1, source_target_pairs={{0,2},{1,3},{2,0},{3,1},{4,6},{5,7},{6,4},{7,5},{8,10},{9,11},{10,... | collective-permute-start | bytes 491528 | tf_op jit(solution)/shard_map/ppermute | solution.py:38
  363.3 133.1 %reduce-scatter.9.cloned.1.call-start = ((), (), s32[]{:S(2)}) async-start(), calls=%async_computation.8 | async-start | bytes 2621440 | tf_op jit(solution)/shard_map/reduce_scatter | solution.py:130
  434.7 19.2 %collective-permute-start.25 = (bf16[512,160]{1,0:T(8,128)(2,1)S(1)}, bf16[512,160]{1,0:T(8,128)(2,1)}, u32[]{:S(2)}, u32[]{:S(2)}) collective-permute-start(bf16[512,160]{1,0:T(8,128)(2,1)S(1)} %pad_maximum_fusion.8), channel_id=1, source_target_pairs={{0,1},{1,0},{2,3},{3,2},{4,5},{5,4},{6,7},{7,6},{8,9},{9,8},{10,11... | collective-permute-start | bytes 491528 | tf_op jit(solution)/shard_map/ppermute | solution.py:38
  434.8 179.9 %reduce-scatter.11.cloned.1.call-start = ((), (), s32[]{:S(2)}) async-start(), calls=%async_computation.10 | async-start | bytes 2621440 | tf_op jit(solution)/shard_map/reduce_scatter | solution.py:130
  440.6 51.0 %collective-permute-start.38 = (bf16[1024,1024]{1,0:T(8,128)(2,1)}, bf16[1024,1024]{1,0:T(8,128)(2,1)}, u32[]{:S(2)}, u32[]{:S(2)}) collective-permute-start(bf16[1024,1024]{1,0:T(8,128)(2,1)} %add_convert_fusion.5), channel_id=1, source_target_pairs={{0,4},{4,0},{1,5},{5,1},{2,6},{6,2},{3,7},{7,3},{8,12},{12,8},{9,1... | collective-permute-start | bytes 6291464 | tf_op jit(solution)/shard_map/ppermute | solution.py:38
  455.1 30.7 %collective-permute-start.26 = (bf16[512,160]{1,0:T(8,128)(2,1)S(1)}, bf16[512,160]{1,0:T(8,128)(2,1)S(1)}, u32[]{:S(2)}, u32[]{:S(2)}) collective-permute-start(bf16[512,160]{1,0:T(8,128)(2,1)S(1)} %add_convert_fusion.18), channel_id=1, source_target_pairs={{0,2},{1,3},{2,0},{3,1},{4,6},{5,7},{6,4},{7,5},{8,10},{9,11},{10,... | collective-permute-start | bytes 491528 | tf_op jit(solution)/shard_map/ppermute | solution.py:38
  519.7 148.2 %all-gather.9.cloned.1.call-start = ((), (), s32[]{:S(2)}) async-start(), calls=%async_computation.9 | async-start | bytes 2621440 | tf_op jit(solution)/shard_map/all_gather | solution.py:134
  539.3 20.4 %collective-permute-start.34 = (bf16[2,256,512]{2,1,0:T(8,128)(2,1)S(1)}, bf16[2,256,512]{2,1,0:T(8,128)(2,1)S(1)}, u32[]{:S(2)}, u32[]{:S(2)}) collective-permute-start(bf16[2,256,512]{2,1,0:T(8,128)(2,1)S(1)} %pad_maximum_fusion.9), channel_id=1, source_target_pairs={{0,8},{8,0},{16,24},{24,16},{1,9},{9,1},{17,25},{25,17},{2,10},{10... | collective-permute-start | bytes 1572872 | tf_op jit(solution)/shard_map/ppermute | solution.py:38
  539.9 21.0 %collective-permute-start.36 = (bf16[2,256,512]{2,1,0:T(8,128)(2,1)S(1)}, bf16[2,256,512]{2,1,0:T(8,128)(2,1)S(1)}, u32[]{:S(2)}, u32[]{:S(2)}) collective-permute-start(bf16[2,256,512]{2,1,0:T(8,128)(2,1)S(1)} %slice.548), channel_id=1, source_target_pairs={{0,16},{8,24},{16,0},{24,8},{1,17},{9,25},{17,1},{25,9},{2,18},{10... | collective-permute-start | bytes 1572872 | tf_op jit(solution)/shard_map/ppermute | solution.py:38
  566.9 101.0 %all-gather.11.cloned.1.call-start = ((), (), s32[]{:S(2)}) async-start(), calls=%async_computation.11 | async-start | bytes 2621440 | tf_op jit(solution)/shard_map/all_gather | solution.py:134
  (185 other events, 2031.8 us)
Sparse Core Ops, SparseCore 0:
  208.0 43.6 reduce-scatter.4
  264.4 44.0 reduce-scatter.6
  315.7 54.9 all-gather.4
  372.1 44.8 all-gather.6
  434.9 50.7 reduce-scatter.8
  519.8 43.2 reduce-scatter.10
  567.0 43.7 all-gather.8
  618.3 43.8 all-gather.10

commit v3 on v2

--- a/solution.py
+++ b/solution.py
@@ -3,6 +3,7 @@
 
 import jax
 import jax.numpy as jnp
+import numpy as np
 from jax import lax
 from jax.experimental import pallas as pl
 from jax.experimental.pallas import tpu as pltpu
@@ -29,6 +30,15 @@
     return lax.optimization_barrier((value,) + others)[0]
 
 
+def after_all(values, *others):
+    return list(lax.optimization_barrier(tuple(values) + others)[: len(values)])
+
+
+def vector(scalars):
+    place = lax.iota(jnp.int32, len(scalars))
+    return in_order([jnp.where(place == i, s, 0.0) for i, s in enumerate(scalars)])
+
+
 def bits(axis):
     size = lax.axis_size(axis)
     return [1 << b for b in range(size.bit_length() - 1)]
@@ -65,21 +75,21 @@
     return jnp.stack([lax.dynamic_index_in_dim(blocks, q, 0, False) for q in order])
 
 
-def fetch(own):
+def fetch(own, release_far=()):
     if lax.axis_size("dp") != 4:
         blocks = [own]
         for bit in bits("dp"):
             blocks = blocks + [swap(block, "dp", bit) for block in blocks]
-        return blocks, blocks[1:]
+        return blocks
     half = own.shape[0] // 2
-    one, two = swap(own, "dp", 1), swap(own, "dp", 2)
-    three = jnp.concatenate([swap(two[:half], "dp", 1), swap(one[half:], "dp", 2)], axis=0)
-    return [own, one, two, three], [one, two]
+    one, two = after_all([swap(own, "dp", 1), swap(own, "dp", 2)], *release_far)
+    far = [swap(two[:half], "dp", 1), swap(one[half:], "dp", 2)]
+    return [own, one, two, jnp.concatenate(far, axis=0)]
 
 
 def fetch_two(left, right, release_far, release_all):
     if lax.axis_size("dp") != 4:
-        return fetch(left)[0], fetch(right)[0]
+        return fetch(left), fetch(right)
     left_one, left_two = swap(left, "dp", 1), swap(left, "dp", 2)
     right_one, right_two = swap(right, "dp", 1), swap(right, "dp", 2)
     left_far = swap(after(left_two, release_far), "dp", 1)
@@ -95,20 +105,24 @@
     return chunks
 
 
-def scatter(chunks):
+def scatter(chunks, release=()):
     for bit in reversed(bits("ctx")):
         half = len(chunks) // 2
         chunks = [
             (keep.astype(FULL) + swap(send, "ctx", bit).astype(FULL)).astype(LOW)
             for keep, send in zip(chunks[:half], chunks[half:])
         ]
+    return scatter_dp(chunks[0], release), chunks[0]
+
+
+def scatter_dp(chunk, release):
     n_dp = lax.axis_size("dp")
-    parts = chunks[0].reshape(n_dp, -1, chunks[0].shape[-1])
+    parts = chunk.reshape(n_dp, -1, chunk.shape[-1])
     if n_dp == 4:
         half = parts.shape[2] // 2
         left, right = parts[:, :, :half], parts[:, :, half:]
-        got_left = swap(jnp.stack([left[1], left[3]]), "dp", 1).astype(FULL)
-        got_right = swap(right[2:], "dp", 2).astype(FULL)
+        got = [swap(jnp.stack([left[1], left[3]]), "dp", 1), swap(right[2:], "dp", 2)]
+        got_left, got_right = (g.astype(FULL) for g in after_all(got, *release))
         far_left = (left[2].astype(FULL) + got_left[1]).astype(LOW)
         far_right = (right[1].astype(FULL) + got_right[1]).astype(LOW)
         end_left = swap(far_left, "dp", 2).astype(FULL)
@@ -135,17 +149,28 @@
 
 
 def tensor_total(term):
+    return tensor_steps(term)[-2]
+
+
+def tensor_steps(term):
+    steps, sent = [], []
     for bit in bits("tensor"):
         low = term.astype(LOW)
         term = low.astype(FULL) + swap(low, "tensor", bit).astype(FULL)
-    return term
+        steps.append(term)
+        sent.append(low)
+    return steps + sent[:1]
 
 
 def gather_few(row):
+    return pick(gather_relative(row), relative_blocks()[1])
+
+
+def gather_relative(row):
     for axis in ("dp", "ctx"):
         for bit in bits(axis):
             row = jnp.concatenate([row, swap(row, axis, bit)], axis=0)
-    return pick(row, relative_blocks()[1])
+    return row
 
 
 def in_order(parts):
@@ -153,19 +178,6 @@
     for part in parts[1:]:
         total = total + part
     return total
-
-
-def few_total(value, axes):
-    for axis in axes:
-        n, me = lax.axis_size(axis), lax.axis_index(axis)
-        if n == 2:
-            value = value + swap(value, axis, 1)
-            continue
-        parts = jnp.stack([value] + [
-            lax.ppermute(value, axis, [(i, i ^ k) for i in range(n)]) for k in range(1, n)
-        ])
-        value = in_order([lax.dynamic_index_in_dim(parts, me ^ k, 0, False) for k in range(n)])
-    return value
 
 
 def spread(target, columns, place, rows, tile):
@@ -246,13 +258,14 @@
 
 def forward_kernel(
     rows, groups, tile, part, unroll,
-    size_ref, value_ref, grad_ref, gate_ref, coef_ref, rate_ref, start_ref, skip_ref, pick_ref,
+    size_ref, value_ref, grad_ref, gate_ref, coef_ref, rate_ref, start_ref, skip_ref,
     gated_ref, gate_grad_ref, before_ref, grad_c_ref, grad_skip_ref,
-    size_s, input_s, grad_s, out_s, b_s, c_s, product_s, state_s,
+    size_s, input_s, grad_s, out_s, b_s, c_s, product_s, state_s, pick_s,
 ):
     @pl.when(pl.program_id(0) == 0)
     def _():
         state_s[...] = start_ref[...]
+        set_picker(pick_s)
         grad_skip_ref[...] = jnp.zeros_like(grad_skip_ref)
 
     blank = jnp.zeros((rows, LANES), FULL)
@@ -309,20 +322,21 @@
         gated_ref[:, cut] = (scan_out * (gate * sigma)).astype(LOW)
         slope = sigma * (1.0 + gate * (1.0 - sigma))
         gate_grad_ref[:, cut] = (grad_ref[:, cut] * scan_out * slope).astype(LOW)
-    sums = jnp.dot(product_s[...].astype(LOW), pick_ref[...], preferred_element_type=FULL)
+    sums = jnp.dot(product_s[...].astype(LOW), pick_s[...], preferred_element_type=FULL)
     grad_c_ref[...] = jnp.sum(sums.reshape(rows, tile, LANES), axis=1)
 
 
 def backward_kernel(
     rows, groups, tile, part, unroll,
-    size_ref, value_ref, grad_ref, gate_ref, coef_ref, rate_ref, tail_ref, skip_ref, pick_ref,
+    size_ref, value_ref, grad_ref, gate_ref, coef_ref, rate_ref, tail_ref, skip_ref,
     before_ref,
     pre_low_ref, grad_value_ref, grad_b_ref, grad_rate_ref, grad_bias_ref,
-    size_s, input_s, grad_s, along_s, rated_s, b_s, c_s, product_s, state_s,
+    size_s, input_s, grad_s, along_s, rated_s, b_s, c_s, product_s, state_s, pick_s,
 ):
     @pl.when(pl.program_id(0) == 0)
     def _():
         state_s[...] = tail_ref[...]
+        set_picker(pick_s)
         grad_rate_ref[...] = jnp.zeros_like(grad_rate_ref)
         grad_bias_ref[...] = jnp.zeros_like(grad_bias_ref)
 
@@ -385,14 +399,13 @@
         grad_bias_ref[:, cut] += jnp.sum(grad_pre, axis=0, keepdims=True)
         scan_grad = grad_s[pl.ds(j, rows, stride=tile), :]
         grad_value_ref[:, cut] = along * size + skip_ref[:, cut] * scan_grad
-    sums = jnp.dot(product_s[...].astype(LOW), pick_ref[...], preferred_element_type=FULL)
+    sums = jnp.dot(product_s[...].astype(LOW), pick_s[...], preferred_element_type=FULL)
     grad_b_ref[...] = jnp.sum(sums.reshape(rows, tile, LANES), axis=1)
 
 
-def picker():
-    shape = (N * LANES, LANES)
-    state = lax.broadcasted_iota(jnp.int32, shape, 0) // LANES
-    return (state == lax.broadcasted_iota(jnp.int32, shape, 1)).astype(LOW)
+def set_picker(pick_s):
+    state = lax.broadcasted_iota(jnp.int32, pick_s.shape, 0) // LANES
+    pick_s[...] = (state == lax.broadcasted_iota(jnp.int32, pick_s.shape, 1)).astype(LOW)
 
 
 def tiles(channels):
@@ -465,7 +478,6 @@
             cube,
             cube,
             row,
-            pl.BlockSpec((N * LANES, LANES), lambda i: (0, 0)),
         ],
         out_specs=[
             wide,
@@ -483,11 +495,12 @@
         ],
         scratch_shapes=[pltpu.VMEM((rows * tile, LANES), FULL)] * 4
         + [pltpu.VMEM((rows * N, LANES), FULL)] * 2
-        + [pltpu.VMEM((rows * tile, N * LANES), FULL), pltpu.VMEM((N, tile, LANES), FULL)],
+        + [pltpu.VMEM((rows * tile, N * LANES), FULL), pltpu.VMEM((N, tile, LANES), FULL)]
+        + [pltpu.VMEM((N * LANES, LANES), LOW)],
         compiler_params=limits(),
         cost_estimate=cost(1, length, 15, size.size * 80),
         name="scan_forward",
-    )(size, value, grad, gate, coef, rate, start, skip, picker())
+    )(size, value, grad, gate, coef, rate, start, skip)
 
 
 def scan_backward(size, value, grad, gate, coef, rate, tail, skip, before):
@@ -507,7 +520,6 @@
             cube,
             cube,
             row,
-            pl.BlockSpec((N * LANES, LANES), lambda i: (0, 0)),
             pl.BlockSpec((rows, N, tile, LANES), lambda i: (last - i, 0, 0, 0)),
         ],
         out_specs=[wide, wide, pl.BlockSpec((rows, LANES), lambda i: (last - i, 0)), cube, row],
@@ -520,11 +532,12 @@
         ],
         scratch_shapes=[pltpu.VMEM((rows * tile, LANES), FULL)] * 5
         + [pltpu.VMEM((rows * N, LANES), FULL)] * 2
-        + [pltpu.VMEM((rows * tile, N * LANES), FULL), pltpu.VMEM((N, tile, LANES), FULL)],
+        + [pltpu.VMEM((rows * tile, N * LANES), FULL), pltpu.VMEM((N, tile, LANES), FULL)]
+        + [pltpu.VMEM((N * LANES, LANES), LOW)],
         compiler_params=limits(),
         cost_estimate=cost(1, length, 20, size.size * 80),
         name="scan_backward",
-    )(size, value, grad, gate, coef, rate, tail, skip, picker(), before)
+    )(size, value, grad, gate, coef, rate, tail, skip, before)
 
 
 def edges(size, value, grad, gate, coef, rate):
@@ -690,6 +703,69 @@
         compiler_params=limits(),
         name="token_rows",
     )(jnp.stack(order + [block]).astype(jnp.int32), x, grad, gain, normed)
+
+
+def update_kernel(owners, *refs):
+    n = len(owners)
+    grads, scales, cols_ref, table_ref, out_ref = refs[:n], refs[n : 2 * n], *refs[2 * n :]
+    out_ref[...] = jnp.zeros_like(out_ref)
+
+    def lanes(squares):
+        total = jnp.sum(squares, axis=0, keepdims=True)
+        cuts = [total[:, columns_of(j)] for j in range(total.shape[1] // LANES)]
+        return in_order(cuts)
+
+    for i, owner in enumerate(owners):
+        update = grads[i][...] * scales[i][...] * cols_ref[i : i + 1, :]
+        out_ref[owner : owner + 1, :] += lanes(update * update)
+    out_ref[5:6, :] = lanes(table_ref[...] * table_ref[...])
+
+
+def update_squares(grads, scales, cols, table):
+    return pl.pallas_call(
+        functools.partial(update_kernel, (1, 1, 2, 3, 4)),
+        out_shape=jax.ShapeDtypeStruct((6, LANES), FULL),
+        compiler_params=limits(),
+        name="update_squares",
+    )(*grads, *scales, cols, table)
+
+
+def pick_kernel(order, blocks_ref, out_ref):
+    for j in range(blocks_ref.shape[0]):
+        out_ref[j] = blocks_ref[order[j]]
+
+
+def pick_rows(blocks, order):
+    return pl.pallas_call(
+        pick_kernel,
+        in_specs=[pl.BlockSpec(memory_space=pltpu.SMEM), pl.BlockSpec(memory_space=pltpu.VMEM)],
+        out_specs=pl.BlockSpec(memory_space=pltpu.VMEM),
+        out_shape=jax.ShapeDtypeStruct(blocks.shape, blocks.dtype),
+        compiler_params=limits(),
+        name="pick_rows",
+    )(jnp.stack(order).astype(jnp.int32), blocks)
+
+
+def fill_kernel(part_ref, *refs):
+    refs[-1][...] = part_ref[...]
+
+
+def fill(whole, count, m, part):
+    height, columns = part.shape
+    rows = min(256, height)
+    spec = pl.BlockSpec((None, rows, columns), lambda i: (m, i, 0))
+    kept = [] if whole is None else [whole]
+    return pl.pallas_call(
+        fill_kernel,
+        grid=(height // rows,),
+        in_specs=[pl.BlockSpec((rows, columns), lambda i: (i, 0))]
+        + [pl.BlockSpec(memory_space=pl.ANY)] * len(kept),
+        out_specs=spec,
+        out_shape=jax.ShapeDtypeStruct((count, height, columns), part.dtype),
+        input_output_aliases={1: 0} if kept else {},
+        compiler_params=limits(),
+        name="fill",
+    )(part, *kept)
 
 
 def conv_kernel(
@@ -791,22 +867,33 @@
     me = lax.axis_index("tensor")
 
     n_x, n_s = xproj_weight.shape[0], step_weight.shape[0]
-    gain_row = jnp.pad(norm_gain.astype(LOW), (0, inner - owned))[None]
+    every = range(micro)
+    tokens_flat = tokens.reshape(micro * length, D)
+    grad_flat = out_grad.reshape(micro * length, D)
+    gain_rounded = after(norm_gain.astype(LOW), gain_second).astype(FULL)
+    gain_row = jnp.stack([gain_rounded, gain_second])[None]
+    for bit in bits("dp"):
+        gain_row = jnp.concatenate([gain_row, swap(gain_row, "dp", bit)], axis=0)
+    gain_low = gain_row
+    for bit in bits("ctx"):
+        gain_low = jnp.concatenate([gain_low, swap(gain_low, "ctx", bit)], axis=0)
+    gain_low, second_low = gain_low[:, 0], gain_low[:, 1]
+    normed, grad_rel = zip(
+        *(normalize(order, m, length, tokens_flat, grad_flat, gain_low, n_ctx) for m in every)
+    )
+    normed, grad_rel = list(normed), list(grad_rel)
     in_own = in_weight.reshape(owned, 2 * inner).astype(LOW)
-    first_own = [in_own[:, :inner], xproj_weight.astype(LOW), step_weight.astype(LOW), gain_row]
-    pad_rows = -(owned + n_x + n_s + 1) % 64
+    first_own = [in_own[:, :inner], xproj_weight.astype(LOW), step_weight.astype(LOW)]
+    pad_rows = -(owned + n_x + n_s) % 64
     if pad_rows:
         first_own.append(jnp.zeros((pad_rows, inner), LOW))
-    blocks, arrived = fetch(jnp.concatenate(first_own, axis=0))
+    blocks = fetch(after(jnp.concatenate(first_own, axis=0), gain_row), [n[0] for n in normed])
+    conv_low = join([block[:owned] for block in blocks])
     small = jnp.concatenate(join([block[owned:] for block in blocks]), axis=0)
-    small = small.reshape(n_owner, -1, inner)
-    conv_low = join([block[:owned] for block in blocks])
-    gain_low = small[:, n_x + n_s, :owned].astype(FULL)
-    small = pick(small, inverse_order)
+    small = pick_rows(small.reshape(n_owner, -1, inner), inverse_order)
     xproj_low = small[:, :n_x].reshape(n_owner * n_x, inner)
     step_low = small[:, n_x : n_x + n_s].reshape(n_owner * n_s, inner)
-    gate_own = after(in_own[:, inner:], *arrived)
-    out_own = after(outproj_weight.astype(LOW), *arrived)
+    gate_own, out_own = in_own[:, inner:], outproj_weight.astype(LOW)
 
     taps = channel_table[:K]
     conv_bias = channel_table[K]
@@ -821,15 +908,10 @@
             total = total + dot(part, weight, ((1,), (0,)))
         return total
 
-    every = range(micro)
-    tokens_flat = tokens.reshape(micro * length, D)
-    grad_flat = out_grad.reshape(micro * length, D)
-    normed, grad_rel = zip(
-        *(normalize(order, m, length, tokens_flat, grad_flat, gain_low, n_ctx) for m in every)
-    )
-    conv_in = [contract(normed[m], conv_low).astype(LOW) for m in every]
-    earlier, values, part_proj = [], [], []
+    conv_in, earlier, values, part_proj, proj_steps = [], [], [], [], []
     for m in every:
+        parts = normed[m] if m == 0 else after_all(normed[m], proj_steps[-1][-1])
+        conv_in.append(contract(parts, conv_low).astype(LOW))
         earlier.append(shifted(conv_in[m][length - 8 :], "ctx", 1))
         padded = jnp.concatenate([earlier[m], conv_in[m]], axis=0).astype(FULL)
         conv = conv_bias + taps[0] * padded[9 - K : 9 - K + length]
@@ -837,20 +919,26 @@
             conv = conv + taps[k] * padded[9 - K + k : 9 - K + k + length]
         values.append(jax.nn.silu(conv).astype(LOW))
         part_proj.append(dot(values[m], xproj_low, ((1,), (1,))))
-    gate_blocks, out_blocks = fetch_two(gate_own, out_own, conv_in[0], part_proj)
+        proj_steps.append(tensor_steps(part_proj[m]))
+    gate_blocks, out_blocks = fetch_two(gate_own, out_own, conv_in[0], proj_steps[0][:1])
     gate_low, out_low = join(gate_blocks), join(out_blocks)
-    gate_in = [contract(normed[m], gate_low).astype(LOW) for m in every]
-    grad_gated, size, coef, rank_low = [], [], [], []
+    weights = (in_weight, xproj_weight, step_weight, outproj_weight)
+    all_weights = [norm_gain] + list(weights) + [channel_table]
+    shares = jnp.array([1.0 / n_tensor, 1.0, 1.0, 1.0, 1.0, 1.0 / n_owner], FULL)
+    gate_in, grad_gated, size, coef, rank_low, own_mixed, mixed = [], [], [], [], [], [], []
+    gated, gate_grad, before, grad_c, grad_skip, tail, branch = [], [], [], [], [], [], []
     for m in every:
-        proj = tensor_total(part_proj[m])
+        proj = proj_steps[m][-2]
         rank_low.append(proj[:, :R].astype(LOW))
         coef.append(proj[:, R:])
-        pre = dot(rank_low[m], step_low, ((1,), (0,))) + step_bias
+        now_low, now_rel, now_normed = rank_low[m], grad_rel[m], normed[m]
+        if m > 0:
+            now_low = after(now_low, branch[-1])
+            now_rel, now_normed = after_all(now_rel, branch[-1]), after_all(now_normed, branch[-1])
+        pre = dot(now_low, step_low, ((1,), (0,))) + step_bias
         size.append(jax.nn.softplus(pre))
-    gated, gate_grad, before, grad_c, grad_skip, tail, branch = [], [], [], [], [], [], []
-    for m in every:
-        weights_now = out_low if m == 0 else [after(w, branch[-1]) for w in out_low]
-        grad_gated.append(contract(grad_rel[m], weights_now))
+        gate_in.append(contract(now_normed, gate_low).astype(LOW))
+        grad_gated.append(contract(now_rel, out_low))
         args = (size[m], values[m], grad_gated[m], gate_in[m], coef[m], rate)
         entering, leaving = edges(*args)
         tail.append(leaving)
@@ -860,18 +948,7 @@
         branch.append(
             jnp.concatenate([dot(gated[m], w, ((1,), (1,)), LOW) for w in out_low], axis=1)
         )
-    own_mixed = [
-        mix(order, m * n_tensor + me, tokens_flat, line_scatter(branch[m])) for m in every
-    ]
-
-    mixed_list = [line_gather(own) for own in own_mixed]
-
-    def stacked(parts):
-        ends = ((0, micro - 1, 0), (0, 0, 0), (0, 0, 0))
-        whole = lax.pad(parts[0][None], jnp.zeros((), LOW), ends)
-        for m in range(1, micro):
-            whole = lax.dynamic_update_slice(whole, parts[m][None], (m, 0, 0))
-        return whole
+        own_mixed.append(mix(order, m * n_tensor + me, tokens_flat, line_scatter(branch[m])))
 
     def over_micros(left, right):
         total = dot(left[0], right[0], ((0,), (0,)))
@@ -882,71 +959,82 @@
     def chunks_of(parts):
         return list(zip(*parts))
 
-    conv_grads, proj_grads, gain_parts, tables, partial, pre_lows = [], [], [], [], [], []
-    part_out = part_gate = ()
-    tokens_out, before_next = [], []
-    mixed_ready = [own_mixed[0]]
+    backs, parts, steps_of, gate_parts, part_out = [], [], [], [], []
     for m in every:
-        leaving = after(tail[m], branch[-1], *mixed_ready, *before_next)
+        leaving = after(tail[m], branch[-1], own_mixed[0])
+        if m > 0:
+            leaving = after(leaving, steps_of[0][0], *part_out, *gate_parts[0], *own_mixed)
         pre_low, value_grad, grad_b, grad_rate, grad_bias = scan_backward(
             size[m], values[m], grad_gated[m], gate_in[m], coef[m], rate, leaving, skip, before[m]
         )
+        backs.append((pre_low, value_grad, grad_rate, grad_bias))
+        grad_rank = dot(pre_low, step_low, ((1,), (1,)))
+        parts.append(jnp.concatenate([grad_rank, grad_b[:, :N], grad_c[m][:, :N]], axis=1))
+        steps_of.append(tensor_steps(parts[m]))
+        if m == 0:
+            for side in chunks_of(grad_rel):
+                part_out.append(over_micros(after_all(side, parts[0]), gated).astype(LOW))
+            gate_grad_then = after(gate_grad[0], parts[0], *own_mixed)
+            gate_parts.append([dot(gate_grad_then, g, ((1,), (1,))) for g in gate_low])
+    mixed = [line_gather(own_mixed[0])]
+    pre_lows = [back[0] for back in backs]
+    conv_grads, proj_grads, gain_parts, tables, partial, tokens_out = [], [], [], [], [], []
+    part_gate = []
+    for m in every:
+        _, value_grad, grad_rate, grad_bias = backs[m]
+        proj_grad = steps_of[m][-2].astype(LOW)
+        proj_grads.append(proj_grad)
+        wait_for = [mixed[0], parts[-1]]
         if m > 0:
-            pre_low = after(pre_low, mixed_list[-1])
-        pre_lows.append(pre_low)
-        grad_rank = dot(pre_low, step_low, ((1,), (1,)))
-        part = jnp.concatenate([grad_rank, grad_b[:, :N], grad_c[m][:, :N]], axis=1)
-        proj_grad = tensor_total(part).astype(LOW)
-        proj_grads.append(proj_grad)
-        if m == 0:
-            gated_then = [after(gated[0], part)] + gated[1:]
-            part_out = [over_micros(g, gated_then).astype(LOW) for g in chunks_of(grad_rel)]
-            filler = part_out
-        else:
-            normed_then = [[after(n, part) for n in parts] for parts in normed]
+            started = [partial[0], steps_of[m][0]]
+            gate_grad_then = after(gate_grad[m], *started)
+            gate_parts.append([dot(gate_grad_then, g, ((1,), (1,))) for g in gate_low])
             if m == micro - 1:
-                part_gate = [
-                    over_micros(g, gate_grad).astype(LOW) for g in chunks_of(normed_then)
-                ]
-            filler = list(part_gate)
-        gate_grad_then = after(gate_grad[m], part)
-        gate_part = [dot(gate_grad_then, g, ((1,), (1,))) for g in gate_low]
+                for c, side in enumerate(chunks_of(normed)):
+                    arrived = started + steps_of[m][-2:-1] if c else started
+                    part_gate.append(over_micros(after_all(side, *arrived), gate_grad).astype(LOW))
+            wait_for = wait_for + gate_parts[m] + part_gate
         conv_grad, last, head, sums = conv_backward(
-            after(value_grad, *filler, *gate_part, *tokens_out, mixed_list[0]),
+            after(value_grad, *wait_for),
             proj_grad, xproj_low, conv_in[m], earlier[m], channel_table[:8],
         )
         last = last + shifted(head, "ctx", -1)
         conv_grad = lax.dynamic_update_slice(conv_grad, last.astype(LOW), (length - 8, 0))
+        if m == 0:
+            conv_grad = after(conv_grad, steps_of[-1][0])
         conv_grads.append(conv_grad)
         partial.append(
             jnp.concatenate(
                 [
                     (g + dot(conv_grad, c, ((1,), (1,)))).astype(LOW)
-                    for g, c in zip(gate_part, conv_low)
+                    for g, c in zip(gate_parts[m], conv_low)
                 ],
                 axis=1,
             )
         )
-        mixed_ready, before_next = own_mixed, [partial[m]]
-        partial[m] = after(partial[m], mixed_list[-1])
+        sent = after(partial[m], steps_of[-1][-2])
         token, gain_part = token_rows(
-            order, m * n_tensor + me, tokens_flat, grad_flat, gain_low, line_scatter(partial[m])
+            order, m * n_tensor + me, tokens_flat, grad_flat, gain_low, line_scatter(sent)
         )
         gain_parts.append(gain_part)
         tokens_out.append(token)
-        tables.append(
-            jnp.concatenate(
-                [sums[: K + 1], grad_bias, grad_skip[m], flat(grad_rate, inner) * a_neg], axis=0
-            )
-        )
-    normed_then = [[after(n, partial[-1]) for n in parts] for parts in normed]
+        rates = flat(grad_rate, inner) * a_neg
+        tables.append(jnp.concatenate([sums[: K + 1], grad_bias, grad_skip[m], rates], axis=0))
+    normed_then = [after_all(sides, partial[-1]) for sides in normed]
     part_conv = [over_micros(g, conv_grads).astype(LOW) for g in chunks_of(normed_then)]
-    shard_out = scatter(part_out)
-    shard_gate = scatter(part_gate)
-    shard_conv = scatter(part_conv)
-    token_grad = stacked([line_gather(token) for token in tokens_out])
+    shard_conv, middle = scatter(part_conv)
+    shard_out, _ = scatter(part_out, [middle])
+    shard_gate, _ = scatter(part_gate, [middle])
+    weight_sq = vector([jnp.sum(jnp.square(after(w, middle))) for w in all_weights]) * shares
+    mixed = mixed + [line_gather(after(own, partial[-1])) for own in own_mixed[1:]]
+    whole_mixed = token_grad = None
+    for m in every:
+        whole_mixed = fill(whole_mixed, micro, m, after(mixed[m], middle))
+        token_grad = fill(token_grad, micro, m, line_gather(tokens_out[m]))
+        token_first = token_grad if m == 0 else token_first
+    mixed = whole_mixed.reshape(tokens.shape)
     token_grad = token_grad.reshape(tokens.shape)
-    mixed = stacked(mixed_list).reshape(tokens.shape)
+    pre_lows, proj_grads = after_all(pre_lows, middle), after_all(proj_grads, middle)
     part_step = over_micros(rank_low, pre_lows)
     part_xproj = over_micros(proj_grads, values)
     part_small = jnp.concatenate(
@@ -954,20 +1042,13 @@
     )
     pad_rows = -(n_x + n_s) % 16
     part_small = jnp.pad(part_small, ((0, 0), (0, pad_rows), (0, 0))).astype(LOW)
-    shard_small = scatter(list(pick(part_small, order).reshape(n_ctx, -1, inner)))
+    shard_small, _ = scatter(list(pick_rows(part_small, order).reshape(n_ctx, -1, inner)))
     shard_xproj = shard_small[:n_x]
     shard_step = shard_small[n_x : n_x + n_s]
-    gain_grad = butterfly(in_order(gain_parts), ("tensor",) + own_axes)
-    owner = lax.axis_index("dp") * n_ctx + lax.axis_index("ctx")
-    shard_gain = lax.dynamic_index_in_dim(gain_grad, owner, 0, False)
     grad_table = in_order(tables)
 
     shard_in = jnp.stack([shard_conv, shard_gate], axis=1)
     matrices = (shard_in, shard_xproj, shard_step, shard_out)
-    weights = (in_weight, xproj_weight, step_weight, outproj_weight)
-    all_weights = [norm_gain] + list(weights) + [channel_table]
-    shares = jnp.array([1.0 / n_tensor, 1.0, 1.0, 1.0, 1.0, 1.0 / n_owner], FULL)
-    weight_sq = jnp.stack([jnp.sum(jnp.square(after(w, pre_lows[0]))) for w in all_weights]) * shares
     old_rows = (in_rows, xproj_rows, step_rows, out_rows)
     old_cols = (in_cols, xproj_cols, step_cols, out_cols)
     width_cols = (2 * E, E, E, E)
@@ -975,32 +1056,29 @@
     squares = [matrix * matrix + square_floor for matrix in matrices]
     row_parts = [jnp.sum(square.reshape(square.shape[0], -1), axis=1) for square in squares]
     col_parts = [jnp.sum(square, axis=0).reshape(-1, inner) for square in squares]
-    row_sums = few_total(jnp.concatenate(row_parts + [weight_sq]), ("tensor",))
-    ends = [0]
-    for part in row_parts + [weight_sq]:
-        ends.append(ends[-1] + part.shape[0])
-    row_sums = [row_sums[ends[i] : ends[i + 1]] for i in range(5)]
-    row_news = [
-        decay_rate * old_rows[i] + (1.0 - decay_rate) * row_sums[i] / width_cols[i]
-        for i in range(4)
-    ]
-    totals = jnp.stack([jnp.sum(row_new) for row_new in row_news])
-    scalars = few_total(jnp.concatenate([totals, row_sums[4]]), own_axes)
-    row_totals, total_weight = scalars[:4], scalars[4:]
-    summed = butterfly(jnp.concatenate(col_parts + [grad_table], axis=0), own_axes)
+    row_sums = butterfly(
+        jnp.concatenate(row_parts + [weight_sq, in_order(gain_parts).reshape(-1)]), ("tensor",)
+    )
+    heights = [part.shape[0] for part in row_parts]
+    ends = np.cumsum([0] + heights)
+    n_rows = int(ends[-1])
+    per_row = np.repeat((1.0 - decay_rate) / np.array(width_cols), heights).astype(np.float32)
+    row_all = decay_rate * jnp.concatenate(old_rows) + per_row * row_sums[:n_rows]
+    row_news = [row_all[ends[i] : ends[i + 1]] for i in range(4)]
+    segment = (np.arange(4)[:, None] == np.repeat(np.arange(4), heights)[None]).astype(np.float32)
+    gain_sums = row_sums[n_rows + 6 :].reshape(-1, inner)
+    n_gain = gain_sums.shape[0]
+    summed = butterfly(jnp.concatenate(col_parts + [gain_sums, grad_table], axis=0), own_axes)
+    gain_grad = summed[5 : 5 + n_gain].reshape(n_owner, owned)
+    owner = lax.axis_index("dp") * n_ctx + lax.axis_index("ctx")
+    shard_gain = lax.dynamic_index_in_dim(gain_grad, owner, 0, False)
     col_sums = [summed[0:2], summed[2], summed[3], summed[4]]
-    table_grad = summed[5:]
+    table_grad = summed[5 + n_gain :]
     col_news = [
         decay_rate * old_cols[i] + (1.0 - decay_rate) * col_sums[i] / width_rows[i]
         for i in range(4)
     ]
-    updates = []
-    for i in range(4):
-        row_mean = row_totals[i] / width_rows[i]
-        shape = (-1,) + (1,) * (matrices[i].ndim - 1)
-        second = row_news[i].reshape(shape) * col_news[i][None] / row_mean
-        updates.append(matrices[i] * lax.rsqrt(second))
-    every_second = decay_rate * gather_few(after(gain_second[None], pre_lows[0])) + (
+    every_second = decay_rate * pick(second_low, inverse_order) + (
         1.0 - decay_rate
     ) * (gain_grad * gain_grad + square_floor)
     every_update = gain_grad * lax.rsqrt(every_second)
@@ -1010,17 +1088,39 @@
         table_grad * table_grad + square_floor
     )
     table_update = table_grad * lax.rsqrt(new_table_second)
-    all_updates = [gain_update] + updates + [table_update]
-    update_sq = jnp.stack([jnp.sum(u * u) for u in all_updates[1:]]) * shares[1:]
-    total_update = few_total(update_sq, own_axes + ("tensor",))
-    gain_sq = jnp.sum(every_update * every_update)[None]
-    total_update = jnp.concatenate([gain_sq, total_update])
+    inverse_cols = lax.rsqrt(jnp.concatenate([col.reshape(-1, inner) for col in col_news], axis=0))
+    inverse_rows = lax.rsqrt(row_all)
+    scaled_sq = update_squares(
+        [shard_conv, shard_gate, shard_xproj, shard_step, shard_out],
+        [inverse_rows[ends[i] : ends[i + 1]][:, None] for i in (0, 0, 1, 2, 3)],
+        inverse_cols,
+        table_update,
+    )
+    sums = jnp.concatenate(
+        [
+            jnp.sum(scaled_sq, axis=1) * shares,
+            jnp.sum(segment * row_all[None], axis=1) / n_tensor,
+            row_sums[n_rows : n_rows + 6] / n_tensor,
+        ]
+    )
+    sums = butterfly(after(sums, token_first), own_axes + ("tensor",))
+    row_means = sums[6:10] / np.array(width_rows, np.float32)
+    total_weight = sums[10:]
+    gain_sq = jnp.sum(every_update * every_update)
     counts = jnp.array([D, 2 * D * E, (R + 2 * N) * E, R * E, D * E, (K + 3 + N) * E], FULL)
+    ones = jnp.ones((1,), FULL)
+    means = jnp.concatenate([ones, row_means, ones])
+    total_update = jnp.where(jnp.arange(6) == 0, gain_sq, sums[:6] * means)
     update_rms = jnp.sqrt(total_update / counts)
     factor = jnp.maximum(1.0, update_rms / clip_limit)
     scale = jnp.sqrt(total_weight / counts)
-    stride = step_rate * scale / factor
-    new_weights = [all_weights[i] - stride[i] * all_updates[i] for i in range(6)]
+    stride = step_rate * scale / factor * jnp.sqrt(means)
+    new_weights = [norm_gain - stride[0] * gain_update]
+    for i in range(4):
+        shape = (-1,) + (1,) * (matrices[i].ndim - 1)
+        second = inverse_rows[ends[i] : ends[i + 1]].reshape(shape) * lax.rsqrt(col_news[i])[None]
+        new_weights.append(weights[i] - stride[i + 1] * matrices[i] * second)
+    new_weights.append(channel_table - stride[5] * table_update)
     return (
         mixed,
         token_grad,

time: 690 us -> 630 us (0.913)
  waiting for transfers between devices: 130 us -> 101 us
  local copies, waits for them, and re-layouts: 63.4 us -> 45.3 us
  Pallas kernels: 183 us -> 201 us
  other arithmetic: 94.7 us -> 83.2 us
  matrix products: 117 us -> 106 us
    ppermute x57, waiting for transfers between devices: 122 us -> 71.8 us  [swap(): lax.ppermute(block, axis, [(i, i ^ bit) for i in range(lax.axis_size(axis...]
    all_gather x4, waiting for transfers between devices: 0.01 us -> 27 us  [line_gather(): return lax.all_gather(own, 'tensor', axis=0, tiled=True)]
    pallas_call x0 -> x7, Pallas kernels: none -> 18.3 us  [the longest x4 10.7 us: fill(): pl.pallas_call(fill_kernel, grid=(height // rows,), in_specs=[pl.BlockSpe...]
    ppermute x12 -> x0, starting transfers between devices: 14.9 us -> none  [few_total(): lax.ppermute(value, axis, [(i, i ^ k) for i in range(n)])]
    dot_general x46, matrix products: 117 us -> 106 us  [dot(): lax.dot_general(a, b, (dims, ((), ())), preferred_element_type=FULL)]
    reduce_sum x15 -> x8, other arithmetic: 18.2 us -> 7.69 us  [the longest x6 6.08 us: per_device(): jnp.sum(jnp.square(after(w, middle)))]
    unnamed x273 -> x279, local copies, waits for them, and re-layouts: 25.2 us -> 15 us
    another operation x6 -> x2, local copies, waits for them, and re-layouts: 10.5 us -> 1.92 us  [the longest x1 1.31 us: per_device(): list(pick_rows(part_small, order).reshape(n_ctx, -1, inner))]
  transfers between devices with their start and end apart: 81 -> 69, of which waited for: 32 -> 28; matrix products, arithmetic and copies ran while one was open for 35% -> 33% of each run, Pallas kernels for 21% -> 28%
where the time goes in v3:
time: 630 us; the launch traced here: 620 us
  Pallas kernels  201 us (32%)
  matrix products  106 us (17%)
  waiting for transfers between devices  101 us (16%)
  other arithmetic  83.2 us (13%)
  starting transfers between devices  66.2 us (11%)
  local copies, waits for them, and re-layouts  45.3 us (7%)
  between operations  16.9 us (3%)
    dot_general x46, matrix products, dot(): lax.dot_general(a, b, (dims, ((), ())), preferred_element_type=FULL)  106 us
    ppermute x57, waiting for transfers between devices, swap(): lax.ppermute(block, axis, [(i, i ^ bit) for i in range(lax.axis_size(axis...  71.8 us
    pallas_call x2, Pallas kernels, scan_backward(): pl.pallas_call(functools.partial(backward_kernel, rows, groups, tile, 8,...  67.1 us
    ppermute x57, starting transfers between devices, swap(): lax.ppermute(block, axis, [(i, i ^ bit) for i in range(lax.axis_size(axis...  58 us
    pallas_call x2, Pallas kernels, scan_forward(): pl.pallas_call(functools.partial(forward_kernel, rows, groups, tile, 8, 4...  54 us
    all_gather x4, waiting for transfers between devices, line_gather(): return lax.all_gather(own, 'tensor', axis=0, tiled=True)  27 us
    pallas_call x2, Pallas kernels, scan_edge(): pl.pallas_call(functools.partial(edge_kernel, rows, groups, tile, 4), gri...  23.2 us
    unnamed x279, local copies, waits for them, and re-layouts  15 us
  transfers between devices with their start and end apart: 69, of which 28 were waited for; matrix products, arithmetic and copies ran while one was open for 33% of the time, Pallas kernels for 28%

profile of v3, /device:TPU:0, one launch (start us, length us, event | category | flops | bytes accessed | tf_op | source)
XLA Modules:
  0.0 620.4 jit_solution(14237028688900297293)
XLA Ops:
  22.9 5.6 normalize.3
  28.5 5.7 normalize.2
  37.6 6.4 %collective-permute-done.6 = bf16[160,1024]{1,0:T(8,128)(2,1)S(1)} collective-permute-done((bf16[160,1024]{1,0:T(8,128)(2,1)S(1)}, bf16[160,1024]{1,0:T(8,128)(2,1)S(1)}, u32[]{:S(2)}, u32[]{:S(2)}) %collective-permute-start.6) | collective-permute-done | bytes 327712 | tf_op jit(solution)/shard_map/ppermute | solution.py:48
  87.8 4.1 collective-permute-done.13
  102.9 9.8 %collective-permute-done.11 = bf16[512,160]{1,0:T(8,128)(2,1)S(1)} collective-permute-done((bf16[512,160]{1,0:T(8,128)(2,1)S(1)}, bf16[512,160]{1,0:T(8,128)(2,1)S(1)}, u32[]{:S(2)}, u32[]{:S(2)}) %collective-permute-start.11) | collective-permute-done | bytes 163872 | tf_op jit(solution)/shard_map/ppermute | solution.py:48
  128.7 11.6 %scan_edge.2 = f32[16,8,128]{2,1,0:T(8,128)} custom-call(s32[1]{0:T(128)} %bitcast.30.flag, f32[512,1024]{1,0:T(8,128)} %compare_select_fusion.1.size_ref, bf16[512,1024]{1,0:T(8,128)(2,1)} %copy-done.22, f32[512,1024]{1,0:T(8,128)} %convolution_add_fusion.1.grad_ref, bf16[512,1024]{1,0:T(8,128)(2,1)} %add_convert_fusion.14.gate_ref, ...), custom_call_target="tpu_custom_call" | custom-call | flops 6710886400 | bytes 6291456 | tf_op jit(solution)/shard_map/scan_edge/pallas_call | solution.py:448
  142.6 27.0 %scan_forward.2 = (bf16[512,1024]{1,0:T(8,128)(2,1)}, bf16[512,1024]{1,0:T(8,128)(2,1)}, f32[512,16,8,128]{3,2,1,0:T(8,128)}, f32[512,128]{1,0:T(8,128)}, f32[1,1024]{1,0:T(1,128)}) custom-call(f32[512,1024]{1,0:T(8,128)} %compare_select_fusion.1.size_ref, bf16[512,1024]{1,0:T(8,128)(2,1)} %copy-done.22, f32[512,1024]{1,0:T(8,128)} %convolution_add_fusion.1.grad_ref, ...), custom_call_target="tpu_custom_call" | custom-call | flops 12582912000 | bytes 41943040 | tf_op jit(solution)/shard_map/scan_forward/pallas_call | solution.py:472
  186.0 4.2 convolution_add_fusion.grad_ref
  190.2 11.6 %scan_edge.3 = f32[16,8,128]{2,1,0:T(8,128)} custom-call(s32[1]{0:T(128)} %bitcast.30.flag, f32[512,1024]{1,0:T(8,128)} %compare_select_fusion.size_ref, bf16[512,1024]{1,0:T(8,128)(2,1)} %copy-done.24, f32[512,1024]{1,0:T(8,128)} %convolution_add_fusion.grad_ref, bf16[512,1024]{1,0:T(8,128)(2,1)} %add_convert_fusion.13.gate_ref, ...), custom_call_target="tpu_custom_call" | custom-call | flops 6710886400 | bytes 6291456 | tf_op jit(solution)/shard_map/scan_edge/pallas_call | solution.py:448
  204.4 27.0 %scan_forward.3 = (bf16[512,1024]{1,0:T(8,128)(2,1)}, bf16[512,1024]{1,0:T(8,128)(2,1)}, f32[512,16,8,128]{3,2,1,0:T(8,128)}, f32[512,128]{1,0:T(8,128)}, f32[1,1024]{1,0:T(1,128)}) custom-call(f32[512,1024]{1,0:T(8,128)} %compare_select_fusion.size_ref, bf16[512,1024]{1,0:T(8,128)(2,1)} %copy-done.24, f32[512,1024]{1,0:T(8,128)} %convolution_add_fusion.grad_ref, ...), custom_call_target="tpu_custom_call" | custom-call | flops 12582912000 | bytes 41943040 | tf_op jit(solution)/shard_map/scan_forward/pallas_call | solution.py:472
  242.7 33.2 %scan_backward.2 = (bf16[512,1024]{1,0:T(8,128)(2,1)}, f32[512,1024]{1,0:T(8,128)}, f32[512,128]{1,0:T(8,128)}, f32[16,8,128]{2,1,0:T(8,128)}, f32[1,1024]{1,0:T(1,128)}) custom-call(f32[512,1024]{1,0:T(8,128)} %compare_select_fusion.1.size_ref, bf16[512,1024]{1,0:T(8,128)(2,1)} %copy-done.22, f32[512,1024]{1,0:T(8,128)} %convolution_add_fusion.1.grad_ref, ...), custom_call_target="tpu_custom_call" | custom-call | flops 16777216000 | bytes 41943040 | tf_op jit(solution)/shard_map/scan_backward/pallas_call | solution.py:514
  287.9 5.1 collective-permute-start.25
  299.8 4.5 fusion.120
  314.9 33.9 %scan_backward.3 = (bf16[512,1024]{1,0:T(8,128)(2,1)}, f32[512,1024]{1,0:T(8,128)}, f32[512,128]{1,0:T(8,128)}, f32[16,8,128]{2,1,0:T(8,128)}, f32[1,1024]{1,0:T(1,128)}) custom-call(f32[512,1024]{1,0:T(8,128)} %compare_select_fusion.size_ref, bf16[512,1024]{1,0:T(8,128)(2,1)} %copy-done.24, f32[512,1024]{1,0:T(8,128)} %convolution_add_fusion.grad_ref, ...), custom_call_target="tpu_custom_call" | custom-call | flops 16777216000 | bytes 41943040 | tf_op jit(solution)/shard_map/scan_backward/pallas_call | solution.py:514
  352.5 7.1 %collective-permute-done.28 = bf16[512,160]{1,0:T(8,128)(2,1)S(1)} collective-permute-done((bf16[512,160]{1,0:T(8,128)(2,1)S(1)}, bf16[512,160]{1,0:T(8,128)(2,1)S(1)}, u32[]{:S(2)}, u32[]{:S(2)}) %collective-permute-start.28) | collective-permute-done | bytes 163872 | tf_op jit(solution)/shard_map/ppermute | solution.py:48
  360.7 7.3 %conv_backward.2 = (bf16[512,1024]{1,0:T(8,128)(2,1)}, f32[8,1024]{1,0:T(8,128)}, f32[8,1024]{1,0:T(8,128)}, f32[8,1024]{1,0:T(8,128)}) custom-call(f32[512,1024]{1,0:T(8,128)} %get-tuple-element.168.value_grad_ref, bf16[512,160]{1,0:T(8,128)(2,1)} %add_convert_fusion.17.proj_ref, bf16[160,1024]{1,0:T(8,128)(2,1)} %copy-done.44, ...), custom_call_target="tpu_custom_call" | custom-call | tf_op jit(solution)/shard_map/conv_backward/pallas_call | solution.py:815
  369.3 4.8 collective-permute-done.29
  396.7 7.2 %conv_backward.3 = (bf16[512,1024]{1,0:T(8,128)(2,1)}, f32[8,1024]{1,0:T(8,128)}, f32[8,1024]{1,0:T(8,128)}, f32[8,1024]{1,0:T(8,128)}) custom-call(f32[512,1024]{1,0:T(8,128)} %get-tuple-element.179.value_grad_ref, bf16[512,160]{1,0:T(8,128)(2,1)} %fusion.43.proj_ref, bf16[160,1024]{1,0:T(8,128)(2,1)} %copy-done.44, bf16[512,1024]{1,0:T(8,128)(2,1)} %copy-done.20, ...), custom_call_target="tpu_custom_call" | custom-call | tf_op jit(solution)/shard_map/conv_backward/pallas_call | solution.py:815
  438.6 4.6 add_convert_fusion.2
  482.3 7.5 %collective-permute-done.42 = bf16[2,48,512]{2,1,0:T(8,128)(2,1)S(1)} collective-permute-done((bf16[2,48,512]{2,1,0:T(8,128)(2,1)S(1)}, bf16[2,48,512]{2,1,0:T(8,128)(2,1)S(1)}, u32[]{:S(2)}, u32[]{:S(2)}) %collective-permute-start.42) | collective-permute-done | bytes 98336 | tf_op jit(solution)/shard_map/ppermute | solution.py:48
  546.7 17.4 %all-gather.11.cloned.1.call-done.part_ref = bf16[512,2048]{1,0:T(8,128)(2,1)} async-done(((bf16[128,2048]{1,0:T(8,128)(2,1)}), bf16[512,2048]{1,0:T(8,128)(2,1)}) %all-gather.11.cloned.1.call-update) | async-done | bytes 2097168 | tf_op jit(solution)/shard_map/all_gather | solution.py:148
  575.0 4.5 collective-permute-done.59
  579.6 4.4 collective-permute-done.60
  602.5 7.9 %all-gather.9.cloned.1.call-done.part_ref = bf16[512,2048]{1,0:T(8,128)(2,1)} async-done(((bf16[128,2048]{1,0:T(8,128)(2,1)}), bf16[512,2048]{1,0:T(8,128)(2,1)}) %all-gather.9.cloned.1.call-update) | async-done | bytes 2097168 | tf_op jit(solution)/shard_map/all_gather | solution.py:148
  (640 shorter events, 341.0 us)
Async XLA Ops:
  7.2 232.7 %reduce-scatter.7.cloned.1.call-start = ((), (), s32[]{:S(2)}) async-start(), calls=%async_computation.5 | async-start | bytes 2621440 | tf_op jit(solution)/shard_map/reduce_scatter | solution.py:144
  45.6 21.8 %collective-permute-start.20 = (bf16[256,1024]{1,0:T(8,128)(2,1)}, bf16[256,1024]{1,0:T(8,128)(2,1)}, u32[]{:S(2)}, u32[]{:S(2)}) collective-permute-start(bf16[256,1024]{1,0:T(8,128)(2,1)} %get-tuple-element.351), channel_id=1, source_target_pairs={{0,16},{8,24},{16,0},{24,8},{1,17},{9,25},{17,1},{25,9},{2,18},{10... | collective-permute-start | bytes 1572872 | tf_op jit(solution)/shard_map/ppermute | solution.py:48
  47.3 44.6 %collective-permute-start.19 = (bf16[256,1024]{1,0:T(8,128)(2,1)}, bf16[256,1024]{1,0:T(8,128)(2,1)}, u32[]{:S(2)}, u32[]{:S(2)}) collective-permute-start(bf16[256,1024]{1,0:T(8,128)(2,1)} %get-tuple-element.351), channel_id=1, source_target_pairs={{0,8},{8,0},{16,24},{24,16},{1,9},{9,1},{17,25},{25,17},{2,10},{10... | collective-permute-start | bytes 1572872 | tf_op jit(solution)/shard_map/ppermute | solution.py:48
  49.7 33.4 %collective-permute-start.15 = (bf16[256,1024]{1,0:T(8,128)(2,1)}, bf16[256,1024]{1,0:T(8,128)(2,1)}, u32[]{:S(2)}, u32[]{:S(2)}) collective-permute-start(bf16[256,1024]{1,0:T(8,128)(2,1)} %convert_element_type.396), channel_id=1, source_target_pairs={{0,8},{8,0},{16,24},{24,16},{1,9},{9,1},{17,25},{25,17},{2,10},{10... | collective-permute-start | bytes 1572872 | tf_op jit(solution)/shard_map/ppermute | solution.py:48
  50.2 46.1 %collective-permute-start.16 = (bf16[256,1024]{1,0:T(8,128)(2,1)}, bf16[256,1024]{1,0:T(8,128)(2,1)}, u32[]{:S(2)}, u32[]{:S(2)}) collective-permute-start(bf16[256,1024]{1,0:T(8,128)(2,1)} %convert_element_type.396), channel_id=1, source_target_pairs={{0,16},{8,24},{16,0},{24,8},{1,17},{9,25},{17,1},{25,9},{2,18},{10... | collective-permute-start | bytes 1572872 | tf_op jit(solution)/shard_map/ppermute | solution.py:48
  67.4 24.5 %collective-permute-start.21 = (bf16[256,1024]{1,0:T(8,128)(2,1)}, bf16[256,1024]{1,0:T(8,128)(2,1)}, u32[]{:S(2)}, u32[]{:S(2)}) collective-permute-start(bf16[256,1024]{1,0:T(8,128)(2,1)} %collective-permute-done.20), channel_id=1, source_target_pairs={{0,8},{8,0},{16,24},{24,16},{1,9},{9,1},{17,25},{25,17},{2,10},{10... | collective-permute-start | bytes 1572872 | tf_op jit(solution)/shard_map/ppermute | solution.py:48
  93.6 25.2 %collective-permute-start.22 = (bf16[1024,1024]{1,0:T(8,128)(2,1)S(1)}, bf16[1024,1024]{1,0:T(8,128)(2,1)S(1)}, u32[]{:S(2)}, u32[]{:S(2)}) collective-permute-start(bf16[1024,1024]{1,0:T(8,128)(2,1)S(1)} %pad_maximum_fusion.2), channel_id=1, source_target_pairs={{0,4},{4,0},{1,5},{5,1},{2,6},{6,2},{3,7},{7,3},{8,12},{12,8},{9,1... | collective-permute-start | bytes 6291464 | tf_op jit(solution)/shard_map/ppermute | solution.py:48
  98.0 24.6 %collective-permute-start.18 = (bf16[1024,1024]{1,0:T(8,128)(2,1)S(1)}, bf16[1024,1024]{1,0:T(8,128)(2,1)S(1)}, u32[]{:S(2)}, u32[]{:S(2)}) collective-permute-start(bf16[1024,1024]{1,0:T(8,128)(2,1)S(1)} %pad_maximum_fusion.1), channel_id=1, source_target_pairs={{0,4},{4,0},{1,5},{5,1},{2,6},{6,2},{3,7},{7,3},{8,12},{12,8},{9,1... | collective-permute-start | bytes 6291464 | tf_op jit(solution)/shard_map/ppermute | solution.py:48
  112.8 27.5 %collective-permute-start.12 = (bf16[512,160]{1,0:T(8,128)(2,1)S(1)}, bf16[512,160]{1,0:T(8,128)(2,1)S(1)}, u32[]{:S(2)}, u32[]{:S(2)}) collective-permute-start(bf16[512,160]{1,0:T(8,128)(2,1)S(1)} %add_convert_fusion.18), channel_id=1, source_target_pairs={{0,2},{1,3},{2,0},{3,1},{4,6},{5,7},{6,4},{7,5},{8,10},{9,11},{10,... | collective-permute-start | bytes 491528 | tf_op jit(solution)/shard_map/ppermute | solution.py:48
  175.6 121.2 %reduce-scatter.5.cloned.1.call-start = ((), (), s32[]{:S(2)}) async-start(), calls=%async_computation.4 | async-start | bytes 2621440 | tf_op jit(solution)/shard_map/reduce_scatter | solution.py:144
  238.2 122.5 %all-gather.5.cloned.1.call-start = ((), (), s32[]{:S(2)}) async-start(), calls=%async_computation.6 | async-start | bytes 2621440 | tf_op jit(solution)/shard_map/all_gather | solution.py:148
  284.6 27.4 %collective-permute-start.46 = (bf16[1024,1024]{1,0:T(8,128)(2,1)}, bf16[1024,1024]{1,0:T(8,128)(2,1)}, u32[]{:S(2)}, u32[]{:S(2)}) collective-permute-start(bf16[1024,1024]{1,0:T(8,128)(2,1)} %add_convert_fusion.7), channel_id=1, source_target_pairs={{0,4},{4,0},{1,5},{5,1},{2,6},{6,2},{3,7},{7,3},{8,12},{12,8},{9,1... | collective-permute-start | bytes 6291464 | tf_op jit(solution)/shard_map/ppermute | solution.py:48
  293.0 141.8 %reduce-scatter.11.cloned.1.call-start = ((), (), s32[]{:S(2)}) async-start(), calls=%async_computation.10 | async-start | bytes 2621440 | tf_op jit(solution)/shard_map/reduce_scatter | solution.py:144
  308.1 43.6 %collective-permute-start.26 = (bf16[512,160]{1,0:T(8,128)(2,1)S(1)}, bf16[512,160]{1,0:T(8,128)(2,1)S(1)}, u32[]{:S(2)}, u32[]{:S(2)}) collective-permute-start(bf16[512,160]{1,0:T(8,128)(2,1)S(1)} %fusion.80), channel_id=1, source_target_pairs={{0,2},{1,3},{2,0},{3,1},{4,6},{5,7},{6,4},{7,5},{8,10},{9,11},{10,... | collective-permute-start | bytes 491528 | tf_op jit(solution)/shard_map/ppermute | solution.py:48
  383.3 121.4 %reduce-scatter.9.cloned.1.call-start = ((), (), s32[]{:S(2)}) async-start(), calls=%async_computation.8 | async-start | bytes 2621440 | tf_op jit(solution)/shard_map/reduce_scatter | solution.py:144
  416.3 101.5 %all-gather.7.cloned.1.call-start = ((), (), s32[]{:S(2)}) async-start(), calls=%async_computation.7 | async-start | bytes 2621440 | tf_op jit(solution)/shard_map/all_gather | solution.py:148
  416.9 147.3 %all-gather.11.cloned.1.call-start = ((), (), s32[]{:S(2)}) async-start(), calls=%async_computation.11 | async-start | bytes 2621440 | tf_op jit(solution)/shard_map/all_gather | solution.py:148
  424.9 21.0 %collective-permute-start.47 = (bf16[2,256,512]{2,1,0:T(8,128)(2,1)}, bf16[2,256,512]{2,1,0:T(8,128)(2,1)}, u32[]{:S(2)}, u32[]{:S(2)}) collective-permute-start(bf16[2,256,512]{2,1,0:T(8,128)(2,1)} %pad_maximum_fusion.16), channel_id=1, source_target_pairs={{0,8},{8,0},{16,24},{24,16},{1,9},{9,1},{17,25},{25,17},{2,10},{10... | collective-permute-start | bytes 1572872 | tf_op jit(solution)/shard_map/ppermute | solution.py:48
  425.0 20.9 %collective-permute-start.48 = (bf16[2,256,512]{2,1,0:T(8,128)(2,1)}, bf16[2,256,512]{2,1,0:T(8,128)(2,1)}, u32[]{:S(2)}, u32[]{:S(2)}) collective-permute-start(bf16[2,256,512]{2,1,0:T(8,128)(2,1)} %slice.581), channel_id=1, source_target_pairs={{0,16},{8,24},{16,0},{24,8},{1,17},{9,25},{17,1},{25,9},{2,18},{10... | collective-permute-start | bytes 1572872 | tf_op jit(solution)/shard_map/ppermute | solution.py:48
  428.2 35.9 %collective-permute-start.37 = (bf16[2,256,512]{2,1,0:T(8,128)(2,1)}, bf16[2,256,512]{2,1,0:T(8,128)(2,1)}, u32[]{:S(2)}, u32[]{:S(2)}) collective-permute-start(bf16[2,256,512]{2,1,0:T(8,128)(2,1)} %pad_maximum_fusion.15), channel_id=1, source_target_pairs={{0,8},{8,0},{16,24},{24,16},{1,9},{9,1},{17,25},{25,17},{2,10},{10... | collective-permute-start | bytes 1572872 | tf_op jit(solution)/shard_map/ppermute | solution.py:48
  430.2 33.9 %collective-permute-start.38 = (bf16[2,256,512]{2,1,0:T(8,128)(2,1)}, bf16[2,256,512]{2,1,0:T(8,128)(2,1)}, u32[]{:S(2)}, u32[]{:S(2)}) collective-permute-start(bf16[2,256,512]{2,1,0:T(8,128)(2,1)} %slice.557), channel_id=1, source_target_pairs={{0,16},{8,24},{16,0},{24,8},{1,17},{9,25},{17,1},{25,9},{2,18},{10... | collective-permute-start | bytes 1572872 | tf_op jit(solution)/shard_map/ppermute | solution.py:48
  438.3 172.1 %all-gather.9.cloned.1.call-start = ((), (), s32[]{:S(2)}) async-start(), calls=%async_computation.9 | async-start | bytes 2621440 | tf_op jit(solution)/shard_map/all_gather | solution.py:148
  449.8 24.4 %collective-permute-start.49 = (bf16[256,512]{1,0:T(8,128)(2,1)}, bf16[256,512]{1,0:T(8,128)(2,1)}, u32[]{:S(2)}, u32[]{:S(2)}) collective-permute-start(bf16[256,512]{1,0:T(8,128)(2,1)} %get-tuple-element.331), channel_id=1, source_target_pairs={{0,16},{8,24},{16,0},{24,8},{1,17},{9,25},{17,1},{25,9},{2,18},{10... | collective-permute-start | bytes 786440 | tf_op jit(solution)/shard_map/ppermute | solution.py:48
  451.2 23.1 %collective-permute-start.50 = (bf16[256,512]{1,0:T(8,128)(2,1)}, bf16[256,512]{1,0:T(8,128)(2,1)}, u32[]{:S(2)}, u32[]{:S(2)}) collective-permute-start(bf16[256,512]{1,0:T(8,128)(2,1)} %get-tuple-element.332), channel_id=1, source_target_pairs={{0,8},{8,0},{16,24},{24,16},{1,9},{9,1},{17,25},{25,17},{2,10},{10... | collective-permute-start | bytes 786440 | tf_op jit(solution)/shard_map/ppermute | solution.py:48
  (182 other events, 1507.5 us)
Sparse Core Ops, SparseCore 0:
  175.7 48.9 reduce-scatter.6
  238.3 48.6 reduce-scatter.4
  293.1 57.6 all-gather.4
  383.5 41.1 reduce-scatter.10
  427.4 43.1 reduce-scatter.8
  472.1 45.6 all-gather.6
  519.4 44.7 all-gather.10
  565.7 44.6 all-gather.8

commit v4 on v3

--- a/solution.py
+++ b/solution.py
@@ -152,6 +152,18 @@
     return tensor_steps(term)[-2]
 
 
+def tensor_first(term):
+    low = term.astype(LOW)
+    return low.astype(FULL) + swap(low, "tensor", 1).astype(FULL)
+
+
+def tensor_rest(term):
+    for bit in bits("tensor")[1:]:
+        low = term.astype(LOW)
+        term = low.astype(FULL) + swap(low, "tensor", bit).astype(FULL)
+    return term
+
+
 def tensor_steps(term):
     steps, sent = [], []
     for bit in bits("tensor"):
@@ -184,20 +196,13 @@
     target[pl.ds(place, rows, stride=tile), :] = columns
 
 
-def splat(target, table, first, rows):
-    for n in range(N):
-        target[pl.ds(n, rows, stride=N), :] = jnp.broadcast_to(
-            table[:, first + n : first + n + 1], (rows, LANES)
-        )
-
-
 def columns_of(j):
     return slice(j * LANES, (j + 1) * LANES)
 
 
 def edge_kernel(
     rows, groups, tile, unroll, flag, size_ref, value_ref, grad_ref, gate_ref, coef_ref, rate_ref,
-    edge_ref, size_s, term_s, coef_s,
+    edge_ref, size_s, term_s,
 ):
     backward = flag[0] == 1
 
@@ -223,13 +228,12 @@
         for j in range(groups):
             cut = columns_of(j)
             spread(term_s, size_ref[:, cut] * value_ref[:, cut].astype(FULL), j, rows, tile)
-        splat(coef_s, coef_ref, 0, rows)
 
         def body(t, state):
             place = pl.ds(pl.multiple_of(t * tile, tile), tile)
             size, term = size_s[place, :], term_s[place, :]
             return tuple(
-                jnp.exp2(size * rate_ref[n]) * state[n] + term * coef_s[pl.ds(t * N + n, 1), :]
+                jnp.exp2(size * rate_ref[n]) * state[n] + term * coef_ref[t, n]
                 for n in range(N)
             )
 
@@ -241,7 +245,6 @@
             cut = columns_of(j)
             gate = gate_ref[:, cut].astype(FULL)
             spread(term_s, grad_ref[:, cut] * gate * jax.nn.sigmoid(gate), j, rows, tile)
-        splat(coef_s, coef_ref, N, rows)
 
         def body(step, state):
             t = rows - 1 - step
@@ -249,7 +252,7 @@
             size, term = size_s[place, :], term_s[place, :]
             return tuple(
                 jnp.exp2(size * rate_ref[n])
-                * (state[n] + term * coef_s[pl.ds(t * N + n, 1), :])
+                * (state[n] + term * coef_ref[t, N + n])
                 for n in range(N)
             )
 
@@ -260,7 +263,7 @@
     rows, groups, tile, part, unroll,
     size_ref, value_ref, grad_ref, gate_ref, coef_ref, rate_ref, start_ref, skip_ref,
     gated_ref, gate_grad_ref, before_ref, grad_c_ref, grad_skip_ref,
-    size_s, input_s, grad_s, out_s, b_s, c_s, product_s, state_s, pick_s,
+    size_s, input_s, grad_s, out_s, product_s, state_s, pick_s,
 ):
     @pl.when(pl.program_id(0) == 0)
     def _():
@@ -283,8 +286,6 @@
         else:
             for target in (size_s, input_s, grad_s):
                 spread(target, blank, j, rows, tile)
-    splat(b_s, coef_ref, 0, rows)
-    splat(c_s, coef_ref, N, rows)
     for low in range(0, N, part):
         rate = [rate_ref[n] for n in range(low, low + part)]
 
@@ -297,9 +298,9 @@
                 n = low + k
                 before_ref[t, n] = state[k]
                 state[k] = (
-                    jnp.exp2(size * rate[k]) * state[k] + term * b_s[pl.ds(t * N + n, 1), :]
+                    jnp.exp2(size * rate[k]) * state[k] + term * coef_ref[t, n]
                 )
-                read = c_s[pl.ds(t * N + n, 1), :] * state[k]
+                read = coef_ref[t, N + n] * state[k]
                 out = read if out is None else out + read
                 product_s[place, columns_of(n)] = state[k] * grad
             if low == 0:
@@ -331,7 +332,7 @@
     size_ref, value_ref, grad_ref, gate_ref, coef_ref, rate_ref, tail_ref, skip_ref,
     before_ref,
     pre_low_ref, grad_value_ref, grad_b_ref, grad_rate_ref, grad_bias_ref,
-    size_s, input_s, grad_s, along_s, rated_s, b_s, c_s, product_s, state_s, pick_s,
+    size_s, input_s, grad_s, along_s, rated_s, product_s, state_s, pick_s,
 ):
     @pl.when(pl.program_id(0) == 0)
     def _():
@@ -352,8 +353,6 @@
         else:
             for target in (size_s, input_s, grad_s):
                 spread(target, blank, j, rows, tile)
-    splat(b_s, coef_ref, 0, rows)
-    splat(c_s, coef_ref, N, rows)
     for low in range(0, N, part):
         rate = [rate_ref[n] for n in range(low, low + part)]
 
@@ -365,10 +364,10 @@
             along = rated = None
             for k in range(part):
                 n = low + k
-                adjoint = c_s[pl.ds(t * N + n, 1), :] * grad + state[k]
+                adjoint = coef_ref[t, N + n] * grad + state[k]
                 state[k] = jnp.exp2(size * rate[k]) * adjoint
                 through = state[k] * before_ref[t, n]
-                first = adjoint * b_s[pl.ds(t * N + n, 1), :]
+                first = adjoint * coef_ref[t, n]
                 second = through * rate[k]
                 along = first if along is None else along + first
                 rated = second if rated is None else rated + second
@@ -450,10 +449,10 @@
         grid_spec=pltpu.PrefetchScalarGridSpec(
             num_scalar_prefetch=1,
             grid=(count,),
-            in_specs=[wide] * 4 + [pl.BlockSpec((rows, 2 * N), place), cube],
+            in_specs=[wide] * 4
+            + [pl.BlockSpec((rows, 2 * N), place, memory_space=pltpu.SMEM), cube],
             out_specs=cube,
-            scratch_shapes=[pltpu.VMEM((rows * tile, LANES), FULL)] * 2
-            + [pltpu.VMEM((rows * N, LANES), FULL)],
+            scratch_shapes=[pltpu.VMEM((rows * tile, LANES), FULL)] * 2,
         ),
         out_shape=jax.ShapeDtypeStruct((N, tile, LANES), FULL),
         compiler_params=limits(),
@@ -474,7 +473,7 @@
         grid=(length // rows,),
         in_specs=[wide] * 4
         + [
-            pl.BlockSpec((rows, 2 * N), lambda i: (i, 0)),
+            pl.BlockSpec((rows, 2 * N), lambda i: (i, 0), memory_space=pltpu.SMEM),
             cube,
             cube,
             row,
@@ -494,7 +493,6 @@
             jax.ShapeDtypeStruct((1, channels), FULL),
         ],
         scratch_shapes=[pltpu.VMEM((rows * tile, LANES), FULL)] * 4
-        + [pltpu.VMEM((rows * N, LANES), FULL)] * 2
         + [pltpu.VMEM((rows * tile, N * LANES), FULL), pltpu.VMEM((N, tile, LANES), FULL)]
         + [pltpu.VMEM((N * LANES, LANES), LOW)],
         compiler_params=limits(),
@@ -516,7 +514,7 @@
         grid=(length // rows,),
         in_specs=[wide] * 4
         + [
-            pl.BlockSpec((rows, 2 * N), lambda i: (last - i, 0)),
+            pl.BlockSpec((rows, 2 * N), lambda i: (last - i, 0), memory_space=pltpu.SMEM),
             cube,
             cube,
             row,
@@ -531,7 +529,6 @@
             jax.ShapeDtypeStruct((1, channels), FULL),
         ],
         scratch_shapes=[pltpu.VMEM((rows * tile, LANES), FULL)] * 5
-        + [pltpu.VMEM((rows * N, LANES), FULL)] * 2
         + [pltpu.VMEM((rows * tile, N * LANES), FULL), pltpu.VMEM((N, tile, LANES), FULL)]
         + [pltpu.VMEM((N * LANES, LANES), LOW)],
         compiler_params=limits(),
@@ -959,18 +956,18 @@
     def chunks_of(parts):
         return list(zip(*parts))
 
-    backs, parts, steps_of, gate_parts, part_out = [], [], [], [], []
+    backs, parts, first_of, gate_parts, part_out = [], [], [], [], []
     for m in every:
         leaving = after(tail[m], branch[-1], own_mixed[0])
         if m > 0:
-            leaving = after(leaving, steps_of[0][0], *part_out, *gate_parts[0], *own_mixed)
+            leaving = after(leaving, first_of[0], *part_out, *gate_parts[0], *own_mixed)
         pre_low, value_grad, grad_b, grad_rate, grad_bias = scan_backward(
             size[m], values[m], grad_gated[m], gate_in[m], coef[m], rate, leaving, skip, before[m]
         )
         backs.append((pre_low, value_grad, grad_rate, grad_bias))
         grad_rank = dot(pre_low, step_low, ((1,), (1,)))
         parts.append(jnp.concatenate([grad_rank, grad_b[:, :N], grad_c[m][:, :N]], axis=1))
-        steps_of.append(tensor_steps(parts[m]))
+        first_of.append(tensor_first(parts[m]))
         if m == 0:
             for side in chunks_of(grad_rel):
                 part_out.append(over_micros(after_all(side, parts[0]), gated).astype(LOW))
@@ -979,19 +976,19 @@
     mixed = [line_gather(own_mixed[0])]
     pre_lows = [back[0] for back in backs]
     conv_grads, proj_grads, gain_parts, tables, partial, tokens_out = [], [], [], [], [], []
-    part_gate = []
+    part_gate, totals = [], [tensor_rest(first_of[0])]
     for m in every:
         _, value_grad, grad_rate, grad_bias = backs[m]
-        proj_grad = steps_of[m][-2].astype(LOW)
+        proj_grad = totals[m].astype(LOW)
         proj_grads.append(proj_grad)
         wait_for = [mixed[0], parts[-1]]
         if m > 0:
-            started = [partial[0], steps_of[m][0]]
+            started = [partial[0], first_of[m]]
             gate_grad_then = after(gate_grad[m], *started)
             gate_parts.append([dot(gate_grad_then, g, ((1,), (1,))) for g in gate_low])
             if m == micro - 1:
                 for c, side in enumerate(chunks_of(normed)):
-                    arrived = started + steps_of[m][-2:-1] if c else started
+                    arrived = started + [totals[m]] if c else started
                     part_gate.append(over_micros(after_all(side, *arrived), gate_grad).astype(LOW))
             wait_for = wait_for + gate_parts[m] + part_gate
         conv_grad, last, head, sums = conv_backward(
@@ -1001,7 +998,7 @@
         last = last + shifted(head, "ctx", -1)
         conv_grad = lax.dynamic_update_slice(conv_grad, last.astype(LOW), (length - 8, 0))
         if m == 0:
-            conv_grad = after(conv_grad, steps_of[-1][0])
+            totals = totals + [tensor_rest(after(first, sums)) for first in first_of[1:]]
         conv_grads.append(conv_grad)
         partial.append(
             jnp.concatenate(
@@ -1012,7 +1009,7 @@
                 axis=1,
             )
         )
-        sent = after(partial[m], steps_of[-1][-2])
+        sent = after(partial[m], totals[-1])
         token, gain_part = token_rows(
             order, m * n_tensor + me, tokens_flat, grad_flat, gain_low, line_scatter(sent)
         )

time: 630 us -> 620 us (0.984)
    unnamed x279 -> x285, local copies, waits for them, and re-layouts: 15 us -> 13.7 us
  transfers between devices with their start and end apart: 69 -> 69, of which waited for: 28 -> 27; matrix products, arithmetic and copies ran while one was open for 33% -> 35% of each run, Pallas kernels for 28% -> 28%
where the time goes in v4:
time: 620 us; the launch traced here: 609 us
  Pallas kernels  196 us (32%)
  matrix products  107 us (17%)
  waiting for transfers between devices  97.9 us (16%)
  other arithmetic  82.6 us (13%)
  starting transfers between devices  66.6 us (11%)
  local copies, waits for them, and re-layouts  42.5 us (7%)
  between operations  17 us (3%)
    dot_general x46, matrix products, dot(): lax.dot_general(a, b, (dims, ((), ())), preferred_element_type=FULL)  107 us
    ppermute x57, waiting for transfers between devices, swap(): lax.ppermute(block, axis, [(i, i ^ bit) for i in range(lax.axis_size(axis...  67.6 us
    pallas_call x2, Pallas kernels, scan_backward(): pl.pallas_call(functools.partial(backward_kernel, rows, groups, tile, 8,...  64.6 us
    ppermute x57, starting transfers between devices, swap(): lax.ppermute(block, axis, [(i, i ^ bit) for i in range(lax.axis_size(axis...  58.5 us
    pallas_call x2, Pallas kernels, scan_forward(): pl.pallas_call(functools.partial(forward_kernel, rows, groups, tile, 8, 4...  51.2 us
    all_gather x4, waiting for transfers between devices, line_gather(): return lax.all_gather(own, 'tensor', axis=0, tiled=True)  27.6 us
    pallas_call x2, Pallas kernels, scan_edge(): pl.pallas_call(functools.partial(edge_kernel, rows, groups, tile, 4), gri...  23.2 us
    pallas_call x2, Pallas kernels, conv_backward(): pl.pallas_call(conv_kernel, grid=(channels // width,), in_specs=[tall, pl...  14.5 us
  transfers between devices with their start and end apart: 69, of which 27 were waited for; matrix products, arithmetic and copies ran while one was open for 35% of the time, Pallas kernels for 28%

profile of v4, /device:TPU:0, one launch (start us, length us, event | category | flops | bytes accessed | tf_op | source)
XLA Modules:
  0.0 609.3 jit_solution(12126665270268077003)
XLA Ops:
  22.9 5.7 normalize.3
  28.5 5.7 normalize.2
  37.6 6.5 %collective-permute-done.6 = bf16[160,1024]{1,0:T(8,128)(2,1)S(1)} collective-permute-done((bf16[160,1024]{1,0:T(8,128)(2,1)S(1)}, bf16[160,1024]{1,0:T(8,128)(2,1)S(1)}, u32[]{:S(2)}, u32[]{:S(2)}) %collective-permute-start.6) | collective-permute-done | bytes 327712 | tf_op jit(solution)/shard_map/ppermute | solution.py:48
  84.3 5.4 collective-permute-done.13
  100.7 9.8 %collective-permute-done.11 = bf16[512,160]{1,0:T(8,128)(2,1)S(1)} collective-permute-done((bf16[512,160]{1,0:T(8,128)(2,1)S(1)}, bf16[512,160]{1,0:T(8,128)(2,1)S(1)}, u32[]{:S(2)}, u32[]{:S(2)}) %collective-permute-start.11) | collective-permute-done | bytes 163872 | tf_op jit(solution)/shard_map/ppermute | solution.py:48
  126.8 11.6 %scan_edge.2 = f32[16,8,128]{2,1,0:T(8,128)} custom-call(s32[1]{0:T(128)} %bitcast.30.flag, f32[512,1024]{1,0:T(8,128)} %compare_select_fusion.1.size_ref, bf16[512,1024]{1,0:T(8,128)(2,1)} %copy-done.15, f32[512,1024]{1,0:T(8,128)} %convolution_add_fusion.1.grad_ref, bf16[512,1024]{1,0:T(8,128)(2,1)} %add_convert_fusion.14.gate_ref, ...), custom_call_target="tpu_custom_call" | custom-call | flops 6710886400 | bytes 6291456 | tf_op jit(solution)/shard_map/scan_edge/pallas_call | solution.py:447
  140.6 25.6 %scan_forward.2 = (bf16[512,1024]{1,0:T(8,128)(2,1)}, bf16[512,1024]{1,0:T(8,128)(2,1)}, f32[512,16,8,128]{3,2,1,0:T(8,128)}, f32[512,128]{1,0:T(8,128)}, f32[1,1024]{1,0:T(1,128)}) custom-call(f32[512,1024]{1,0:T(8,128)} %compare_select_fusion.1.size_ref, bf16[512,1024]{1,0:T(8,128)(2,1)} %copy-done.15, f32[512,1024]{1,0:T(8,128)} %convolution_add_fusion.1.grad_ref, ...), custom_call_target="tpu_custom_call" | custom-call | flops 12582912000 | bytes 41943040 | tf_op jit(solution)/shard_map/scan_forward/pallas_call | solution.py:471
  185.5 11.6 %scan_edge.3 = f32[16,8,128]{2,1,0:T(8,128)} custom-call(s32[1]{0:T(128)} %bitcast.30.flag, f32[512,1024]{1,0:T(8,128)} %compare_select_fusion.size_ref, bf16[512,1024]{1,0:T(8,128)(2,1)} %copy-done.17, f32[512,1024]{1,0:T(8,128)} %convolution_add_fusion.grad_ref, bf16[512,1024]{1,0:T(8,128)(2,1)} %add_convert_fusion.13.gate_ref, ...), custom_call_target="tpu_custom_call" | custom-call | flops 6710886400 | bytes 6291456 | tf_op jit(solution)/shard_map/scan_edge/pallas_call | solution.py:447
  199.5 25.6 %scan_forward.3 = (bf16[512,1024]{1,0:T(8,128)(2,1)}, bf16[512,1024]{1,0:T(8,128)(2,1)}, f32[512,16,8,128]{3,2,1,0:T(8,128)}, f32[512,128]{1,0:T(8,128)}, f32[1,1024]{1,0:T(1,128)}) custom-call(f32[512,1024]{1,0:T(8,128)} %compare_select_fusion.size_ref, bf16[512,1024]{1,0:T(8,128)(2,1)} %copy-done.17, f32[512,1024]{1,0:T(8,128)} %convolution_add_fusion.grad_ref, ...), custom_call_target="tpu_custom_call" | custom-call | flops 12582912000 | bytes 41943040 | tf_op jit(solution)/shard_map/scan_forward/pallas_call | solution.py:471
  236.4 31.9 %scan_backward.2 = (bf16[512,1024]{1,0:T(8,128)(2,1)}, f32[512,1024]{1,0:T(8,128)}, f32[512,128]{1,0:T(8,128)}, f32[16,8,128]{2,1,0:T(8,128)}, f32[1,1024]{1,0:T(1,128)}) custom-call(f32[512,1024]{1,0:T(8,128)} %compare_select_fusion.1.size_ref, bf16[512,1024]{1,0:T(8,128)(2,1)} %copy-done.15, f32[512,1024]{1,0:T(8,128)} %convolution_add_fusion.1.grad_ref, ...), custom_call_target="tpu_custom_call" | custom-call | flops 16777216000 | bytes 41943040 | tf_op jit(solution)/shard_map/scan_backward/pallas_call | solution.py:512
  280.1 5.3 collective-permute-start.25
  285.9 4.5 fusion.120
  293.4 4.4 fusion.119
  307.5 32.7 %scan_backward.3 = (bf16[512,1024]{1,0:T(8,128)(2,1)}, f32[512,1024]{1,0:T(8,128)}, f32[512,128]{1,0:T(8,128)}, f32[16,8,128]{2,1,0:T(8,128)}, f32[1,1024]{1,0:T(1,128)}) custom-call(f32[512,1024]{1,0:T(8,128)} %compare_select_fusion.size_ref, bf16[512,1024]{1,0:T(8,128)(2,1)} %copy-done.17, f32[512,1024]{1,0:T(8,128)} %convolution_add_fusion.grad_ref, ...), custom_call_target="tpu_custom_call" | custom-call | flops 16777216000 | bytes 41943040 | tf_op jit(solution)/shard_map/scan_backward/pallas_call | solution.py:512
  344.5 7.3 %conv_backward.2 = (bf16[512,1024]{1,0:T(8,128)(2,1)}, f32[8,1024]{1,0:T(8,128)}, f32[8,1024]{1,0:T(8,128)}, f32[8,1024]{1,0:T(8,128)}) custom-call(f32[512,1024]{1,0:T(8,128)} %get-tuple-element.168.value_grad_ref, bf16[512,160]{1,0:T(8,128)(2,1)} %add_convert_fusion.17.proj_ref, bf16[160,1024]{1,0:T(8,128)(2,1)} %copy-done.44, ...), custom_call_target="tpu_custom_call" | custom-call | tf_op jit(solution)/shard_map/conv_backward/pallas_call | solution.py:812
  365.1 5.6 collective-permute-done.29
  384.4 7.2 %conv_backward.3 = (bf16[512,1024]{1,0:T(8,128)(2,1)}, f32[8,1024]{1,0:T(8,128)}, f32[8,1024]{1,0:T(8,128)}, f32[8,1024]{1,0:T(8,128)}) custom-call(f32[512,1024]{1,0:T(8,128)} %get-tuple-element.180.value_grad_ref, bf16[512,160]{1,0:T(8,128)(2,1)} %fusion.80.proj_ref, bf16[160,1024]{1,0:T(8,128)(2,1)} %copy-done.44, bf16[512,1024]{1,0:T(8,128)(2,1)} %copy-done.13, ...), custom_call_target="tpu_custom_call" | custom-call | tf_op jit(solution)/shard_map/conv_backward/pallas_call | solution.py:812
  426.3 4.6 add_convert_fusion.2
  469.9 7.6 %collective-permute-done.42 = bf16[2,48,512]{2,1,0:T(8,128)(2,1)S(1)} collective-permute-done((bf16[2,48,512]{2,1,0:T(8,128)(2,1)S(1)}, bf16[2,48,512]{2,1,0:T(8,128)(2,1)S(1)}, u32[]{:S(2)}, u32[]{:S(2)}) %collective-permute-start.42) | collective-permute-done | bytes 98336 | tf_op jit(solution)/shard_map/ppermute | solution.py:48
  496.9 4.5 collective-permute-done.51
  535.6 17.4 %all-gather.11.cloned.1.call-done.part_ref = bf16[512,2048]{1,0:T(8,128)(2,1)} async-done(((bf16[128,2048]{1,0:T(8,128)(2,1)}), bf16[512,2048]{1,0:T(8,128)(2,1)}) %all-gather.11.cloned.1.call-update) | async-done | bytes 2097168 | tf_op jit(solution)/shard_map/all_gather | solution.py:148
  563.9 4.5 collective-permute-done.59
  568.5 4.4 collective-permute-done.60
  591.5 7.9 %all-gather.9.cloned.1.call-done.part_ref = bf16[512,2048]{1,0:T(8,128)(2,1)} async-done(((bf16[128,2048]{1,0:T(8,128)(2,1)}), bf16[512,2048]{1,0:T(8,128)(2,1)}) %all-gather.9.cloned.1.call-update) | async-done | bytes 2097168 | tf_op jit(solution)/shard_map/all_gather | solution.py:148
  (646 shorter events, 335.1 us)
Async XLA Ops:
  7.2 226.4 %reduce-scatter.7.cloned.1.call-start = ((), (), s32[]{:S(2)}) async-start(), calls=%async_computation.5 | async-start | bytes 2621440 | tf_op jit(solution)/shard_map/reduce_scatter | solution.py:144
  47.4 42.3 %collective-permute-start.19 = (bf16[256,1024]{1,0:T(8,128)(2,1)}, bf16[256,1024]{1,0:T(8,128)(2,1)}, u32[]{:S(2)}, u32[]{:S(2)}) collective-permute-start(bf16[256,1024]{1,0:T(8,128)(2,1)} %get-tuple-element.351), channel_id=1, source_target_pairs={{0,8},{8,0},{16,24},{24,16},{1,9},{9,1},{17,25},{25,17},{2,10},{10... | collective-permute-start | bytes 1572872 | tf_op jit(solution)/shard_map/ppermute | solution.py:48
  49.7 31.1 %collective-permute-start.15 = (bf16[256,1024]{1,0:T(8,128)(2,1)}, bf16[256,1024]{1,0:T(8,128)(2,1)}, u32[]{:S(2)}, u32[]{:S(2)}) collective-permute-start(bf16[256,1024]{1,0:T(8,128)(2,1)} %convert_element_type.396), channel_id=1, source_target_pairs={{0,8},{8,0},{16,24},{24,16},{1,9},{9,1},{17,25},{25,17},{2,10},{10... | collective-permute-start | bytes 1572872 | tf_op jit(solution)/shard_map/ppermute | solution.py:48
  50.3 43.8 %collective-permute-start.16 = (bf16[256,1024]{1,0:T(8,128)(2,1)}, bf16[256,1024]{1,0:T(8,128)(2,1)}, u32[]{:S(2)}, u32[]{:S(2)}) collective-permute-start(bf16[256,1024]{1,0:T(8,128)(2,1)} %convert_element_type.396), channel_id=1, source_target_pairs={{0,16},{8,24},{16,0},{24,8},{1,17},{9,25},{17,1},{25,9},{2,18},{10... | collective-permute-start | bytes 1572872 | tf_op jit(solution)/shard_map/ppermute | solution.py:48
  65.7 23.9 %collective-permute-start.21 = (bf16[256,1024]{1,0:T(8,128)(2,1)}, bf16[256,1024]{1,0:T(8,128)(2,1)}, u32[]{:S(2)}, u32[]{:S(2)}) collective-permute-start(bf16[256,1024]{1,0:T(8,128)(2,1)} %collective-permute-done.20), channel_id=1, source_target_pairs={{0,8},{8,0},{16,24},{24,16},{1,9},{9,1},{17,25},{25,17},{2,10},{10... | collective-permute-start | bytes 1572872 | tf_op jit(solution)/shard_map/ppermute | solution.py:48
  91.4 25.2 %collective-permute-start.22 = (bf16[1024,1024]{1,0:T(8,128)(2,1)S(1)}, bf16[1024,1024]{1,0:T(8,128)(2,1)S(1)}, u32[]{:S(2)}, u32[]{:S(2)}) collective-permute-start(bf16[1024,1024]{1,0:T(8,128)(2,1)S(1)} %pad_maximum_fusion.2), channel_id=1, source_target_pairs={{0,4},{4,0},{1,5},{5,1},{2,6},{6,2},{3,7},{7,3},{8,12},{12,8},{9,1... | collective-permute-start | bytes 6291464 | tf_op jit(solution)/shard_map/ppermute | solution.py:48
  95.7 25.0 %collective-permute-start.18 = (bf16[1024,1024]{1,0:T(8,128)(2,1)S(1)}, bf16[1024,1024]{1,0:T(8,128)(2,1)S(1)}, u32[]{:S(2)}, u32[]{:S(2)}) collective-permute-start(bf16[1024,1024]{1,0:T(8,128)(2,1)S(1)} %pad_maximum_fusion.1), channel_id=1, source_target_pairs={{0,4},{4,0},{1,5},{5,1},{2,6},{6,2},{3,7},{7,3},{8,12},{12,8},{9,1... | collective-permute-start | bytes 6291464 | tf_op jit(solution)/shard_map/ppermute | solution.py:48
  110.5 27.9 %collective-permute-start.12 = (bf16[512,160]{1,0:T(8,128)(2,1)S(1)}, bf16[512,160]{1,0:T(8,128)(2,1)S(1)}, u32[]{:S(2)}, u32[]{:S(2)}) collective-permute-start(bf16[512,160]{1,0:T(8,128)(2,1)S(1)} %add_convert_fusion.18), channel_id=1, source_target_pairs={{0,2},{1,3},{2,0},{3,1},{4,6},{5,7},{6,4},{7,5},{8,10},{9,11},{10,... | collective-permute-start | bytes 491528 | tf_op jit(solution)/shard_map/ppermute | solution.py:48
  172.3 118.2 %reduce-scatter.5.cloned.1.call-start = ((), (), s32[]{:S(2)}) async-start(), calls=%async_computation.4 | async-start | bytes 2621440 | tf_op jit(solution)/shard_map/reduce_scatter | solution.py:144
  231.9 112.6 %all-gather.5.cloned.1.call-start = ((), (), s32[]{:S(2)}) async-start(), calls=%async_computation.6 | async-start | bytes 2621440 | tf_op jit(solution)/shard_map/all_gather | solution.py:148
  276.8 27.7 %collective-permute-start.46 = (bf16[1024,1024]{1,0:T(8,128)(2,1)}, bf16[1024,1024]{1,0:T(8,128)(2,1)}, u32[]{:S(2)}, u32[]{:S(2)}) collective-permute-start(bf16[1024,1024]{1,0:T(8,128)(2,1)} %add_convert_fusion.7), channel_id=1, source_target_pairs={{0,4},{4,0},{1,5},{5,1},{2,6},{6,2},{3,7},{7,3},{8,12},{12,8},{9,1... | collective-permute-start | bytes 6291464 | tf_op jit(solution)/shard_map/ppermute | solution.py:48
  280.1 20.3 %collective-permute-start.25 = (bf16[512,160]{1,0:T(8,128)(2,1)}, bf16[512,160]{1,0:T(8,128)(2,1)S(1)}, u32[]{:S(2)}, u32[]{:S(2)}) collective-permute-start(bf16[512,160]{1,0:T(8,128)(2,1)} %pad_maximum_fusion.12), channel_id=1, source_target_pairs={{0,1},{1,0},{2,3},{3,2},{4,5},{5,4},{6,7},{7,6},{8,9},{9,8},{10,11... | collective-permute-start | bytes 491528 | tf_op jit(solution)/shard_map/ppermute | solution.py:48
  285.4 137.1 %reduce-scatter.11.cloned.1.call-start = ((), (), s32[]{:S(2)}) async-start(), calls=%async_computation.10 | async-start | bytes 2621440 | tf_op jit(solution)/shard_map/reduce_scatter | solution.py:144
  300.6 43.1 %collective-permute-start.26 = (bf16[512,160]{1,0:T(8,128)(2,1)S(1)}, bf16[512,160]{1,0:T(8,128)(2,1)S(1)}, u32[]{:S(2)}, u32[]{:S(2)}) collective-permute-start(bf16[512,160]{1,0:T(8,128)(2,1)S(1)} %fusion.79), channel_id=1, source_target_pairs={{0,2},{1,3},{2,0},{3,1},{4,6},{5,7},{6,4},{7,5},{8,10},{9,11},{10,... | collective-permute-start | bytes 491528 | tf_op jit(solution)/shard_map/ppermute | solution.py:48
  370.7 121.6 %reduce-scatter.9.cloned.1.call-start = ((), (), s32[]{:S(2)}) async-start(), calls=%async_computation.8 | async-start | bytes 2621440 | tf_op jit(solution)/shard_map/reduce_scatter | solution.py:144
  404.1 102.7 %all-gather.7.cloned.1.call-start = ((), (), s32[]{:S(2)}) async-start(), calls=%async_computation.7 | async-start | bytes 2621440 | tf_op jit(solution)/shard_map/all_gather | solution.py:148
  404.7 148.4 %all-gather.11.cloned.1.call-start = ((), (), s32[]{:S(2)}) async-start(), calls=%async_computation.11 | async-start | bytes 2621440 | tf_op jit(solution)/shard_map/all_gather | solution.py:148
  412.7 20.9 %collective-permute-start.47 = (bf16[2,256,512]{2,1,0:T(8,128)(2,1)}, bf16[2,256,512]{2,1,0:T(8,128)(2,1)}, u32[]{:S(2)}, u32[]{:S(2)}) collective-permute-start(bf16[2,256,512]{2,1,0:T(8,128)(2,1)} %pad_maximum_fusion.16), channel_id=1, source_target_pairs={{0,8},{8,0},{16,24},{24,16},{1,9},{9,1},{17,25},{25,17},{2,10},{10... | collective-permute-start | bytes 1572872 | tf_op jit(solution)/shard_map/ppermute | solution.py:48
  412.7 20.9 %collective-permute-start.48 = (bf16[2,256,512]{2,1,0:T(8,128)(2,1)}, bf16[2,256,512]{2,1,0:T(8,128)(2,1)}, u32[]{:S(2)}, u32[]{:S(2)}) collective-permute-start(bf16[2,256,512]{2,1,0:T(8,128)(2,1)} %slice.581), channel_id=1, source_target_pairs={{0,16},{8,24},{16,0},{24,8},{1,17},{9,25},{17,1},{25,9},{2,18},{10... | collective-permute-start | bytes 1572872 | tf_op jit(solution)/shard_map/ppermute | solution.py:48
  416.0 35.9 %collective-permute-start.37 = (bf16[2,256,512]{2,1,0:T(8,128)(2,1)}, bf16[2,256,512]{2,1,0:T(8,128)(2,1)}, u32[]{:S(2)}, u32[]{:S(2)}) collective-permute-start(bf16[2,256,512]{2,1,0:T(8,128)(2,1)} %pad_maximum_fusion.15), channel_id=1, source_target_pairs={{0,8},{8,0},{16,24},{24,16},{1,9},{9,1},{17,25},{25,17},{2,10},{10... | collective-permute-start | bytes 1572872 | tf_op jit(solution)/shard_map/ppermute | solution.py:48
  417.8 34.1 %collective-permute-start.38 = (bf16[2,256,512]{2,1,0:T(8,128)(2,1)}, bf16[2,256,512]{2,1,0:T(8,128)(2,1)}, u32[]{:S(2)}, u32[]{:S(2)}) collective-permute-start(bf16[2,256,512]{2,1,0:T(8,128)(2,1)} %slice.557), channel_id=1, source_target_pairs={{0,16},{8,24},{16,0},{24,8},{1,17},{9,25},{17,1},{25,9},{2,18},{10... | collective-permute-start | bytes 1572872 | tf_op jit(solution)/shard_map/ppermute | solution.py:48
  426.0 173.3 %all-gather.9.cloned.1.call-start = ((), (), s32[]{:S(2)}) async-start(), calls=%async_computation.9 | async-start | bytes 2621440 | tf_op jit(solution)/shard_map/all_gather | solution.py:148
  437.4 24.4 %collective-permute-start.49 = (bf16[256,512]{1,0:T(8,128)(2,1)}, bf16[256,512]{1,0:T(8,128)(2,1)}, u32[]{:S(2)}, u32[]{:S(2)}) collective-permute-start(bf16[256,512]{1,0:T(8,128)(2,1)} %get-tuple-element.331), channel_id=1, source_target_pairs={{0,16},{8,24},{16,0},{24,8},{1,17},{9,25},{17,1},{25,9},{2,18},{10... | collective-permute-start | bytes 786440 | tf_op jit(solution)/shard_map/ppermute | solution.py:48
  438.8 23.2 %collective-permute-start.50 = (bf16[256,512]{1,0:T(8,128)(2,1)}, bf16[256,512]{1,0:T(8,128)(2,1)}, u32[]{:S(2)}, u32[]{:S(2)}) collective-permute-start(bf16[256,512]{1,0:T(8,128)(2,1)} %get-tuple-element.332), channel_id=1, source_target_pairs={{0,8},{8,0},{16,24},{24,16},{1,9},{9,1},{17,25},{25,17},{2,10},{10... | collective-permute-start | bytes 786440 | tf_op jit(solution)/shard_map/ppermute | solution.py:48
  (185 other events, 1538.7 us)
Sparse Core Ops, SparseCore 0:
  172.4 48.9 reduce-scatter.6
  232.0 48.8 reduce-scatter.4
  285.6 57.6 all-gather.4
  370.9 42.5 reduce-scatter.10
  416.3 43.1 reduce-scatter.8
  460.9 45.8 all-gather.6
  508.4 44.6 all-gather.10
  554.6 44.6 all-gather.8

commit v5 on v4

--- a/solution.py
+++ b/solution.py
@@ -747,22 +747,21 @@
     refs[-1][...] = part_ref[...]
 
 
-def fill(whole, count, m, part):
-    height, columns = part.shape
-    rows = min(256, height)
-    spec = pl.BlockSpec((None, rows, columns), lambda i: (m, i, 0))
+def fill(whole, count, m, gathered, parts=1, k=0):
+    height, columns = gathered.shape[0] // parts, gathered.shape[1]
+    rows = height // lax.axis_size("tensor") if parts > 1 else min(256, height)
     kept = [] if whole is None else [whole]
     return pl.pallas_call(
         fill_kernel,
         grid=(height // rows,),
-        in_specs=[pl.BlockSpec((rows, columns), lambda i: (i, 0))]
+        in_specs=[pl.BlockSpec((rows, columns), lambda i: (i * parts + k, 0))]
         + [pl.BlockSpec(memory_space=pl.ANY)] * len(kept),
-        out_specs=spec,
-        out_shape=jax.ShapeDtypeStruct((count, height, columns), part.dtype),
+        out_specs=pl.BlockSpec((None, rows, columns), lambda i: (m, i, 0)),
+        out_shape=jax.ShapeDtypeStruct((count, height, columns), gathered.dtype),
         input_output_aliases={1: 0} if kept else {},
         compiler_params=limits(),
         name="fill",
-    )(part, *kept)
+    )(gathered, *kept)
 
 
 def conv_kernel(
@@ -890,7 +889,8 @@
     small = pick_rows(small.reshape(n_owner, -1, inner), inverse_order)
     xproj_low = small[:, :n_x].reshape(n_owner * n_x, inner)
     step_low = small[:, n_x : n_x + n_s].reshape(n_owner * n_s, inner)
-    gate_own, out_own = in_own[:, inner:], outproj_weight.astype(LOW)
+    gate_own = in_own[:, inner:]
+    out_own = after(outproj_weight.astype(LOW), conv_low[-1])
 
     taps = channel_table[:K]
     conv_bias = channel_table[K]
@@ -1023,15 +1023,20 @@
     shard_out, _ = scatter(part_out, [middle])
     shard_gate, _ = scatter(part_gate, [middle])
     weight_sq = vector([jnp.sum(jnp.square(after(w, middle))) for w in all_weights]) * shares
-    mixed = mixed + [line_gather(after(own, partial[-1])) for own in own_mixed[1:]]
-    whole_mixed = token_grad = None
-    for m in every:
-        whole_mixed = fill(whole_mixed, micro, m, after(mixed[m], middle))
-        token_grad = fill(token_grad, micro, m, line_gather(tokens_out[m]))
-        token_first = token_grad if m == 0 else token_first
+    group = own_mixed[1:] + tokens_out[:-1]
+    whole_mixed = fill(None, micro, 0, after(mixed[0], middle))
+    token_grad = None
+    if group:
+        group_all, parts_all = line_gather(jnp.concatenate(group, axis=0)), len(group)
+    for m in range(1, micro):
+        whole_mixed = fill(whole_mixed, micro, m, group_all, parts_all, m - 1)
+    for m in range(micro - 1):
+        token_grad = fill(token_grad, micro, m, group_all, parts_all, micro - 1 + m)
+    token_first = whole_mixed if token_grad is None else token_grad
+    token_last = line_gather(tokens_out[-1])
     mixed = whole_mixed.reshape(tokens.shape)
-    token_grad = token_grad.reshape(tokens.shape)
-    pre_lows, proj_grads = after_all(pre_lows, middle), after_all(proj_grads, middle)
+    pre_lows = after_all(pre_lows, middle, tokens_out[0])
+    proj_grads = after_all(proj_grads, middle, tokens_out[0])
     part_step = over_micros(rank_low, pre_lows)
     part_xproj = over_micros(proj_grads, values)
     part_small = jnp.concatenate(
@@ -1118,6 +1123,8 @@
         second = inverse_rows[ends[i] : ends[i + 1]].reshape(shape) * lax.rsqrt(col_news[i])[None]
         new_weights.append(weights[i] - stride[i + 1] * matrices[i] * second)
     new_weights.append(channel_table - stride[5] * table_update)
+    token_last = after(token_last, *new_weights)
+    token_grad = fill(token_grad, micro, micro - 1, token_last).reshape(tokens.shape)
     return (
         mixed,
         token_grad,

time: 620 us -> 612 us (0.987)
  matrix products: 107 us -> 95.8 us
  other arithmetic: 82.6 us -> 88.9 us
    all_gather x4 -> x3, waiting for transfers between devices: 27.6 us -> 12.9 us  [line_gather(): return lax.all_gather(own, 'tensor', axis=0, tiled=True)]
    ppermute x57, waiting for transfers between devices: 67.6 us -> 79.2 us  [swap(): lax.ppermute(block, axis, [(i, i ^ bit) for i in range(lax.axis_size(axis...]
    dot_general x46, matrix products: 107 us -> 95.8 us  [dot(): lax.dot_general(a, b, (dims, ((), ())), preferred_element_type=FULL)]
    unnamed x285 -> x282, local copies, waits for them, and re-layouts: 13.7 us -> 14.3 us
  transfers between devices with their start and end apart: 69 -> 68, of which waited for: 27 -> 30; matrix products, arithmetic and copies ran while one was open for 35% -> 34% of each run, Pallas kernels for 28% -> 28%
where the time goes in v5:
time: 612 us; the launch traced here: 602 us
  Pallas kernels  199 us (33%)
  matrix products  95.8 us (16%)
  waiting for transfers between devices  94.3 us (15%)
  other arithmetic  88.9 us (15%)
  starting transfers between devices  65.7 us (11%)
  local copies, waits for them, and re-layouts  41.9 us (7%)
  between operations  16.8 us (3%)
    dot_general x46, matrix products, dot(): lax.dot_general(a, b, (dims, ((), ())), preferred_element_type=FULL)  95.8 us
    ppermute x57, waiting for transfers between devices, swap(): lax.ppermute(block, axis, [(i, i ^ bit) for i in range(lax.axis_size(axis...  79.2 us
    pallas_call x2, Pallas kernels, scan_backward(): pl.pallas_call(functools.partial(backward_kernel, rows, groups, tile, 8,...  64.6 us
    ppermute x57, starting transfers between devices, swap(): lax.ppermute(block, axis, [(i, i ^ bit) for i in range(lax.axis_size(axis...  57.6 us
    pallas_call x2, Pallas kernels, scan_forward(): pl.pallas_call(functools.partial(forward_kernel, rows, groups, tile, 8, 4...  51.2 us
    pallas_call x2, Pallas kernels, scan_edge(): pl.pallas_call(functools.partial(edge_kernel, rows, groups, tile, 4), gri...  23.2 us
    pallas_call x2, Pallas kernels, conv_backward(): pl.pallas_call(conv_kernel, grid=(channels // width,), in_specs=[tall, pl...  14.4 us
    unnamed x282, local copies, waits for them, and re-layouts  14.3 us
  transfers between devices with their start and end apart: 68, of which 30 were waited for; matrix products, arithmetic and copies ran while one was open for 34% of the time, Pallas kernels for 28%

profile of v5, /device:TPU:0, one launch (start us, length us, event | category | flops | bytes accessed | tf_op | source)
XLA Modules:
  0.0 601.9 jit_solution(13853875870111105942)
XLA Ops:
  22.9 5.7 normalize.3
  28.5 5.7 normalize.2
  37.7 6.4 %collective-permute-done.6 = bf16[160,1024]{1,0:T(8,128)(2,1)S(1)} collective-permute-done((bf16[160,1024]{1,0:T(8,128)(2,1)S(1)}, bf16[160,1024]{1,0:T(8,128)(2,1)S(1)}, u32[]{:S(2)}, u32[]{:S(2)}) %collective-permute-start.6) | collective-permute-done | bytes 327712 | tf_op jit(solution)/shard_map/ppermute | solution.py:48
  82.2 6.4 %collective-permute-done.13 = bf16[512,160]{1,0:T(8,128)(2,1)S(1)} collective-permute-done((bf16[512,160]{1,0:T(8,128)(2,1)S(1)}, bf16[512,160]{1,0:T(8,128)(2,1)S(1)}, u32[]{:S(2)}, u32[]{:S(2)}) %collective-permute-start.13) | collective-permute-done | bytes 163872 | tf_op jit(solution)/shard_map/ppermute | solution.py:48
  95.1 8.6 %collective-permute-done.17 = bf16[256,1024]{1,0:T(8,128)(2,1)S(1)} collective-permute-done((bf16[256,1024]{1,0:T(8,128)(2,1)S(1)}, bf16[256,1024]{1,0:T(8,128)(2,1)S(1)}, u32[]{:S(2)}, u32[]{:S(2)}) %collective-permute-start.17) | collective-permute-done | bytes 524320 | tf_op jit(solution)/shard_map/ppermute | solution.py:48
  108.7 9.8 %collective-permute-done.11 = bf16[512,160]{1,0:T(8,128)(2,1)S(1)} collective-permute-done((bf16[512,160]{1,0:T(8,128)(2,1)S(1)}, bf16[512,160]{1,0:T(8,128)(2,1)S(1)}, u32[]{:S(2)}, u32[]{:S(2)}) %collective-permute-start.11) | collective-permute-done | bytes 163872 | tf_op jit(solution)/shard_map/ppermute | solution.py:48
  133.4 11.6 %scan_edge.2 = f32[16,8,128]{2,1,0:T(8,128)} custom-call(s32[1]{0:T(128)} %bitcast.30.flag, f32[512,1024]{1,0:T(8,128)} %compare_select_fusion.1.size_ref, bf16[512,1024]{1,0:T(8,128)(2,1)} %copy-done.19, f32[512,1024]{1,0:T(8,128)} %convolution_add_fusion.1.grad_ref, bf16[512,1024]{1,0:T(8,128)(2,1)} %add_convert_fusion.14.gate_ref, ...), custom_call_target="tpu_custom_call" | custom-call | flops 6710886400 | bytes 6291456 | tf_op jit(solution)/shard_map/scan_edge/pallas_call | solution.py:447
  147.2 25.6 %scan_forward.2 = (bf16[512,1024]{1,0:T(8,128)(2,1)}, bf16[512,1024]{1,0:T(8,128)(2,1)}, f32[512,16,8,128]{3,2,1,0:T(8,128)}, f32[512,128]{1,0:T(8,128)}, f32[1,1024]{1,0:T(1,128)}) custom-call(f32[512,1024]{1,0:T(8,128)} %compare_select_fusion.1.size_ref, bf16[512,1024]{1,0:T(8,128)(2,1)} %copy-done.19, f32[512,1024]{1,0:T(8,128)} %convolution_add_fusion.1.grad_ref, ...), custom_call_target="tpu_custom_call" | custom-call | flops 12582912000 | bytes 41943040 | tf_op jit(solution)/shard_map/scan_forward/pallas_call | solution.py:471
  190.7 11.6 %scan_edge.3 = f32[16,8,128]{2,1,0:T(8,128)} custom-call(s32[1]{0:T(128)} %bitcast.30.flag, f32[512,1024]{1,0:T(8,128)} %compare_select_fusion.size_ref, bf16[512,1024]{1,0:T(8,128)(2,1)} %copy-done.21, f32[512,1024]{1,0:T(8,128)} %convolution_add_fusion.grad_ref, bf16[512,1024]{1,0:T(8,128)(2,1)} %add_convert_fusion.13.gate_ref, ...), custom_call_target="tpu_custom_call" | custom-call | flops 6710886400 | bytes 6291456 | tf_op jit(solution)/shard_map/scan_edge/pallas_call | solution.py:447
  204.7 25.6 %scan_forward.3 = (bf16[512,1024]{1,0:T(8,128)(2,1)}, bf16[512,1024]{1,0:T(8,128)(2,1)}, f32[512,16,8,128]{3,2,1,0:T(8,128)}, f32[512,128]{1,0:T(8,128)}, f32[1,1024]{1,0:T(1,128)}) custom-call(f32[512,1024]{1,0:T(8,128)} %compare_select_fusion.size_ref, bf16[512,1024]{1,0:T(8,128)(2,1)} %copy-done.21, f32[512,1024]{1,0:T(8,128)} %convolution_add_fusion.grad_ref, ...), custom_call_target="tpu_custom_call" | custom-call | flops 12582912000 | bytes 41943040 | tf_op jit(solution)/shard_map/scan_forward/pallas_call | solution.py:471
  240.3 31.9 %scan_backward.2 = (bf16[512,1024]{1,0:T(8,128)(2,1)}, f32[512,1024]{1,0:T(8,128)}, f32[512,128]{1,0:T(8,128)}, f32[16,8,128]{2,1,0:T(8,128)}, f32[1,1024]{1,0:T(1,128)}) custom-call(f32[512,1024]{1,0:T(8,128)} %compare_select_fusion.1.size_ref, bf16[512,1024]{1,0:T(8,128)(2,1)} %copy-done.19, f32[512,1024]{1,0:T(8,128)} %convolution_add_fusion.1.grad_ref, ...), custom_call_target="tpu_custom_call" | custom-call | flops 16777216000 | bytes 41943040 | tf_op jit(solution)/shard_map/scan_backward/pallas_call | solution.py:512
  283.8 5.7 collective-permute-start.25
  289.9 4.5 fusion.120
  309.8 32.7 %scan_backward.3 = (bf16[512,1024]{1,0:T(8,128)(2,1)}, f32[512,1024]{1,0:T(8,128)}, f32[512,128]{1,0:T(8,128)}, f32[16,8,128]{2,1,0:T(8,128)}, f32[1,1024]{1,0:T(1,128)}) custom-call(f32[512,1024]{1,0:T(8,128)} %compare_select_fusion.size_ref, bf16[512,1024]{1,0:T(8,128)(2,1)} %copy-done.21, f32[512,1024]{1,0:T(8,128)} %convolution_add_fusion.grad_ref, ...), custom_call_target="tpu_custom_call" | custom-call | flops 16777216000 | bytes 41943040 | tf_op jit(solution)/shard_map/scan_backward/pallas_call | solution.py:512
  346.8 7.3 %conv_backward.2 = (bf16[512,1024]{1,0:T(8,128)(2,1)}, f32[8,1024]{1,0:T(8,128)}, f32[8,1024]{1,0:T(8,128)}, f32[8,1024]{1,0:T(8,128)}) custom-call(f32[512,1024]{1,0:T(8,128)} %get-tuple-element.168.value_grad_ref, bf16[512,160]{1,0:T(8,128)(2,1)} %add_convert_fusion.17.proj_ref, bf16[160,1024]{1,0:T(8,128)(2,1)} %copy-done.48, ...), custom_call_target="tpu_custom_call" | custom-call | tf_op jit(solution)/shard_map/conv_backward/pallas_call | solution.py:811
  367.3 5.7 collective-permute-done.29
  386.7 7.2 %conv_backward.3 = (bf16[512,1024]{1,0:T(8,128)(2,1)}, f32[8,1024]{1,0:T(8,128)}, f32[8,1024]{1,0:T(8,128)}, f32[8,1024]{1,0:T(8,128)}) custom-call(f32[512,1024]{1,0:T(8,128)} %get-tuple-element.183.value_grad_ref, bf16[512,160]{1,0:T(8,128)(2,1)} %fusion.80.proj_ref, bf16[160,1024]{1,0:T(8,128)(2,1)} %copy-done.48, bf16[512,1024]{1,0:T(8,128)(2,1)} %copy-done.17, ...), custom_call_target="tpu_custom_call" | custom-call | tf_op jit(solution)/shard_map/conv_backward/pallas_call | solution.py:811
  434.0 6.6 %collective-permute-done.37 = bf16[2,256,512]{2,1,0:T(8,128)(2,1)} collective-permute-done((bf16[2,256,512]{2,1,0:T(8,128)(2,1)}, bf16[2,256,512]{2,1,0:T(8,128)(2,1)}, u32[]{:S(2)}, u32[]{:S(2)}) %collective-permute-start.37) | collective-permute-done | bytes 524320 | tf_op jit(solution)/shard_map/ppermute | solution.py:48
  463.7 4.4 fusion.77
  471.7 5.2 collective-permute-done.49
  505.0 4.2 collective-permute-done.51
  542.9 3.8 fill.6.refs_0_
  559.5 3.8 fill.5
  578.8 10.2 %all-gather.8.cloned.1.call-done.part_ref = bf16[512,2048]{1,0:T(8,128)(2,1)} async-done(((bf16[128,2048]{1,0:T(8,128)(2,1)}), bf16[512,2048]{1,0:T(8,128)(2,1)}) %all-gather.8.cloned.1.call-update) | async-done | bytes 2097168 | tf_op jit(solution)/shard_map/all_gather | solution.py:148
  (641 shorter events, 335.1 us)
Async XLA Ops:
  7.2 230.2 %reduce-scatter.7.cloned.1.call-start = ((), (), s32[]{:S(2)}) async-start(), calls=%async_computation.5 | async-start | bytes 2621440 | tf_op jit(solution)/shard_map/reduce_scatter | solution.py:144
  45.6 22.5 %collective-permute-start.20 = (bf16[256,1024]{1,0:T(8,128)(2,1)}, bf16[256,1024]{1,0:T(8,128)(2,1)}, u32[]{:S(2)}, u32[]{:S(2)}) collective-permute-start(bf16[256,1024]{1,0:T(8,128)(2,1)} %get-tuple-element.351), channel_id=1, source_target_pairs={{0,16},{8,24},{16,0},{24,8},{1,17},{9,25},{17,1},{25,9},{2,18},{10... | collective-permute-start | bytes 1572872 | tf_op jit(solution)/shard_map/ppermute | solution.py:48
  47.4 44.7 %collective-permute-start.19 = (bf16[256,1024]{1,0:T(8,128)(2,1)}, bf16[256,1024]{1,0:T(8,128)(2,1)}, u32[]{:S(2)}, u32[]{:S(2)}) collective-permute-start(bf16[256,1024]{1,0:T(8,128)(2,1)} %get-tuple-element.351), channel_id=1, source_target_pairs={{0,8},{8,0},{16,24},{24,16},{1,9},{9,1},{17,25},{25,17},{2,10},{10... | collective-permute-start | bytes 1572872 | tf_op jit(solution)/shard_map/ppermute | solution.py:48
  67.5 21.1 %collective-permute-start.15 = (bf16[256,1024]{1,0:T(8,128)(2,1)S(1)}, bf16[256,1024]{1,0:T(8,128)(2,1)S(1)}, u32[]{:S(2)}, u32[]{:S(2)}) collective-permute-start(bf16[256,1024]{1,0:T(8,128)(2,1)S(1)} %copy-done.55), channel_id=1, source_target_pairs={{0,8},{8,0},{16,24},{24,16},{1,9},{9,1},{17,25},{25,17},{2,10},{10... | collective-permute-start | bytes 1572872 | tf_op jit(solution)/shard_map/ppermute | solution.py:48
  68.1 23.9 %collective-permute-start.21 = (bf16[256,1024]{1,0:T(8,128)(2,1)}, bf16[256,1024]{1,0:T(8,128)(2,1)S(1)}, u32[]{:S(2)}, u32[]{:S(2)}) collective-permute-start(bf16[256,1024]{1,0:T(8,128)(2,1)} %collective-permute-done.20), channel_id=1, source_target_pairs={{0,8},{8,0},{16,24},{24,16},{1,9},{9,1},{17,25},{25,17},{2,10},{10... | collective-permute-start | bytes 1572872 | tf_op jit(solution)/shard_map/ppermute | solution.py:48
  93.6 31.0 %collective-permute-start.22 = (bf16[1024,1024]{1,0:T(8,128)(2,1)S(1)}, bf16[1024,1024]{1,0:T(8,128)(2,1)S(1)}, u32[]{:S(2)}, u32[]{:S(2)}) collective-permute-start(bf16[1024,1024]{1,0:T(8,128)(2,1)S(1)} %pad_maximum_fusion.1), channel_id=1, source_target_pairs={{0,4},{4,0},{1,5},{5,1},{2,6},{6,2},{3,7},{7,3},{8,12},{12,8},{9,1... | collective-permute-start | bytes 6291464 | tf_op jit(solution)/shard_map/ppermute | solution.py:48
  103.8 25.0 %collective-permute-start.18 = (bf16[1024,1024]{1,0:T(8,128)(2,1)S(1)}, bf16[1024,1024]{1,0:T(8,128)(2,1)S(1)}, u32[]{:S(2)}, u32[]{:S(2)}) collective-permute-start(bf16[1024,1024]{1,0:T(8,128)(2,1)S(1)} %constant_dynamic-update-slice_fusion.5), channel_id=1, source_target_pairs={{0,4},{4,0},{1,5},{5,1},{2,6},{6,2},{3,7},{7,3},{8,12},{12,8},{9,1... | collective-permute-start | bytes 6291464 | tf_op jit(solution)/shard_map/ppermute | solution.py:48
  118.5 26.4 %collective-permute-start.12 = (bf16[512,160]{1,0:T(8,128)(2,1)S(1)}, bf16[512,160]{1,0:T(8,128)(2,1)S(1)}, u32[]{:S(2)}, u32[]{:S(2)}) collective-permute-start(bf16[512,160]{1,0:T(8,128)(2,1)S(1)} %add_convert_fusion.18), channel_id=1, source_target_pairs={{0,2},{1,3},{2,0},{3,1},{4,6},{5,7},{6,4},{7,5},{8,10},{9,11},{10,... | collective-permute-start | bytes 491528 | tf_op jit(solution)/shard_map/ppermute | solution.py:48
  178.4 116.0 %reduce-scatter.5.cloned.1.call-start = ((), (), s32[]{:S(2)}) async-start(), calls=%async_computation.4 | async-start | bytes 2621440 | tf_op jit(solution)/shard_map/reduce_scatter | solution.py:144
  235.8 111.0 %all-gather.4.cloned.1.call-start = ((), (), s32[]{:S(2)}) async-start(), calls=%async_computation.6 | async-start | bytes 2621440 | tf_op jit(solution)/shard_map/all_gather | solution.py:148
  280.5 26.3 %collective-permute-start.46 = (bf16[1024,1024]{1,0:T(8,128)(2,1)}, bf16[1024,1024]{1,0:T(8,128)(2,1)}, u32[]{:S(2)}, u32[]{:S(2)}) collective-permute-start(bf16[1024,1024]{1,0:T(8,128)(2,1)} %add_convert_fusion.7), channel_id=1, source_target_pairs={{0,4},{4,0},{1,5},{5,1},{2,6},{6,2},{3,7},{7,3},{8,12},{12,8},{9,1... | collective-permute-start | bytes 6291464 | tf_op jit(solution)/shard_map/ppermute | solution.py:48
  289.4 133.4 %reduce-scatter.9.cloned.1.call-start = ((), (), s32[]{:S(2)}) async-start(), calls=%async_computation.7 | async-start | bytes 2621440 | tf_op jit(solution)/shard_map/reduce_scatter | solution.py:144
  303.3 42.8 %collective-permute-start.26 = (bf16[512,160]{1,0:T(8,128)(2,1)S(1)}, bf16[512,160]{1,0:T(8,128)(2,1)S(1)}, u32[]{:S(2)}, u32[]{:S(2)}) collective-permute-start(bf16[512,160]{1,0:T(8,128)(2,1)S(1)} %fusion.79), channel_id=1, source_target_pairs={{0,2},{1,3},{2,0},{3,1},{4,6},{5,7},{6,4},{7,5},{8,10},{9,11},{10,... | collective-permute-start | bytes 491528 | tf_op jit(solution)/shard_map/ppermute | solution.py:48
  373.0 126.8 %reduce-scatter.11.cloned.1.call-start = ((), (), s32[]{:S(2)}) async-start(), calls=%async_computation.9 | async-start | bytes 2621440 | tf_op jit(solution)/shard_map/reduce_scatter | solution.py:144
  406.3 136.6 %all-gather.6.cloned.1.call-start = ((), (), s32[]{:S(2)}) async-start(), calls=%async_computation.8 | async-start | bytes 5242880 | tf_op jit(solution)/shard_map/all_gather | solution.py:148
  414.3 40.0 %collective-permute-start.47 = (bf16[2,256,512]{2,1,0:T(8,128)(2,1)}, bf16[2,256,512]{2,1,0:T(8,128)(2,1)S(1)}, u32[]{:S(2)}, u32[]{:S(2)}) collective-permute-start(bf16[2,256,512]{2,1,0:T(8,128)(2,1)} %pad_maximum_fusion.16), channel_id=1, source_target_pairs={{0,8},{8,0},{16,24},{24,16},{1,9},{9,1},{17,25},{25,17},{2,10},{10... | collective-permute-start | bytes 1572872 | tf_op jit(solution)/shard_map/ppermute | solution.py:48
  414.7 40.2 %collective-permute-start.48 = (bf16[2,256,512]{2,1,0:T(8,128)(2,1)}, bf16[2,256,512]{2,1,0:T(8,128)(2,1)}, u32[]{:S(2)}, u32[]{:S(2)}) collective-permute-start(bf16[2,256,512]{2,1,0:T(8,128)(2,1)} %slice.581), channel_id=1, source_target_pairs={{0,16},{8,24},{16,0},{24,8},{1,17},{9,25},{17,1},{25,9},{2,18},{10... | collective-permute-start | bytes 1572872 | tf_op jit(solution)/shard_map/ppermute | solution.py:48
  417.9 22.7 %collective-permute-start.37 = (bf16[2,256,512]{2,1,0:T(8,128)(2,1)}, bf16[2,256,512]{2,1,0:T(8,128)(2,1)}, u32[]{:S(2)}, u32[]{:S(2)}) collective-permute-start(bf16[2,256,512]{2,1,0:T(8,128)(2,1)} %pad_maximum_fusion.15), channel_id=1, source_target_pairs={{0,8},{8,0},{16,24},{24,16},{1,9},{9,1},{17,25},{25,17},{2,10},{10... | collective-permute-start | bytes 1572872 | tf_op jit(solution)/shard_map/ppermute | solution.py:48
  418.5 22.5 %collective-permute-start.38 = (bf16[2,256,512]{2,1,0:T(8,128)(2,1)}, bf16[2,256,512]{2,1,0:T(8,128)(2,1)}, u32[]{:S(2)}, u32[]{:S(2)}) collective-permute-start(bf16[2,256,512]{2,1,0:T(8,128)(2,1)} %slice.557), channel_id=1, source_target_pairs={{0,16},{8,24},{16,0},{24,8},{1,17},{9,25},{17,1},{25,9},{2,18},{10... | collective-permute-start | bytes 1572872 | tf_op jit(solution)/shard_map/ppermute | solution.py:48
  428.6 160.4 %all-gather.8.cloned.1.call-start = ((), (), s32[]{:S(2)}) async-start(), calls=%async_computation.10 | async-start | bytes 2621440 | tf_op jit(solution)/shard_map/all_gather | solution.py:148
  433.3 52.7 %collective-permute-start.32 = (bf16[2,256,512]{2,1,0:T(8,128)(2,1)}, bf16[2,256,512]{2,1,0:T(8,128)(2,1)}, u32[]{:S(2)}, u32[]{:S(2)}) collective-permute-start(bf16[2,256,512]{2,1,0:T(8,128)(2,1)} %pad_maximum_fusion.14), channel_id=1, source_target_pairs={{0,8},{8,0},{16,24},{24,16},{1,9},{9,1},{17,25},{25,17},{2,10},{10... | collective-permute-start | bytes 1572872 | tf_op jit(solution)/shard_map/ppermute | solution.py:48
  440.6 45.4 %collective-permute-start.33 = (bf16[2,256,512]{2,1,0:T(8,128)(2,1)}, bf16[2,256,512]{2,1,0:T(8,128)(2,1)}, u32[]{:S(2)}, u32[]{:S(2)}) collective-permute-start(bf16[2,256,512]{2,1,0:T(8,128)(2,1)} %slice.546), channel_id=1, source_target_pairs={{0,16},{8,24},{16,0},{24,8},{1,17},{9,25},{17,1},{25,9},{2,18},{10... | collective-permute-start | bytes 1572872 | tf_op jit(solution)/shard_map/ppermute | solution.py:48
  446.2 22.1 %collective-permute-start.39 = (bf16[256,512]{1,0:T(8,128)(2,1)}, bf16[256,512]{1,0:T(8,128)(2,1)}, u32[]{:S(2)}, u32[]{:S(2)}) collective-permute-start(bf16[256,512]{1,0:T(8,128)(2,1)} %get-tuple-element.343), channel_id=1, source_target_pairs={{0,16},{8,24},{16,0},{24,8},{1,17},{9,25},{17,1},{25,9},{2,18},{10... | collective-permute-start | bytes 786440 | tf_op jit(solution)/shard_map/ppermute | solution.py:48
  455.1 23.0 %collective-permute-start.41 = (bf16[192,1024]{1,0:T(8,128)(2,1)S(1)}, bf16[192,1024]{1,0:T(8,128)(2,1)S(1)}, u32[]{:S(2)}, u32[]{:S(2)}) collective-permute-start(bf16[192,1024]{1,0:T(8,128)(2,1)S(1)} %bitcast.281), channel_id=1, source_target_pairs={{0,4},{4,0},{1,5},{5,1},{2,6},{6,2},{3,7},{7,3},{8,12},{12,8},{9,1... | collective-permute-start | bytes 1179656 | tf_op jit(solution)/shard_map/ppermute | solution.py:48
  (181 other events, 1316.9 us)
Sparse Core Ops, SparseCore 0:
  178.5 47.9 reduce-scatter.6
  235.9 47.8 reduce-scatter.4
  289.6 56.3 all-gather.3
  373.1 41.6 reduce-scatter.8
  417.6 43.1 reduce-scatter.10
  462.3 80.5 all-gather.5
  544.5 44.5 all-gather.7

commit v6 on v5

--- a/solution.py
+++ b/solution.py
@@ -749,7 +749,7 @@
 
 def fill(whole, count, m, gathered, parts=1, k=0):
     height, columns = gathered.shape[0] // parts, gathered.shape[1]
-    rows = height // lax.axis_size("tensor") if parts > 1 else min(256, height)
+    rows = height // lax.axis_size("tensor") if parts > 1 else min(512, height)
     kept = [] if whole is None else [whole]
     return pl.pallas_call(
         fill_kernel,
@@ -883,7 +883,7 @@
     pad_rows = -(owned + n_x + n_s) % 64
     if pad_rows:
         first_own.append(jnp.zeros((pad_rows, inner), LOW))
-    blocks = fetch(after(jnp.concatenate(first_own, axis=0), gain_row), [n[0] for n in normed])
+    blocks = fetch(after(jnp.concatenate(first_own, axis=0), gain_row), [normed[0][0]])
     conv_low = join([block[:owned] for block in blocks])
     small = jnp.concatenate(join([block[owned:] for block in blocks]), axis=0)
     small = pick_rows(small.reshape(n_owner, -1, inner), inverse_order)

time: 612 us -> 616 us (level)
  transfers between devices with their start and end apart: 68 -> 68, of which waited for: 30 -> 33; matrix products, arithmetic and copies ran while one was open for 34% -> 34% of each run, Pallas kernels for 28% -> 28%
where the time goes in v6:
time: 616 us; the launch traced here: 605 us
  Pallas kernels  199 us (32%)
  waiting for transfers between devices  96.4 us (16%)
  matrix products  95.8 us (16%)
  other arithmetic  88 us (14%)
  starting transfers between devices  67.8 us (11%)
  local copies, waits for them, and re-layouts  41.2 us (7%)
  between operations  16.8 us (3%)
    dot_general x46, matrix products, dot(): lax.dot_general(a, b, (dims, ((), ())), preferred_element_type=FULL)  95.8 us
    ppermute x57, waiting for transfers between devices, swap(): lax.ppermute(block, axis, [(i, i ^ bit) for i in range(lax.axis_size(axis...  81.5 us
    pallas_call x2, Pallas kernels, scan_backward(): pl.pallas_call(functools.partial(backward_kernel, rows, groups, tile, 8,...  64.6 us
    ppermute x57, starting transfers between devices, swap(): lax.ppermute(block, axis, [(i, i ^ bit) for i in range(lax.axis_size(axis...  59.7 us
    pallas_call x2, Pallas kernels, scan_forward(): pl.pallas_call(functools.partial(forward_kernel, rows, groups, tile, 8, 4...  51.2 us
    pallas_call x2, Pallas kernels, scan_edge(): pl.pallas_call(functools.partial(edge_kernel, rows, groups, tile, 4), gri...  23.2 us
    pallas_call x2, Pallas kernels, conv_backward(): pl.pallas_call(conv_kernel, grid=(channels // width,), in_specs=[tall, pl...  14.5 us
    unnamed x282, local copies, waits for them, and re-layouts  14.2 us
  transfers between devices with their start and end apart: 68, of which 33 were waited for; matrix products, arithmetic and copies ran while one was open for 34% of the time, Pallas kernels for 28%

profile of v6, /device:TPU:0, one launch (start us, length us, event | category | flops | bytes accessed | tf_op | source)
XLA Modules:
  0.0 605.0 jit_solution(11307299907244479631)
XLA Ops:
  22.9 5.7 normalize.3
  28.6 5.5 collective-permute-done.3
  48.6 5.7 normalize.2
  85.0 5.4 collective-permute-done.13
  96.9 8.6 %collective-permute-done.17 = bf16[256,1024]{1,0:T(8,128)(2,1)S(1)} collective-permute-done((bf16[256,1024]{1,0:T(8,128)(2,1)S(1)}, bf16[256,1024]{1,0:T(8,128)(2,1)S(1)}, u32[]{:S(2)}, u32[]{:S(2)}) %collective-permute-start.17) | collective-permute-done | bytes 524320 | tf_op jit(solution)/shard_map/ppermute | solution.py:48
  110.5 9.8 %collective-permute-done.11 = bf16[512,160]{1,0:T(8,128)(2,1)S(1)} collective-permute-done((bf16[512,160]{1,0:T(8,128)(2,1)S(1)}, bf16[512,160]{1,0:T(8,128)(2,1)S(1)}, u32[]{:S(2)}, u32[]{:S(2)}) %collective-permute-start.11) | collective-permute-done | bytes 163872 | tf_op jit(solution)/shard_map/ppermute | solution.py:48
  135.1 11.6 %scan_edge.2 = f32[16,8,128]{2,1,0:T(8,128)} custom-call(s32[1]{0:T(128)} %bitcast.30.flag, f32[512,1024]{1,0:T(8,128)} %compare_select_fusion.1.size_ref, bf16[512,1024]{1,0:T(8,128)(2,1)} %copy-done.19, f32[512,1024]{1,0:T(8,128)} %convolution_add_fusion.1.grad_ref, bf16[512,1024]{1,0:T(8,128)(2,1)} %add_convert_fusion.14.gate_ref, ...), custom_call_target="tpu_custom_call" | custom-call | flops 6710886400 | bytes 6291456 | tf_op jit(solution)/shard_map/scan_edge/pallas_call | solution.py:447
  149.0 25.6 %scan_forward.2 = (bf16[512,1024]{1,0:T(8,128)(2,1)}, bf16[512,1024]{1,0:T(8,128)(2,1)}, f32[512,16,8,128]{3,2,1,0:T(8,128)}, f32[512,128]{1,0:T(8,128)}, f32[1,1024]{1,0:T(1,128)}) custom-call(f32[512,1024]{1,0:T(8,128)} %compare_select_fusion.1.size_ref, bf16[512,1024]{1,0:T(8,128)(2,1)} %copy-done.19, f32[512,1024]{1,0:T(8,128)} %convolution_add_fusion.1.grad_ref, ...), custom_call_target="tpu_custom_call" | custom-call | flops 12582912000 | bytes 41943040 | tf_op jit(solution)/shard_map/scan_forward/pallas_call | solution.py:471
  192.5 11.6 %scan_edge.3 = f32[16,8,128]{2,1,0:T(8,128)} custom-call(s32[1]{0:T(128)} %bitcast.30.flag, f32[512,1024]{1,0:T(8,128)} %compare_select_fusion.size_ref, bf16[512,1024]{1,0:T(8,128)(2,1)} %copy-done.21, f32[512,1024]{1,0:T(8,128)} %convolution_add_fusion.grad_ref, bf16[512,1024]{1,0:T(8,128)(2,1)} %add_convert_fusion.13.gate_ref, ...), custom_call_target="tpu_custom_call" | custom-call | flops 6710886400 | bytes 6291456 | tf_op jit(solution)/shard_map/scan_edge/pallas_call | solution.py:447
  206.5 25.6 %scan_forward.3 = (bf16[512,1024]{1,0:T(8,128)(2,1)}, bf16[512,1024]{1,0:T(8,128)(2,1)}, f32[512,16,8,128]{3,2,1,0:T(8,128)}, f32[512,128]{1,0:T(8,128)}, f32[1,1024]{1,0:T(1,128)}) custom-call(f32[512,1024]{1,0:T(8,128)} %compare_select_fusion.size_ref, bf16[512,1024]{1,0:T(8,128)(2,1)} %copy-done.21, f32[512,1024]{1,0:T(8,128)} %convolution_add_fusion.grad_ref, ...), custom_call_target="tpu_custom_call" | custom-call | flops 12582912000 | bytes 41943040 | tf_op jit(solution)/shard_map/scan_forward/pallas_call | solution.py:471
  242.0 31.9 %scan_backward.2 = (bf16[512,1024]{1,0:T(8,128)(2,1)}, f32[512,1024]{1,0:T(8,128)}, f32[512,128]{1,0:T(8,128)}, f32[16,8,128]{2,1,0:T(8,128)}, f32[1,1024]{1,0:T(1,128)}) custom-call(f32[512,1024]{1,0:T(8,128)} %compare_select_fusion.1.size_ref, bf16[512,1024]{1,0:T(8,128)(2,1)} %copy-done.19, f32[512,1024]{1,0:T(8,128)} %convolution_add_fusion.1.grad_ref, ...), custom_call_target="tpu_custom_call" | custom-call | flops 16777216000 | bytes 41943040 | tf_op jit(solution)/shard_map/scan_backward/pallas_call | solution.py:512
  285.5 5.3 collective-permute-start.25
  291.3 4.5 fusion.120
  304.5 4.1 collective-permute-start.26
  311.5 32.7 %scan_backward.3 = (bf16[512,1024]{1,0:T(8,128)(2,1)}, f32[512,1024]{1,0:T(8,128)}, f32[512,128]{1,0:T(8,128)}, f32[16,8,128]{2,1,0:T(8,128)}, f32[1,1024]{1,0:T(1,128)}) custom-call(f32[512,1024]{1,0:T(8,128)} %compare_select_fusion.size_ref, bf16[512,1024]{1,0:T(8,128)(2,1)} %copy-done.21, f32[512,1024]{1,0:T(8,128)} %convolution_add_fusion.grad_ref, ...), custom_call_target="tpu_custom_call" | custom-call | flops 16777216000 | bytes 41943040 | tf_op jit(solution)/shard_map/scan_backward/pallas_call | solution.py:512
  348.6 7.3 %conv_backward.2 = (bf16[512,1024]{1,0:T(8,128)(2,1)}, f32[8,1024]{1,0:T(8,128)}, f32[8,1024]{1,0:T(8,128)}, f32[8,1024]{1,0:T(8,128)}) custom-call(f32[512,1024]{1,0:T(8,128)} %get-tuple-element.168.value_grad_ref, bf16[512,160]{1,0:T(8,128)(2,1)} %add_convert_fusion.17.proj_ref, bf16[160,1024]{1,0:T(8,128)(2,1)} %copy-done.48, ...), custom_call_target="tpu_custom_call" | custom-call | tf_op jit(solution)/shard_map/conv_backward/pallas_call | solution.py:811
  369.1 5.7 collective-permute-done.29
  388.6 7.2 %conv_backward.3 = (bf16[512,1024]{1,0:T(8,128)(2,1)}, f32[8,1024]{1,0:T(8,128)}, f32[8,1024]{1,0:T(8,128)}, f32[8,1024]{1,0:T(8,128)}) custom-call(f32[512,1024]{1,0:T(8,128)} %get-tuple-element.183.value_grad_ref, bf16[512,160]{1,0:T(8,128)(2,1)} %fusion.80.proj_ref, bf16[160,1024]{1,0:T(8,128)(2,1)} %copy-done.48, bf16[512,1024]{1,0:T(8,128)(2,1)} %copy-done.17, ...), custom_call_target="tpu_custom_call" | custom-call | tf_op jit(solution)/shard_map/conv_backward/pallas_call | solution.py:811
  436.7 5.8 collective-permute-done.37
  466.4 4.4 fusion.77
  474.5 5.1 collective-permute-done.49
  507.8 4.2 collective-permute-done.51
  562.2 3.8 fill.5
  581.4 10.3 %all-gather.8.cloned.1.call-done.part_ref = bf16[512,2048]{1,0:T(8,128)(2,1)} async-done(((bf16[128,2048]{1,0:T(8,128)(2,1)}), bf16[512,2048]{1,0:T(8,128)(2,1)}) %all-gather.8.cloned.1.call-update) | async-done | bytes 2097168 | tf_op jit(solution)/shard_map/all_gather | solution.py:148
  (641 shorter events, 340.9 us)
Async XLA Ops:
  7.2 232.0 %reduce-scatter.7.cloned.1.call-start = ((), (), s32[]{:S(2)}) async-start(), calls=%async_computation.5 | async-start | bytes 2621440 | tf_op jit(solution)/shard_map/reduce_scatter | solution.py:144
  44.5 25.2 %collective-permute-start.20 = (bf16[256,1024]{1,0:T(8,128)(2,1)}, bf16[256,1024]{1,0:T(8,128)(2,1)}, u32[]{:S(2)}, u32[]{:S(2)}) collective-permute-start(bf16[256,1024]{1,0:T(8,128)(2,1)} %get-tuple-element.351), channel_id=1, source_target_pairs={{0,16},{8,24},{16,0},{24,8},{1,17},{9,25},{17,1},{25,9},{2,18},{10... | collective-permute-start | bytes 1572872 | tf_op jit(solution)/shard_map/ppermute | solution.py:48
  44.8 49.0 %collective-permute-start.19 = (bf16[256,1024]{1,0:T(8,128)(2,1)}, bf16[256,1024]{1,0:T(8,128)(2,1)}, u32[]{:S(2)}, u32[]{:S(2)}) collective-permute-start(bf16[256,1024]{1,0:T(8,128)(2,1)} %get-tuple-element.351), channel_id=1, source_target_pairs={{0,8},{8,0},{16,24},{24,16},{1,9},{9,1},{17,25},{25,17},{2,10},{10... | collective-permute-start | bytes 1572872 | tf_op jit(solution)/shard_map/ppermute | solution.py:48
  69.3 21.1 %collective-permute-start.15 = (bf16[256,1024]{1,0:T(8,128)(2,1)S(1)}, bf16[256,1024]{1,0:T(8,128)(2,1)S(1)}, u32[]{:S(2)}, u32[]{:S(2)}) collective-permute-start(bf16[256,1024]{1,0:T(8,128)(2,1)S(1)} %convert_element_type.396), channel_id=1, source_target_pairs={{0,8},{8,0},{16,24},{24,16},{1,9},{9,1},{17,25},{25,17},{2,10},{10... | collective-permute-start | bytes 1572872 | tf_op jit(solution)/shard_map/ppermute | solution.py:48
  69.7 24.1 %collective-permute-start.21 = (bf16[256,1024]{1,0:T(8,128)(2,1)}, bf16[256,1024]{1,0:T(8,128)(2,1)S(1)}, u32[]{:S(2)}, u32[]{:S(2)}) collective-permute-start(bf16[256,1024]{1,0:T(8,128)(2,1)} %collective-permute-done.20), channel_id=1, source_target_pairs={{0,8},{8,0},{16,24},{24,16},{1,9},{9,1},{17,25},{25,17},{2,10},{10... | collective-permute-start | bytes 1572872 | tf_op jit(solution)/shard_map/ppermute | solution.py:48
  95.4 31.0 %collective-permute-start.22 = (bf16[1024,1024]{1,0:T(8,128)(2,1)S(1)}, bf16[1024,1024]{1,0:T(8,128)(2,1)S(1)}, u32[]{:S(2)}, u32[]{:S(2)}) collective-permute-start(bf16[1024,1024]{1,0:T(8,128)(2,1)S(1)} %pad_maximum_fusion.1), channel_id=1, source_target_pairs={{0,4},{4,0},{1,5},{5,1},{2,6},{6,2},{3,7},{7,3},{8,12},{12,8},{9,1... | collective-permute-start | bytes 6291464 | tf_op jit(solution)/shard_map/ppermute | solution.py:48
  105.6 25.0 %collective-permute-start.18 = (bf16[1024,1024]{1,0:T(8,128)(2,1)S(1)}, bf16[1024,1024]{1,0:T(8,128)(2,1)S(1)}, u32[]{:S(2)}, u32[]{:S(2)}) collective-permute-start(bf16[1024,1024]{1,0:T(8,128)(2,1)S(1)} %constant_dynamic-update-slice_fusion.5), channel_id=1, source_target_pairs={{0,4},{4,0},{1,5},{5,1},{2,6},{6,2},{3,7},{7,3},{8,12},{12,8},{9,1... | collective-permute-start | bytes 6291464 | tf_op jit(solution)/shard_map/ppermute | solution.py:48
  120.3 26.4 %collective-permute-start.12 = (bf16[512,160]{1,0:T(8,128)(2,1)S(1)}, bf16[512,160]{1,0:T(8,128)(2,1)S(1)}, u32[]{:S(2)}, u32[]{:S(2)}) collective-permute-start(bf16[512,160]{1,0:T(8,128)(2,1)S(1)} %add_convert_fusion.18), channel_id=1, source_target_pairs={{0,2},{1,3},{2,0},{3,1},{4,6},{5,7},{6,4},{7,5},{8,10},{9,11},{10,... | collective-permute-start | bytes 491528 | tf_op jit(solution)/shard_map/ppermute | solution.py:48
  180.2 115.6 %reduce-scatter.5.cloned.1.call-start = ((), (), s32[]{:S(2)}) async-start(), calls=%async_computation.4 | async-start | bytes 2621440 | tf_op jit(solution)/shard_map/reduce_scatter | solution.py:144
  237.6 111.0 %all-gather.4.cloned.1.call-start = ((), (), s32[]{:S(2)}) async-start(), calls=%async_computation.6 | async-start | bytes 2621440 | tf_op jit(solution)/shard_map/all_gather | solution.py:148
  282.3 26.3 %collective-permute-start.46 = (bf16[1024,1024]{1,0:T(8,128)(2,1)}, bf16[1024,1024]{1,0:T(8,128)(2,1)}, u32[]{:S(2)}, u32[]{:S(2)}) collective-permute-start(bf16[1024,1024]{1,0:T(8,128)(2,1)} %add_convert_fusion.7), channel_id=1, source_target_pairs={{0,4},{4,0},{1,5},{5,1},{2,6},{6,2},{3,7},{7,3},{8,12},{12,8},{9,1... | collective-permute-start | bytes 6291464 | tf_op jit(solution)/shard_map/ppermute | solution.py:48
  290.9 133.9 %reduce-scatter.9.cloned.1.call-start = ((), (), s32[]{:S(2)}) async-start(), calls=%async_computation.7 | async-start | bytes 2621440 | tf_op jit(solution)/shard_map/reduce_scatter | solution.py:144
  304.5 43.3 %collective-permute-start.26 = (bf16[512,160]{1,0:T(8,128)(2,1)S(1)}, bf16[512,160]{1,0:T(8,128)(2,1)S(1)}, u32[]{:S(2)}, u32[]{:S(2)}) collective-permute-start(bf16[512,160]{1,0:T(8,128)(2,1)S(1)} %fusion.79), channel_id=1, source_target_pairs={{0,2},{1,3},{2,0},{3,1},{4,6},{5,7},{6,4},{7,5},{8,10},{9,11},{10,... | collective-permute-start | bytes 491528 | tf_op jit(solution)/shard_map/ppermute | solution.py:48
  374.8 127.8 %reduce-scatter.11.cloned.1.call-start = ((), (), s32[]{:S(2)}) async-start(), calls=%async_computation.9 | async-start | bytes 2621440 | tf_op jit(solution)/shard_map/reduce_scatter | solution.py:144
  408.2 137.4 %all-gather.6.cloned.1.call-start = ((), (), s32[]{:S(2)}) async-start(), calls=%async_computation.8 | async-start | bytes 5242880 | tf_op jit(solution)/shard_map/all_gather | solution.py:148
  416.2 40.1 %collective-permute-start.47 = (bf16[2,256,512]{2,1,0:T(8,128)(2,1)}, bf16[2,256,512]{2,1,0:T(8,128)(2,1)S(1)}, u32[]{:S(2)}, u32[]{:S(2)}) collective-permute-start(bf16[2,256,512]{2,1,0:T(8,128)(2,1)} %pad_maximum_fusion.16), channel_id=1, source_target_pairs={{0,8},{8,0},{16,24},{24,16},{1,9},{9,1},{17,25},{25,17},{2,10},{10... | collective-permute-start | bytes 1572872 | tf_op jit(solution)/shard_map/ppermute | solution.py:48
  417.5 40.2 %collective-permute-start.48 = (bf16[2,256,512]{2,1,0:T(8,128)(2,1)}, bf16[2,256,512]{2,1,0:T(8,128)(2,1)}, u32[]{:S(2)}, u32[]{:S(2)}) collective-permute-start(bf16[2,256,512]{2,1,0:T(8,128)(2,1)} %slice.581), channel_id=1, source_target_pairs={{0,16},{8,24},{16,0},{24,8},{1,17},{9,25},{17,1},{25,9},{2,18},{10... | collective-permute-start | bytes 1572872 | tf_op jit(solution)/shard_map/ppermute | solution.py:48
  420.7 21.8 %collective-permute-start.37 = (bf16[2,256,512]{2,1,0:T(8,128)(2,1)}, bf16[2,256,512]{2,1,0:T(8,128)(2,1)}, u32[]{:S(2)}, u32[]{:S(2)}) collective-permute-start(bf16[2,256,512]{2,1,0:T(8,128)(2,1)} %pad_maximum_fusion.15), channel_id=1, source_target_pairs={{0,8},{8,0},{16,24},{24,16},{1,9},{9,1},{17,25},{25,17},{2,10},{10... | collective-permute-start | bytes 1572872 | tf_op jit(solution)/shard_map/ppermute | solution.py:48
  421.2 22.5 %collective-permute-start.38 = (bf16[2,256,512]{2,1,0:T(8,128)(2,1)}, bf16[2,256,512]{2,1,0:T(8,128)(2,1)}, u32[]{:S(2)}, u32[]{:S(2)}) collective-permute-start(bf16[2,256,512]{2,1,0:T(8,128)(2,1)} %slice.557), channel_id=1, source_target_pairs={{0,16},{8,24},{16,0},{24,8},{1,17},{9,25},{17,1},{25,9},{2,18},{10... | collective-permute-start | bytes 1572872 | tf_op jit(solution)/shard_map/ppermute | solution.py:48
  430.6 161.1 %all-gather.8.cloned.1.call-start = ((), (), s32[]{:S(2)}) async-start(), calls=%async_computation.10 | async-start | bytes 2621440 | tf_op jit(solution)/shard_map/all_gather | solution.py:148
  435.2 53.4 %collective-permute-start.32 = (bf16[2,256,512]{2,1,0:T(8,128)(2,1)}, bf16[2,256,512]{2,1,0:T(8,128)(2,1)}, u32[]{:S(2)}, u32[]{:S(2)}) collective-permute-start(bf16[2,256,512]{2,1,0:T(8,128)(2,1)} %pad_maximum_fusion.14), channel_id=1, source_target_pairs={{0,8},{8,0},{16,24},{24,16},{1,9},{9,1},{17,25},{25,17},{2,10},{10... | collective-permute-start | bytes 1572872 | tf_op jit(solution)/shard_map/ppermute | solution.py:48
  442.5 46.1 %collective-permute-start.33 = (bf16[2,256,512]{2,1,0:T(8,128)(2,1)}, bf16[2,256,512]{2,1,0:T(8,128)(2,1)}, u32[]{:S(2)}, u32[]{:S(2)}) collective-permute-start(bf16[2,256,512]{2,1,0:T(8,128)(2,1)} %slice.546), channel_id=1, source_target_pairs={{0,16},{8,24},{16,0},{24,8},{1,17},{9,25},{17,1},{25,9},{2,18},{10... | collective-permute-start | bytes 1572872 | tf_op jit(solution)/shard_map/ppermute | solution.py:48
  449.0 22.0 %collective-permute-start.39 = (bf16[256,512]{1,0:T(8,128)(2,1)}, bf16[256,512]{1,0:T(8,128)(2,1)}, u32[]{:S(2)}, u32[]{:S(2)}) collective-permute-start(bf16[256,512]{1,0:T(8,128)(2,1)} %get-tuple-element.343), channel_id=1, source_target_pairs={{0,16},{8,24},{16,0},{24,8},{1,17},{9,25},{17,1},{25,9},{2,18},{10... | collective-permute-start | bytes 786440 | tf_op jit(solution)/shard_map/ppermute | solution.py:48
  457.7 23.2 %collective-permute-start.41 = (bf16[192,1024]{1,0:T(8,128)(2,1)S(1)}, bf16[192,1024]{1,0:T(8,128)(2,1)S(1)}, u32[]{:S(2)}, u32[]{:S(2)}) collective-permute-start(bf16[192,1024]{1,0:T(8,128)(2,1)S(1)} %bitcast.281), channel_id=1, source_target_pairs={{0,4},{4,0},{1,5},{5,1},{2,6},{6,2},{3,7},{7,3},{8,12},{12,8},{9,1... | collective-permute-start | bytes 1179656 | tf_op jit(solution)/shard_map/ppermute | solution.py:48
  (181 other events, 1323.5 us)
Sparse Core Ops, SparseCore 0:
  180.3 48.9 reduce-scatter.6
  237.7 48.8 reduce-scatter.4
  291.0 57.6 all-gather.3
  375.0 42.4 reduce-scatter.8
  420.3 43.1 reduce-scatter.10
  465.0 80.5 all-gather.5
  547.1 44.4 all-gather.7
